TPU v7x, 256 devices: a whole 4x4x8 slice. The times are simulated.
256 devices in a mesh: pos: 32 (over x, z), head: 8 (over y, core).
Axes of the slice: x: 4, y: 4, z: 8, core: 2. Of those that a mesh axis runs over, the one named last changes fastest.
Arguments:
- query: bfloat16 [8192, 12288], P('pos', 'head'), may hold values from -8 to 8
- latent: bfloat16 [8192, 576], P('pos'), may hold values from -8 to 8
- norm_gain: float32 [512], replicated, may hold values from 0.25 to 1.75
- key_up: bfloat16 [512, 64, 128], P(None, 'head'), may hold values from -0.25 to 0.25
- value_up: bfloat16 [512, 64, 128], P(None, 'head'), may hold values from -0.25 to 0.25
- out_grad: bfloat16 [8192, 8192], P('pos', 'head'), may hold values from -6 to 6
- ancestors: int32 [64, 4], P('pos'), may hold values from 0 to 63, as said below
- visible: int32 [64, 4], P('pos'), may hold values from 1 to 128
Outputs:
- attn_out: bfloat16 [8192, 8192], P('pos', 'head')
- query_grad: bfloat16 [8192, 12288], P('pos', 'head')
- latent_grad: float32 [8192, 576], P('pos')
- key_up_grad: float32 [512, 64, 128], P('pos', 'head')
- value_up_grad: float32 [512, 64, 128], P('pos', 'head')
Inputs may be any that keep to these rules, and one draw needn't show every extreme that they name: `ancestors`: blocks are numbered globally, 2 consecutive ones to each index of pos. In one row the listed blocks are distinct and differ from the row's own block. Blocks held by pos index 0 may be listed by any row; for every pos index d and every other pos index s of 1 or more, all rows held by d name at most one block of s.
All inputs are finite; a program needn't handle non-finite values.
Results may differ from a plain program's by a relative error of at most 0.02.
Values may be sent and summed in bfloat16 or wider, within the bound.
No kernel may reach another device: no remote copies, remote signals or barrier semaphores. Data moves between devices by JAX's collectives and lax.ppermute only.
A program may use at most 128 MiB of HBM per device.

v0:
```python
import math

import jax
import jax.numpy as jnp
from jax import lax
from jax.sharding import PartitionSpec as P

LATENT = 512
ROPE = 64
HEAD_DIM = 128
BLOCK = 128
SLOTS = 4


norm_epsilon = 1e-06


def from_root(block, axis, source):
    block = jnp.where(lax.axis_index(axis) == source, block, jnp.zeros_like(block))
    return lax.psum(block, axis)


def shards(query, latent, norm_gain, key_up, value_up, out_grad, ancestors, visible):
    tokens_dev = latent.shape[0]
    blocks_dev = tokens_dev // BLOCK
    heads_dev = key_up.shape[1]
    kv_width = LATENT + ROPE
    pos_count = lax.axis_size("pos")
    my_index = lax.axis_index("pos")
    score_scale = 1.0 / math.sqrt(HEAD_DIM + ROPE)
    latent_raw = latent[:, :LATENT].astype(jnp.float32)
    inverse = lax.rsqrt(jnp.mean(latent_raw * latent_raw, axis=1, keepdims=True) + norm_epsilon)
    normed = (latent_raw * inverse * norm_gain).astype(jnp.bfloat16)
    key_rows = jnp.concatenate([normed, latent[:, LATENT:]], axis=1)
    own_tiles = key_rows.reshape(blocks_dev, BLOCK, kv_width)
    owner_dev = ancestors // blocks_dev
    local_block = ancestors % blocks_dev
    remote_slot = (visible > 0) & (owner_dev != 0) & (owner_dev != my_index)
    sources = jnp.arange(pos_count, dtype=jnp.int32)
    matches = remote_slot[:, :, None] & (owner_dev[:, :, None] == sources[None, None, :])
    wanted = jnp.max(jnp.where(matches, local_block[:, :, None] + 1, 0), axis=(0, 1))
    asked = lax.all_to_all(
        wanted.reshape(pos_count, 1), "pos", split_axis=0, concat_axis=0, tiled=True
    )
    chosen = asked == jnp.arange(1, blocks_dev + 1, dtype=jnp.int32)[None, :]
    outgoing = jnp.dot(
        chosen.astype(jnp.bfloat16),
        own_tiles.reshape(blocks_dev, BLOCK * kv_width),
        preferred_element_type=jnp.float32,
    )
    outgoing = outgoing.astype(jnp.bfloat16).reshape(pos_count, BLOCK, kv_width)
    fetched = lax.all_to_all(outgoing, "pos", split_axis=0, concat_axis=0, tiled=True)
    trunk = from_root(own_tiles, "pos", 0)
    candidates = jnp.concatenate([trunk, own_tiles, fetched], axis=0)
    cand_count = candidates.shape[0]
    slot_index = jnp.where(
        owner_dev == my_index,
        blocks_dev + local_block,
        jnp.where(owner_dev == 0, local_block, 2 * blocks_dev + owner_dev),
    )
    selector = slot_index.reshape(-1)[:, None] == jnp.arange(cand_count, dtype=jnp.int32)[None, :]
    slot_tiles = jnp.dot(
        selector.astype(jnp.bfloat16),
        candidates.reshape(cand_count, BLOCK * kv_width),
        preferred_element_type=jnp.float32,
    )
    slot_tiles = slot_tiles.astype(jnp.bfloat16).reshape(blocks_dev, SLOTS, BLOCK, kv_width)
    key_tiles = jnp.concatenate([own_tiles[:, None], slot_tiles], axis=1).reshape(
        blocks_dev, (SLOTS + 1) * BLOCK, kv_width
    )
    latent_keys = key_tiles[:, :, :LATENT]
    offsets = jnp.arange(BLOCK, dtype=jnp.int32)
    causal = offsets[None, :] <= offsets[:, None]
    seen_slots = offsets[None, None, :] < visible[:, :, None]
    allowed = jnp.concatenate(
        [
            jnp.broadcast_to(causal[None, :, None, :], (blocks_dev, BLOCK, 1, BLOCK)),
            jnp.broadcast_to(seen_slots[:, None, :, :], (blocks_dev, BLOCK, SLOTS, BLOCK)),
        ],
        axis=2,
    )
    allowed = allowed.reshape(blocks_dev, 1, BLOCK, (SLOTS + 1) * BLOCK)
    query_blocks = query.reshape(blocks_dev, BLOCK, heads_dev, HEAD_DIM + ROPE)
    query_nope_blocks = query_blocks[:, :, :, :HEAD_DIM]
    absorbed = jnp.einsum(
        "bqhd,lhd->bhql", query_nope_blocks, key_up, preferred_element_type=jnp.float32
    ).astype(jnp.bfloat16)
    query_rope = jnp.transpose(query_blocks[:, :, :, HEAD_DIM:], (0, 2, 1, 3))
    query_full = jnp.concatenate([absorbed, query_rope], axis=3)
    scores = (
        jnp.einsum("bhqx,bkx->bhqk", query_full, key_tiles, preferred_element_type=jnp.float32)
        * score_scale
    )
    scores = jnp.where(allowed, scores, -jnp.inf)
    exp_terms = jnp.exp(scores - jnp.max(scores, axis=3, keepdims=True))
    weights = exp_terms / jnp.sum(exp_terms, axis=3, keepdims=True)
    weights_half = weights.astype(jnp.bfloat16)
    mixed = jnp.einsum(
        "bhqk,bkl->bhql", weights_half, latent_keys, preferred_element_type=jnp.float32
    ).astype(jnp.bfloat16)
    attention_out = jnp.einsum(
        "bhql,lhd->bqhd", mixed, value_up, preferred_element_type=jnp.float32
    ).astype(jnp.bfloat16)
    attention_out = attention_out.reshape(tokens_dev, heads_dev * HEAD_DIM)
    grad_heads = out_grad.reshape(blocks_dev, BLOCK, heads_dev, HEAD_DIM)
    mixed_grad = jnp.einsum(
        "bqhd,lhd->bhql", grad_heads, value_up, preferred_element_type=jnp.float32
    ).astype(jnp.bfloat16)
    weight_grad = jnp.einsum(
        "bhql,bkl->bhqk", mixed_grad, latent_keys, preferred_element_type=jnp.float32
    )
    score_grad = (
        weights
        * (weight_grad - jnp.sum(weights * weight_grad, axis=3, keepdims=True))
        * score_scale
    ).astype(jnp.bfloat16)
    full_grad = jnp.einsum(
        "bhqk,bkx->bhqx", score_grad, key_tiles, preferred_element_type=jnp.float32
    )
    absorbed_grad = full_grad[..., :LATENT].astype(jnp.bfloat16)
    nope_grad = jnp.einsum(
        "bhql,lhd->bqhd", absorbed_grad, key_up, preferred_element_type=jnp.float32
    )
    rope_grad = jnp.transpose(full_grad[..., LATENT:], (0, 2, 1, 3))
    query_grad = jnp.concatenate([nope_grad, rope_grad], axis=3).astype(jnp.bfloat16)
    query_grad = query_grad.reshape(tokens_dev, heads_dev * (HEAD_DIM + ROPE))
    tile_grad = jnp.einsum(
        "bhqk,bhqx->bkx", score_grad, query_full, preferred_element_type=jnp.float32
    )
    value_part = jnp.einsum(
        "bhqk,bhql->bkl", weights_half, mixed_grad, preferred_element_type=jnp.float32
    )
    tile_grad = (tile_grad + jnp.pad(value_part, ((0, 0), (0, 0), (0, ROPE)))).reshape(
        blocks_dev, SLOTS + 1, BLOCK, kv_width
    )
    slot_grad = tile_grad[:, 1:].reshape(blocks_dev * SLOTS, BLOCK * kv_width)
    cand_grad = jnp.dot(
        selector.astype(jnp.float32).T, slot_grad, precision=lax.Precision.HIGHEST
    ).reshape(cand_count, BLOCK, kv_width)
    trunk_grad = cand_grad[:blocks_dev]
    local_grad = tile_grad[:, 0] + cand_grad[blocks_dev : 2 * blocks_dev]
    fetched_grad = cand_grad[2 * blocks_dev :]
    chosen_f = chosen.astype(jnp.float32)
    returned = lax.all_to_all(
        fetched_grad.astype(jnp.bfloat16), "pos", split_axis=0, concat_axis=0, tiled=True
    ).astype(fetched_grad.dtype)
    remote_grad = jnp.dot(
        chosen_f.T, returned.reshape(pos_count, BLOCK * kv_width), precision=lax.Precision.HIGHEST
    )
    remote_grad = remote_grad.reshape(blocks_dev, BLOCK, kv_width)
    trunk_total = lax.psum(trunk_grad.astype(jnp.bfloat16), "pos").astype(jnp.float32)
    partial_grad = local_grad + remote_grad + jnp.where(my_index == 0, trunk_total, 0.0)
    total_grad = (
        lax.psum(partial_grad.astype(jnp.bfloat16), "head")
        .astype(jnp.float32)
        .reshape(tokens_dev, kv_width)
    )
    gained = total_grad[:, :LATENT] * norm_gain
    latent_part = inverse * gained - latent_raw * inverse * inverse * inverse * jnp.mean(
        latent_raw * gained, axis=1, keepdims=True
    )
    latent_grad = jnp.concatenate([latent_part, total_grad[:, LATENT:]], axis=1)
    key_term = jnp.einsum(
        "bhql,bqhd->lhd", absorbed_grad, query_nope_blocks, preferred_element_type=jnp.float32
    )
    value_term = jnp.einsum("bhql,bqhd->lhd", mixed, grad_heads, preferred_element_type=jnp.float32)
    weight_grads = lax.psum_scatter(
        jnp.stack([key_term, value_term], axis=1).astype(jnp.bfloat16),
        "pos",
        scatter_dimension=0,
        tiled=True,
    ).astype(jnp.float32)
    return (attention_out, query_grad, latent_grad, weight_grads[:, 0], weight_grads[:, 1])


def solution(mesh):
    placed = (
        P("pos", "head"),
        P("pos", None),
        P(),
        P(None, "head", None),
        P(None, "head", None),
        P("pos", "head"),
        P("pos", None),
        P("pos", None),
    )
    return jax.shard_map(
        shards,
        mesh=mesh,
        in_specs=placed,
        out_specs=(
            P("pos", "head"),
            P("pos", "head"),
            P("pos", None),
            P("pos", "head", None),
            P("pos", "head", None),
        ),
        check_vma=False,
    )
```

profile of v0, /device:TPU:2, one launch (start us, length us, event | category | flops | bytes accessed | tf_op | source)
XLA Modules:
  0.0 800.4 jit_solution(13522415926263440059)
XLA Ops:
  9.3 11.6 %all-to-all-start = ((s32[32,1,1]{2,1,0:T(1,128)}), s32[32,1,1]{2,1,0:T(1,128)S(1)}, u32[]{:S(2)}, u32[]{:S(2)}) async-start(s32[32,1,1]{2,1,0:T(1,128)} %copy.158), calls=%async_computation | async-start | bytes 32768 | tf_op jit(solution)/shard_map/all_to_all | solution.py:42
  21.0 1.0 fusion.67
  22.8 1.1 fusion.63
  24.6 4.9 all-to-all-done
  30.2 3.3 convolution_convert_fusion
  33.5 8.9 %reshape.114 = bf16[32,128,576]{2,1,0:T(8,128)(2,1)} reshape(bf16[32,73728]{1,0:T(8,128)(2,1)} %convolution_convert_fusion) | data formatting | bytes 9437184 | tf_op jit(solution)/shard_map/reshape | solution.py:51
  42.4 7.6 copy.159
  50.0 6.0 all-to-all-start.1
  56.8 1.1 concatenate.32
  59.4 0.9 copy.150
  60.4 0.8 copy.267
  61.2 1.6 copy.197
  62.8 2.1 convert_bitcast_fusion.1
  64.9 1.9 convert_bitcast_fusion
  66.9 95.7 %all-to-all-done.1 = bf16[32,128,576]{1,2,0:T(8,128)(2,1)} async-done(((bf16[32,128,576]{1,2,0:T(8,128)(2,1)}), bf16[32,128,576]{1,2,0:T(8,128)(2,1)}, u32[]{:S(2)}, u32[]{:S(2)}) %all-to-all-start.1) | async-done | bytes 4718624 | tf_op jit(solution)/shard_map/all_to_all | solution.py:52
  162.6 7.6 copy.160
  170.2 8.8 %concatenate.34 = bf16[32,73728]{1,0:T(8,128)(2,1)} reshape(bf16[32,128,576]{2,1,0:T(8,128)(2,1)} %copy.160) | data formatting | bytes 9437184 | tf_op jit(solution)/shard_map/concatenate | solution.py:54
  179.0 42.9 %all-reduce.5.cloned.1.call-done = bf16[2,73728]{1,0:T(2,128)(2,1)} async-done(((bf16[2,73728]{1,0:T(2,128)(2,1)}), bf16[2,73728]{1,0:T(2,128)(2,1)}) %all-reduce.5.cloned.1.call-update) | async-done | bytes 294928 | tf_op jit(solution)/shard_map/psum | solution.py:20
  221.9 5.1 convolution_convert_fusion.1
  227.0 1.6 reshape.139
  228.6 2.8 reshape.115
  231.4 1.2 pad_maximum_fusion.2
  232.6 4.4 fusion.32
  237.1 2.9 fusion.25
  240.0 2.4 fusion.90
  242.5 2.3 copy-done.20
  244.7 3.5 fusion.34
  248.2 17.6 %bitcast_add_fusion = f32[2,640,576]{1,2,0:T(8,128)} fusion(f32[2,640,512]{1,2,0:T(8,128)} %fusion.34, f32[2,8,128,640]{3,2,1,0:T(8,128)} %fusion.32, f32[2,8,128,640]{3,2,1,0:T(8,128)} %copy-done.20, f32[2,8,128]{2,1,0:T(8,128)S(1)} %get-tuple-element.37, bf16[2,8,128,64]{2,3,0,1:T(8,128)(2,1)S(1)} %bitcast.119, ...), kind=kOutput, calls=%fused_computation.15 | convolution fusion | flops 1524583040 | bytes 18423808 | tf_op jit(solution)/shard_map/bhqk,bhqx->bkx/dot_general | solution.py:127
  265.9 2.4 copy.176
  268.3 1.7 slice.80
  269.9 4.5 reshape.120
  274.4 9.1 %fusion.91 = (bf16[36,73728]{1,0:T(8,128)(2,1)S(1)}, f32[36,73728]{1,0:T(8,128)}) fusion(f32[8,73728]{1,0:T(8,128)} %reshape.120, s32[8]{0:T(128)S(1)} %eq.61), kind=kOutput, calls=%fused_computation.123 | convolution fusion | flops 257458464 | bytes 18284576 | tf_op jit(solution)/shard_map/dot_general | solution.py:137
  283.5 2.5 copy-done
  286.0 3.3 slice.82
  289.3 8.8 %convert_element_type.85 = bf16[32,128,576]{2,1,0:T(8,128)(2,1)} reshape(bf16[32,73728]{1,0:T(8,128)(2,1)} %slice.82) | data formatting | bytes 9437184 | tf_op jit(solution)/shard_map/convert_element_type | solution.py:145
  298.0 7.5 copy.179
  305.5 7.6 all-to-all-start.2
  313.2 4.8 convolution_convert_fusion.2
  318.0 1.4 copy-done.9
  319.3 1.8 fusion.42
  321.2 18.4 %fusion.27 = bf16[2,8,128,576]{2,3,1,0:T(8,128)(2,1)} fusion(bf16[2,640,576,1]{2,1,3,0:T(8,128)(2,1)} %bitcast.105, f32[2,8,128,640]{3,2,1,0:T(8,128)} %fusion.32, f32[2,8,128,640]{3,2,1,0:T(8,128)} %copy-done.20, f32[2,8,128]{2,1,0:T(8,128)S(1)} %get-tuple-element.37), kind=kOutput, calls=%fused_computation.35 | convolution fusion | flops 1520306816 | bytes 14327808 | tf_op jit(solution)/shard_map/bhqk,bkx->bhqx/dot_general | solution.py:117
  339.6 2.5 fusion.41
  342.1 1.5 pad_maximum_fusion.1
  343.9 0.9 slice.79
  344.8 1.4 slice.83
  346.2 2.4 fusion.52
  348.7 1.2 pad_maximum_fusion.3
  349.9 0.9 copy.215
  350.8 1.8 reshape.137
  352.9 0.9 copy.182
  354.0 2.0 fusion.55
  356.3 0.9 copy.265
  357.5 1.9 slice.81
  360.2 215.7 %reduce-scatter.2.cloned.1.call-done = bf16[16,2,8,128]{3,0,2,1:T(8,128)(2,1)} async-done(((bf16[512,2,8,128]{3,0,2,1:T(8,128)(2,1)}), bf16[16,2,8,128]{3,0,2,1:T(8,128)(2,1)}) %reduce-scatter.2.cloned.1.call-update) | async-done | bytes 65552 | tf_op jit(solution)/shard_map/reduce_scatter | solution.py:167
  575.9 0.8 convert_element_type.89
  576.7 7.7 copy.180
  584.4 8.7 %reshape.121 = bf16[32,73728]{1,0:T(8,128)(2,1)} reshape(bf16[32,128,576]{2,1,0:T(8,128)(2,1)} %copy.180) | data formatting | bytes 9437184 | tf_op jit(solution)/shard_map/reshape | solution.py:148
  593.1 8.8 %dot_general.66 = bf16[128,576,32]{1,0,2:T(8,128)(2,1)} reshape(bf16[73728,32]{0,1:T(8,128)(2,1)} %bitcast.99) | data formatting | bytes 9437184 | tf_op jit(solution)/shard_map/dot_general | solution.py:147
  601.9 8.5 %copy.181 = bf16[128,576,32]{0,2,1:T(8,128)(2,1)} copy(bf16[128,576,32]{1,0,2:T(8,128)(2,1)} %dot_general.66) | data formatting | bytes 9437184 | tf_op jit(solution)/shard_map/dot_general | solution.py:147
  610.5 111.9 %all-reduce.7.cloned.1.call-done = bf16[2,128,576]{1,0,2:T(2,128)(2,1)} async-done(((bf16[2,128,576]{1,0,2:T(2,128)(2,1)}), bf16[2,128,576]{1,0,2:T(2,128)(2,1)}) %all-reduce.7.cloned.1.call-update) | async-done | bytes 294928 | tf_op jit(solution)/shard_map/psum | solution.py:151
  722.4 3.2 fusion.58
  727.7 62.8 %all-reduce.9.cloned.1.call-done = bf16[256,576]{0,1:T(8,128)(2,1)} async-done(((bf16[256,576]{0,1:T(8,128)(2,1)}), bf16[256,576]{0,1:T(8,128)(2,1)}) %all-reduce.9.cloned.1.call-update) | async-done | bytes 294928 | tf_op jit(solution)/shard_map/psum | solution.py:154
  790.4 1.0 reshape.123
  792.6 0.9 pad_maximum_fusion.4
  (84 shorter events, 11.9 us)
Async XLA Ops:
  9.3 20.2 %all-to-all-start = ((s32[32,1,1]{2,1,0:T(1,128)}), s32[32,1,1]{2,1,0:T(1,128)S(1)}, u32[]{:S(2)}, u32[]{:S(2)}) async-start(s32[32,1,1]{2,1,0:T(1,128)} %copy.158), calls=%async_computation | async-start | bytes 32768 | tf_op jit(solution)/shard_map/all_to_all | solution.py:42
  24.2 18.2 %copy-start.7 = (bf16[256,576]{1,0:T(8,128)(2,1)}, bf16[256,576]{1,0:T(8,128)(2,1)S(1)}, u32[]{:S(2)}) copy-start(bf16[256,576]{1,0:T(8,128)(2,1)S(1)} %copy.155) | copy-start | bytes 884740
  24.6 17.8 %copy-start.13 = (bf16[2,73728]{1,0:T(2,128)(2,1)}, bf16[2,73728]{1,0:T(2,128)(2,1)S(1)}, u32[]{:S(2)}) copy-start(bf16[2,73728]{1,0:T(2,128)(2,1)S(1)} %concatenate.33) | copy-start | bytes 884740
  50.0 7.9 copy-start.14
  50.0 112.6 %all-to-all-start.1 = ((bf16[32,128,576]{1,2,0:T(8,128)(2,1)}), bf16[32,128,576]{1,2,0:T(8,128)(2,1)}, u32[]{:S(2)}, u32[]{:S(2)}) async-start(bf16[32,128,576]{1,2,0:T(8,128)(2,1)} %copy.159), calls=%async_computation.1 | async-start | bytes 9437184 | tf_op jit(solution)/shard_map/all_to_all | solution.py:52
  56.0 165.9 %all-reduce.5.cloned.1.call-start = ((), (), s32[]{:S(2)}) async-start(), calls=%async_computation.4 | async-start | bytes 589824 | tf_op jit(solution)/shard_map/psum | solution.py:20
  56.7 2.3 copy-start.19
  57.8 2.4 copy-start.15
  58.9 6.0 copy-start.12
  60.4 4.6 copy-start.2
  62.8 2.1 copy-start.4
  232.6 4.5 copy-start.1
  232.6 4.5 copy-start.11
  232.6 4.5 copy-start.16
  237.1 3.0 copy-start.17
  242.5 2.3 copy-start.20
  283.5 2.5 copy-start
  305.5 271.2 %all-to-all-start.2 = ((bf16[32,128,576]{1,2,0:T(8,128)(2,1)}), bf16[32,128,576]{1,2,0:T(8,128)(2,1)}, u32[]{:S(2)}, u32[]{:S(2)}) async-start(bf16[32,128,576]{1,2,0:T(8,128)(2,1)} %copy.179), calls=%async_computation.2 | async-start | bytes 9437184 | tf_op jit(solution)/shard_map/all_to_all | solution.py:144
  313.1 262.8 %reduce-scatter.2.cloned.1.call-start = ((), (), s32[]{:S(2)}) async-start(), calls=%async_computation.7 | async-start | bytes 2162688 | tf_op jit(solution)/shard_map/reduce_scatter | solution.py:167
  313.2 6.2 copy-start.3
  317.9 1.4 copy-start.9
  339.6 2.5 copy-start.5
  343.6 378.8 %all-reduce.7.cloned.1.call-start = ((), (), s32[]{:S(2)}) async-start(), calls=%async_computation.5 | async-start | bytes 589824 | tf_op jit(solution)/shard_map/psum | solution.py:151
  350.8 3.2 copy-start.10
  353.9 3.3 copy-start.8
  353.9 436.5 %all-reduce.9.cloned.1.call-start = ((), (), s32[]{:S(2)}) async-start(), calls=%async_computation.6 | async-start | bytes 589824 | tf_op jit(solution)/shard_map/psum | solution.py:154
  610.5 181.0 %copy-start.6 = (bf16[256,576]{0,1:T(8,128)(2,1)S(1)}, bf16[256,576]{0,1:T(8,128)(2,1)}, u32[]{:S(2)}) copy-start(bf16[256,576]{0,1:T(8,128)(2,1)} %param.9) | copy-start | bytes 884740
  610.5 181.0 %copy-start.18 = (f32[512]{0:T(512)S(1)}, f32[512]{0:T(512)}, u32[]{:S(2)}) copy-start(f32[512]{0:T(512)} %param.10) | copy-start | bytes 6148
Sparse Core Ops, SparseCore 0:
  60.3 161.5 all-reduce.4
  343.7 232.1 reduce-scatter.1
  580.3 142.0 all-reduce.6
  726.5 63.9 all-reduce.8
where the time goes:
time: 806 us; the launch traced here: 800 us
  waiting for transfers between devices  534 us (66%)
  local copies, waits for them, and re-layouts  127 us (16%)
  matrix products  85.2 us (11%)
  starting transfers between devices  26.1 us (3%)
  between operations  14.7 us (2%)
  other arithmetic  13.8 us (2%)
    reduce_scatter x1, waiting for transfers between devices, shards(): lax.psum_scatter(jnp.stack([key_term, value_term], axis=1).astype(jnp.bfl...  216 us
    psum x1, waiting for transfers between devices, shards(): lax.psum(trunk_grad.astype(jnp.bfloat16), 'pos').astype(jnp.float32)  112 us
    all_to_all x1, waiting for transfers between devices, shards(): lax.all_to_all(outgoing, 'pos', split_axis=0, concat_axis=0, tiled=True)  95.7 us
    psum x1, waiting for transfers between devices, shards(): lax.psum(partial_grad.astype(jnp.bfloat16), 'head').astype(jnp.float32)  62.8 us
    psum x1, waiting for transfers between devices, from_root(): return lax.psum(block, axis)  42.9 us
    dot_general x1, matrix products, shards(): jnp.einsum('bhqk,bkx->bhqx', score_grad, key_tiles, preferred_element_typ...  18.4 us
    dot_general x1, matrix products, shards(): jnp.einsum('bhqk,bhqx->bkx', score_grad, query_full, preferred_element_ty...  17.6 us
    dot_general x2, local copies, waits for them, and re-layouts, shards(): jnp.dot(chosen_f.T, returned.reshape(pos_count, BLOCK * kv_width), precis...  17.3 us
  transfers between devices with their start and end apart: 7, of which 6 were waited for; matrix products, arithmetic and copies ran while one was open for 14% of the time, Pallas kernels for 0%

commit v1 on v0

v1 whole, which is shorter than its diff:
```python
import functools
import math

import jax
import jax.numpy as jnp
from jax import lax
from jax.experimental import pallas as pl
from jax.experimental.pallas import tpu as pltpu
from jax.sharding import Mesh
from jax.sharding import PartitionSpec as P

LATENT = 512
ROPE = 64
KV = LATENT + ROPE
HEAD_DIM = 128
QDIM = HEAD_DIM + ROPE
BLOCK = 128
SLOTS = 4
BLOCKS_DEV = 2
NX, NZ, NY, NC = 4, 8, 4, 2
SHARES = NY * NC
ROWS = BLOCK // SHARES
HALF = NY * ROWS
HEADS_DEV = 8
TILES = BLOCKS_DEV * (1 + SLOTS)
KEYS = (1 + SLOTS) * BLOCK
HEADS_STEP = 2
norm_epsilon = 1e-06

bf16 = jnp.bfloat16
f32 = jnp.float32
VMEM_LIMIT = 48 * 1024 * 1024


def dot(a, b):
    return lax.dot_general(a, b, (((1,), (0,)), ((), ())), preferred_element_type=f32)


def dot_nt(a, b):
    return lax.dot_general(a, b, (((1,), (1,)), ((), ())), preferred_element_type=f32)


def dot_tn(a, b):
    return lax.dot_general(a, b, (((0,), (0,)), ((), ())), preferred_element_type=f32)


def smem():
    return pl.BlockSpec(memory_space=pltpu.SMEM)


def vmem():
    return pl.BlockSpec(memory_space=pltpu.VMEM)


def norm_inverse(raw):
    return lax.rsqrt(jnp.mean(raw * raw, axis=1, keepdims=True) + norm_epsilon)


def share_kernel(share_ref, latent_ref, gain_ref, out_ref):
    for b in range(BLOCKS_DEV):
        start = pl.multiple_of(b * BLOCK + share_ref[0] * ROWS, ROWS)
        raw = latent_ref[pl.ds(start, ROWS), :LATENT].astype(f32)
        keys = (raw * norm_inverse(raw) * gain_ref[...]).astype(bf16)
        rope = latent_ref[pl.ds(start, ROWS), LATENT:]
        for z in range(NZ):
            out_ref[z, b, :, :LATENT] = keys
            out_ref[z, b, :, LATENT:] = rope


def spread_kernel(in_ref, out_ref):
    for x in range(NX):
        out_ref[x] = in_ref[...]


def select_kernel(anc_ref, all_ref, out_ref):
    for s in range(BLOCKS_DEV * SLOTS):
        tile = all_ref[anc_ref[s]]
        for y in range(NY):
            out_ref[y, s] = tile


def attend_kernel(
    core_ref, vis_ref, query_ref, grad_ref, key_up_ref, value_up_ref, latent_ref, gain_ref, near_ref, far_ref,
    attn_ref, qgrad_ref, wgrad_ref, keep_ref, send_ref,
    klat, krope, bias, glat, grope,
):
    step = pl.program_id(0)
    core = core_ref[0]
    scale = 1.0 / math.sqrt(QDIM)

    @pl.when(step == 0)
    def _():
        raw = latent_ref[:, :LATENT].astype(f32)
        own = (raw * norm_inverse(raw) * gain_ref[...]).astype(bf16)
        own = own.reshape(BLOCKS_DEV, NY, NC, ROWS, LATENT)
        rope = latent_ref[:, LATENT:].reshape(BLOCKS_DEV, NY, NC, ROWS, ROPE)
        for b in range(BLOCKS_DEV):
            for side in range(NC):
                for y in range(NY):
                    at = side * HALF + y * ROWS
                    first = core == side
                    klat[b, at : at + ROWS, :] = jnp.where(first, own[b, y, 0], own[b, y, 1])
                    krope[b, at : at + ROWS, :] = jnp.where(first, rope[b, y, 0], rope[b, y, 1])
                    for j in range(SLOTS):
                        src = (near_ref, far_ref)[side]
                        to = (1 + j) * BLOCK + at
                        klat[b, to : to + ROWS, :] = src[y, b * SLOTS + j, :, :LATENT]
                        krope[b, to : to + ROWS, :] = src[y, b * SLOTS + j, :, LATENT:]
        col = lax.broadcasted_iota(jnp.int32, (BLOCK, BLOCK), 1)
        row = lax.broadcasted_iota(jnp.int32, (BLOCK, BLOCK), 0)
        side = jnp.where(col >= HALF, 1, 0)
        rest = col - side * HALF
        piece = rest // ROWS
        owner = jnp.where(core == 0, side, 1 - side)
        offset = (piece * NC + owner) * ROWS + (rest - piece * ROWS)
        for b in range(BLOCKS_DEV):
            bias[b, :, :BLOCK] = jnp.where(offset <= row, 0.0, -jnp.inf)
            for j in range(SLOTS):
                limit = vis_ref[b * SLOTS + j]
                bias[b, :, (1 + j) * BLOCK : (2 + j) * BLOCK] = jnp.where(offset < limit, 0.0, -jnp.inf)
        glat[...] = jnp.zeros_like(glat)
        grope[...] = jnp.zeros_like(grope)

    heads = range(HEADS_STEP)
    nope = [query_ref[:, h * QDIM : h * QDIM + HEAD_DIM] for h in heads]
    rope = [query_ref[:, h * QDIM + HEAD_DIM : (h + 1) * QDIM] for h in heads]
    grad = [grad_ref[:, h * HEAD_DIM : (h + 1) * HEAD_DIM] for h in heads]
    key_up = [key_up_ref[:, h * HEAD_DIM : (h + 1) * HEAD_DIM] for h in heads]
    value_up = [value_up_ref[:, h * HEAD_DIM : (h + 1) * HEAD_DIM] for h in heads]
    absorbed = [dot_nt(nope[h], key_up[h]).astype(bf16) for h in heads]
    mixed_grad = [dot_nt(grad[h], value_up[h]).astype(bf16) for h in heads]

    mixed_parts, full_parts, rope_parts = [], [], []
    for b in range(BLOCKS_DEV):
        rows = slice(b * BLOCK, (b + 1) * BLOCK)
        ab = jnp.concatenate([absorbed[h][rows] for h in heads], axis=0)
        rb = jnp.concatenate([rope[h][rows] for h in heads], axis=0)
        mg = jnp.concatenate([mixed_grad[h][rows] for h in heads], axis=0)
        lat = klat[b]
        rop = krope[b]
        mask = jnp.concatenate([bias[b]] * HEADS_STEP, axis=0)
        scores = (dot_nt(ab, lat) + dot_nt(rb, rop)) * scale + mask
        exp_terms = jnp.exp(scores - jnp.max(scores, axis=1, keepdims=True))
        weights = exp_terms * (1.0 / jnp.sum(exp_terms, axis=1, keepdims=True))
        half = weights.astype(bf16)
        mixed_parts.append(dot(half, lat).astype(bf16))
        weight_grad = dot_nt(mg, lat)
        inner = jnp.sum(weights * weight_grad, axis=1, keepdims=True)
        score_grad = (weights * (weight_grad - inner) * scale).astype(bf16)
        full_parts.append(dot(score_grad, lat).astype(bf16))
        rope_parts.append(dot(score_grad, rop).astype(bf16))
        both = jnp.concatenate([score_grad, half], axis=0)
        glat[b] += dot_tn(both, jnp.concatenate([ab, mg], axis=0))
        grope[b] += dot_tn(score_grad, rb)

    def head_rows(parts, h):
        return jnp.concatenate([part[h * BLOCK : (h + 1) * BLOCK] for part in parts], axis=0)

    width = HEADS_STEP * HEAD_DIM
    for h in heads:
        mixed = head_rows(mixed_parts, h)
        full = head_rows(full_parts, h)
        attn_ref[:, h * HEAD_DIM : (h + 1) * HEAD_DIM] = dot(mixed, value_up[h]).astype(bf16)
        qgrad_ref[:, h * QDIM : h * QDIM + HEAD_DIM] = dot(full, key_up[h]).astype(bf16)
        qgrad_ref[:, h * QDIM + HEAD_DIM : (h + 1) * QDIM] = head_rows(rope_parts, h)
        at = h * HEAD_DIM
        wgrad_ref[:, at : at + HEAD_DIM] = dot_tn(full, nope[h]).astype(bf16)
        wgrad_ref[:, width + at : width + at + HEAD_DIM] = dot_tn(mixed, grad[h]).astype(bf16)

    @pl.when(step == pl.num_programs(0) - 1)
    def _():
        for b in range(BLOCKS_DEV):
            for j in range(1 + SLOTS):
                tile = b if j == 0 else BLOCKS_DEV + b * SLOTS + j - 1
                for y in range(NY):
                    at = j * BLOCK + y * ROWS
                    keep_ref[y, tile, :, :LATENT] = glat[b, at : at + ROWS, :]
                    keep_ref[y, tile, :, LATENT:] = grope[b, at : at + ROWS, :]
                    at = at + HALF
                    send_ref[y, tile, :, :LATENT] = glat[b, at : at + ROWS, :].astype(bf16)
                    send_ref[y, tile, :, LATENT:] = grope[b, at : at + ROWS, :].astype(bf16)


def pair_kernel(keep_ref, recv_ref, out_ref):
    out_ref[...] = (keep_ref[...] + recv_ref[...].astype(f32)).astype(bf16)


def scatter_kernel(dest_ref, in_ref, out_ref, acc):
    acc[...] = jnp.zeros_like(acc)
    for t in range(TILES):
        tile = in_ref[0, t].astype(f32)
        for y in range(1, NY):
            tile = tile + in_ref[y, t].astype(f32)
        at = dest_ref[t]
        acc[at] = acc[at] + tile
    out_ref[...] = acc[...].astype(bf16)


def sum_kernel(in_ref, out_ref):
    total = in_ref[0].astype(f32)
    for i in range(1, in_ref.shape[0]):
        total = total + in_ref[i].astype(f32)
    total = total.astype(bf16)
    if len(out_ref.shape) == len(total.shape):
        out_ref[...] = total
    else:
        for i in range(out_ref.shape[0]):
            out_ref[i] = total


def final_kernel(core_ref, near_ref, far_ref, latent_ref, gain_ref, out_ref):
    core = core_ref[0]
    for b in range(BLOCKS_DEV):
        pieces = []
        for y in range(NY):
            near, far = near_ref[y, b], far_ref[y, b]
            pieces.append(jnp.where(core == 0, near, far))
            pieces.append(jnp.where(core == 0, far, near))
        total = jnp.concatenate(pieces, axis=0).astype(f32)
        rows = slice(b * BLOCK, (b + 1) * BLOCK)
        raw = latent_ref[rows, :LATENT].astype(f32)
        inverse = norm_inverse(raw)
        gained = total[:, :LATENT] * gain_ref[...]
        out_ref[rows, :LATENT] = inverse * gained - raw * inverse * inverse * inverse * jnp.mean(
            raw * gained, axis=1, keepdims=True
        )
        out_ref[rows, LATENT:] = total[:, LATENT:]


def call(kernel, out_shape, in_specs, **kw):
    return pl.pallas_call(
        kernel,
        out_shape=out_shape,
        in_specs=in_specs,
        out_specs=kw.pop("out_specs", vmem()),
        compiler_params=pltpu.CompilerParams(vmem_limit_bytes=VMEM_LIMIT),
        **kw,
    )


def shape(*dims, dtype=bf16):
    return jax.ShapeDtypeStruct(dims, dtype)


def exchange(values, axis):
    return lax.all_to_all(values, axis, split_axis=0, concat_axis=0, tiled=True)


def swap_cores(values):
    return lax.ppermute(values, "c", [(0, 1), (1, 0)])


def shards(query, latent, norm_gain, key_up, value_up, out_grad, ancestors, visible):
    core = lax.axis_index("c").astype(jnp.int32).reshape(1)
    share = (lax.axis_index("y") * NC + lax.axis_index("c")).astype(jnp.int32).reshape(1)
    place = lax.axis_index("x") * NZ + lax.axis_index("z")
    gain = norm_gain.reshape(1, LATENT)
    listed = ancestors.reshape(BLOCKS_DEV * SLOTS)
    limits = visible.reshape(BLOCKS_DEV * SLOTS)

    mine = call(share_kernel, shape(NZ, BLOCKS_DEV, ROWS, KV), [smem(), vmem(), vmem()])(share, latent, gain)
    column = exchange(mine, "z").reshape(NZ * BLOCKS_DEV, ROWS, KV)
    column = call(spread_kernel, shape(NX, NZ * BLOCKS_DEV, ROWS, KV), [vmem()])(column)
    everyone = exchange(column, "x").reshape(NX * NZ * BLOCKS_DEV, ROWS, KV)
    picked = call(select_kernel, shape(NY, BLOCKS_DEV * SLOTS, ROWS, KV), [smem(), vmem()])(listed, everyone)
    near = exchange(picked, "y")
    far = swap_cores(near)

    key_up_flat = key_up.reshape(LATENT, HEADS_DEV * HEAD_DIM)
    value_up_flat = value_up.reshape(LATENT, HEADS_DEV * HEAD_DIM)
    tokens = query.shape[0]
    steps = HEADS_DEV // HEADS_STEP
    width = HEADS_STEP * HEAD_DIM
    qwidth = HEADS_STEP * QDIM

    def columns(rows, cols):
        return pl.BlockSpec((rows, cols), lambda g: (0, g))

    def whole(*dims):
        return pl.BlockSpec(dims, lambda g: (0,) * len(dims))

    attn_out, query_grad, wgrad, keep, send = call(
        attend_kernel,
        (
            shape(tokens, HEADS_DEV * HEAD_DIM),
            shape(tokens, HEADS_DEV * QDIM),
            shape(LATENT, 2 * HEADS_DEV * HEAD_DIM),
            shape(NY, TILES, ROWS, KV, dtype=f32),
            shape(NY, TILES, ROWS, KV),
        ),
        [
            smem(),
            smem(),
            columns(tokens, qwidth),
            columns(tokens, width),
            columns(LATENT, width),
            columns(LATENT, width),
            whole(tokens, KV),
            whole(1, LATENT),
            whole(NY, BLOCKS_DEV * SLOTS, ROWS, KV),
            whole(NY, BLOCKS_DEV * SLOTS, ROWS, KV),
        ],
        out_specs=(
            columns(tokens, width),
            columns(tokens, qwidth),
            columns(LATENT, 2 * width),
            whole(NY, TILES, ROWS, KV),
            whole(NY, TILES, ROWS, KV),
        ),
        grid=(steps,),
        scratch_shapes=[
            pltpu.VMEM((BLOCKS_DEV, KEYS, LATENT), bf16),
            pltpu.VMEM((BLOCKS_DEV, KEYS, ROPE), bf16),
            pltpu.VMEM((BLOCKS_DEV, BLOCK, KEYS), f32),
            pltpu.VMEM((BLOCKS_DEV, KEYS, LATENT), f32),
            pltpu.VMEM((BLOCKS_DEV, KEYS, ROPE), f32),
        ],
        cost_estimate=pl.CostEstimate(flops=11_000_000_000, bytes_accessed=16_000_000, transcendentals=1_400_000),
    )(core, limits, query, out_grad, key_up_flat, value_up_flat, latent, gain, near, far)

    wgrad = lax.psum_scatter(wgrad, "x", scatter_dimension=0, tiled=True)
    wgrad = lax.psum_scatter(wgrad, "z", scatter_dimension=0, tiled=True)
    wgrad = wgrad.astype(f32).reshape(LATENT // (NX * NZ), steps, 2, HEADS_STEP, HEAD_DIM)
    key_up_grad = wgrad[:, :, 0].reshape(-1, HEADS_DEV, HEAD_DIM)
    value_up_grad = wgrad[:, :, 1].reshape(-1, HEADS_DEV, HEAD_DIM)

    paired = call(pair_kernel, shape(NY, TILES, ROWS, KV), [vmem(), vmem()])(keep, swap_cores(send))
    paired = exchange(paired, "y")
    dest = jnp.concatenate([place * BLOCKS_DEV + jnp.arange(BLOCKS_DEV, dtype=jnp.int32), listed])
    spread = call(
        scatter_kernel,
        shape(NX * NZ * BLOCKS_DEV, ROWS, KV),
        [smem(), vmem()],
        scratch_shapes=[pltpu.VMEM((NX * NZ * BLOCKS_DEV, ROWS, KV), f32)],
    )(dest, paired)
    spread = exchange(spread.reshape(NX, NZ * BLOCKS_DEV, ROWS, KV), "x")
    line = call(sum_kernel, shape(NZ * BLOCKS_DEV, ROWS, KV), [vmem()])(spread)
    line = exchange(line.reshape(NZ, BLOCKS_DEV, ROWS, KV), "z")
    total = call(sum_kernel, shape(NY, BLOCKS_DEV, ROWS, KV), [vmem()])(line)
    total = exchange(total, "y")
    latent_grad = call(
        final_kernel, shape(tokens, KV, dtype=f32), [smem(), vmem(), vmem(), vmem(), vmem()]
    )(core, total, swap_cores(total), latent, gain)
    return attn_out, query_grad, latent_grad, key_up_grad, value_up_grad


def solution(mesh):
    grid = Mesh(mesh.devices.reshape(NX, NZ, NY, NC), ("x", "z", "y", "c"))
    pos, head = ("x", "z"), ("y", "c")
    return jax.shard_map(
        shards,
        mesh=grid,
        in_specs=(
            P(pos, head),
            P(pos, None),
            P(),
            P(None, head, None),
            P(None, head, None),
            P(pos, head),
            P(pos, None),
            P(pos, None),
        ),
        out_specs=(
            P(pos, head),
            P(pos, head),
            P(pos, None),
            P(pos, head, None),
            P(pos, head, None),
        ),
        check_vma=False,
    )
```

time: 806 us -> 178 us (0.22)
  waiting for transfers between devices: 534 us -> 47.9 us
  local copies, waits for them, and re-layouts: 127 us -> 7.47 us
  matrix products: 85.2 us -> 0 us
  blocking collectives: 0 us -> 62 us
  Pallas kernels: 0 us -> 29.3 us
  other arithmetic: 13.8 us -> 0.08 us
  starting transfers between devices: 26.1 us -> 13.9 us
    psum x3 -> x0, waiting for transfers between devices: 218 us -> none  [the longest x1 112 us: shards(): lax.psum(trunk_grad.astype(jnp.bfloat16), 'pos').astype(jnp.float32)]
    reduce_scatter x1 -> x2, waiting for transfers between devices: 216 us -> 0.01 us  [the longest x1 0.01 us: shards(): wgrad = lax.psum_scatter(wgrad, 'x', scatter_dimension=0, tiled=True)]
    dot_general x16 -> x0, matrix products: 85.2 us -> none  [the longest x1 18.4 us: shards(): jnp.einsum('bhqk,bkx->bhqx', score_grad, key_tiles, preferred_element_typ...]
    all_to_all x0 -> x4, blocking collectives: none -> 62 us  [exchange(): return lax.all_to_all(values, axis, split_axis=0, concat_axis=0, tiled=True)]
    all_to_all x3, waiting for transfers between devices: 101 us -> 43.5 us  [exchange(): return lax.all_to_all(values, axis, split_axis=0, concat_axis=0, tiled=True)]
    reshape x6 -> x4, local copies, waits for them, and re-layouts: 32.6 us -> 2.99 us  [the longest x1 1.85 us: shards(): value_up_flat = value_up.reshape(LATENT, HEADS_DEV * HEAD_DIM)]
    pallas_call x0 -> x9, Pallas kernels: none -> 29.3 us  [the longest x1 23.8 us: shards(): call(attend_kernel, (shape(tokens, HEADS_DEV * HEAD_DIM), shape(tokens, H...]
    convert_element_type x5 -> x0, local copies, waits for them, and re-layouts: 17.9 us -> none  [the longest x2 16.3 us: shards(): fetched_grad.astype(jnp.bfloat16)]
  transfers between devices with their start and end apart: 7 -> 8, of which waited for: 6 -> 6; matrix products, arithmetic and copies ran while one was open for 14% -> 2% of each run, Pallas kernels for 0% -> 2%
where the time goes in v1:
time: 178 us; the launch traced here: 175 us
  blocking collectives  62 us (35%)
  waiting for transfers between devices  47.9 us (27%)
  Pallas kernels  29.3 us (16%)
  between operations  14.1 us (8%)
  starting transfers between devices  13.9 us (8%)
  local copies, waits for them, and re-layouts  7.47 us (4%)
    all_to_all x4, blocking collectives, exchange(): return lax.all_to_all(values, axis, split_axis=0, concat_axis=0, tiled=True)  62 us
    all_to_all x3, waiting for transfers between devices, exchange(): return lax.all_to_all(values, axis, split_axis=0, concat_axis=0, tiled=True)  43.5 us
    pallas_call x1, Pallas kernels, shards(): call(attend_kernel, (shape(tokens, HEADS_DEV * HEAD_DIM), shape(tokens, H...  23.8 us
    all_to_all x3, starting transfers between devices, exchange(): return lax.all_to_all(values, axis, split_axis=0, concat_axis=0, tiled=True)  13.5 us
    unnamed x20, local copies, waits for them, and re-layouts  3.78 us
    ppermute x3, waiting for transfers between devices, swap_cores(): return lax.ppermute(values, 'c', [(0, 1), (1, 0)])  3.7 us
  transfers between devices with their start and end apart: 8, of which 6 were waited for; matrix products, arithmetic and copies ran while one was open for 2% of the time, Pallas kernels for 2%

profile of v1, /device:TPU:2, one launch (start us, length us, event | category | flops | bytes accessed | tf_op | source)
XLA Modules:
  0.0 174.8 jit_solution(2210634143632138088)
XLA Ops:
  7.2 1.2 copy.14.latent_ref
  8.3 0.0 copy-start.1
  8.4 0.7 copy-done.1
  9.0 0.1 shard_map.119
  9.1 21.5 %all_to_all.35 = bf16[8,2,16,576]{3,2,1,0:T(8,128)(2,1)S(1)} all-to-all(bf16[8,2,16,576]{3,2,1,0:T(8,128)(2,1)S(1)} %shard_map.119), channel_id=1, replica_groups=mesh['x'=4,'z'=8,'y'=4,'c'=2] {'z'}, dimensions={0} | all-to-all | bytes 589824 | tf_op jit(solution)/shard_map/all_to_all | solution.py:246
  30.7 1.2 shard_map.120
  31.9 0.0 copy-start.7
  31.9 5.0 %all-to-all-start.1 = ((bf16[4,16,16,576]{3,2,1,0:T(8,128)(2,1)}), bf16[4,16,16,576]{3,2,1,0:T(8,128)(2,1)S(1)}, u32[]{:S(2)}, u32[]{:S(2)}) async-start(bf16[4,16,16,576]{3,2,1,0:T(8,128)(2,1)} %shard_map.120), calls=%async_computation.1 | async-start | bytes 2621440 | tf_op jit(solution)/shard_map/all_to_all | solution.py:246
  36.8 0.0 reduce-scatter.3.cloned.1.call-start
  36.8 0.0 copy-done.7
  36.8 0.1 reshape.54.anc_ref
  36.9 14.5 %all-to-all-done.1 = bf16[4,16,16,576]{3,2,1,0:T(8,128)(2,1)S(1)} async-done(((bf16[4,16,16,576]{3,2,1,0:T(8,128)(2,1)}), bf16[4,16,16,576]{3,2,1,0:T(8,128)(2,1)S(1)}, u32[]{:S(2)}, u32[]{:S(2)}) %all-to-all-start.1) | async-done | bytes 1179680 | tf_op jit(solution)/shard_map/all_to_all | solution.py:246
  51.4 0.0 copy-start.8
  51.4 0.0 copy-start.6
  51.4 0.6 shard_map.121
  52.0 13.1 %all_to_all.36.near_ref = bf16[4,8,16,576]{3,2,1,0:T(8,128)(2,1)S(1)} all-to-all(bf16[4,8,16,576]{3,2,1,0:T(8,128)(2,1)S(1)} %shard_map.121), channel_id=1, replica_groups=mesh['x'=4,'z'=8,'y'=4,'c'=2] {'y'}, dimensions={0} | all-to-all | bytes 1179648 | tf_op jit(solution)/shard_map/all_to_all | solution.py:246
  65.0 0.0 collective-permute-start
  65.0 0.0 copy-done.8
  65.0 0.1 reshape.50.vis_ref
  65.1 0.0 copy-done.6
  65.1 0.0 copy-start.2
  65.1 0.0 copy-start.4
  65.1 0.0 copy-start.5
  65.1 1.8 %copy_bitcast_fusion = (bf16[512,1024]{1,0:T(8,128)(2,1)S(1)}, bf16[512,1024]{1,0:T(8,128)(2,1)S(1)}) fusion(bf16[64,8,8,128]{3,2,1,0:T(8,128)(2,1)S(1)} %bitcast.21, bf16[64,8,8,128]{3,2,1,0:T(8,128)(2,1)} %bitcast.22), kind=kLoop, calls=%fused_computation | loop fusion | bytes 4194304 | tf_op jit(solution)/shard_map/reshape | solution.py:270
  67.0 0.1 collective-permute-done.far_ref
  67.1 0.0 copy-done.2
  67.1 0.0 copy-done.4
  67.1 0.0 copy-done.5
  67.1 23.8 %shard_map.122 = (bf16[256,1024]{1,0:T(8,128)(2,1)}, bf16[256,1536]{1,0:T(8,128)(2,1)}, bf16[512,2048]{1,0:T(8,128)(2,1)}, f32[4,10,16,576]{3,2,1,0:T(8,128)}, bf16[4,10,16,576]{3,2,1,0:T(8,128)(2,1)S(1)}) custom-call(s32[1]{0:T(128)} %bitcast.core_ref, s32[8]{0:T(128)S(1)} %reshape.50.vis_ref, bf16[256,1536]{1,0:T(8,128)(2,1)S(1)} %copy-done.4, ...), custom_call_target="tpu_custom_call" | custom-call | flops 11000000512 | bytes 16000000 | tf_op jit(solution)/shard_map/pallas_call | solution.py:282
  90.9 0.0 copy-start.3
  90.9 0.9 copy-done.3
  91.8 0.0 copy-start
  91.8 0.0 reduce-scatter.3.cloned.1.call-update
  91.9 0.5 collective-permute-start.1
  92.3 2.2 %collective-permute-done.1.recv_ref = bf16[4,10,16,576]{3,2,1,0:T(8,128)(2,1)S(1)} collective-permute-done((bf16[4,10,16,576]{3,2,1,0:T(8,128)(2,1)}, bf16[4,10,16,576]{3,2,1,0:T(8,128)(2,1)S(1)}, u32[]{:S(2)}, u32[]{:S(2)}) %collective-permute-start.1) | collective-permute-done | bytes 737312 | tf_op jit(solution)/shard_map/ppermute | solution.py:250
  94.5 0.0 copy-done
  94.5 1.1 shard_map.123
  95.6 3.5 %all-to-all-start.3 = ((bf16[4,10,16,576]{3,2,1,0:T(8,128)(2,1)}), bf16[4,10,16,576]{3,2,1,0:T(8,128)(2,1)S(1)}, u32[]{:S(2)}, u32[]{:S(2)}) async-start(bf16[4,10,16,576]{3,2,1,0:T(8,128)(2,1)} %shard_map.123), calls=%async_computation.3 | async-start | bytes 1638400 | tf_op jit(solution)/shard_map/all_to_all | solution.py:246
  99.1 0.1 pad_add_fusion.dest_ref
  99.2 13.3 %all-to-all-done.3.in_ref = bf16[4,10,16,576]{3,2,1,0:T(8,128)(2,1)S(1)} async-done(((bf16[4,10,16,576]{3,2,1,0:T(8,128)(2,1)}), bf16[4,10,16,576]{3,2,1,0:T(8,128)(2,1)S(1)}, u32[]{:S(2)}, u32[]{:S(2)}) %all-to-all-start.3) | async-done | bytes 737312 | tf_op jit(solution)/shard_map/all_to_all | solution.py:246
  112.5 2.0 %shard_map.124 = bf16[64,16,576]{2,1,0:T(8,128)(2,1)} custom-call(s32[10]{0:T(128)S(1)} %pad_add_fusion.dest_ref, bf16[4,10,16,576]{3,2,1,0:T(8,128)(2,1)S(1)} %all-to-all-done.3.in_ref), custom_call_target="tpu_custom_call" | custom-call | tf_op jit(solution)/shard_map/pallas_call | solution.py:330
  114.5 5.0 %all-to-all-start.4 = ((bf16[4,16,16,576]{3,2,1,0:T(8,128)(2,1)}), bf16[4,16,16,576]{3,2,1,0:T(8,128)(2,1)S(1)}, u32[]{:S(2)}, u32[]{:S(2)}) async-start(bf16[4,16,16,576]{3,2,1,0:T(8,128)(2,1)} %bitcast.5), calls=%async_computation.4 | async-start | bytes 2621440 | tf_op jit(solution)/shard_map/all_to_all | solution.py:246
  119.5 0.0 reduce-scatter.5.cloned.1.call-start
  119.5 0.0 reduce-scatter.3.cloned.1.call-done
  119.5 0.7 reduce-scatter.5.cloned.1.call-update
  120.3 15.7 %all-to-all-done.4.in_ref = bf16[4,16,16,576]{3,2,1,0:T(8,128)(2,1)S(1)} async-done(((bf16[4,16,16,576]{3,2,1,0:T(8,128)(2,1)}), bf16[4,16,16,576]{3,2,1,0:T(8,128)(2,1)S(1)}, u32[]{:S(2)}, u32[]{:S(2)}) %all-to-all-start.4) | async-done | bytes 1179680 | tf_op jit(solution)/shard_map/all_to_all | solution.py:246
  136.0 0.2 shard_map.125
  136.1 17.2 %all_to_all.37.in_ref = bf16[8,2,16,576]{3,2,1,0:T(8,128)(2,1)S(1)} all-to-all(bf16[8,2,16,576]{3,2,1,0:T(8,128)(2,1)S(1)} %bitcast.17), channel_id=1, replica_groups=mesh['x'=4,'z'=8,'y'=4,'c'=2] {'z'}, dimensions={0} | all-to-all | bytes 589824 | tf_op jit(solution)/shard_map/all_to_all | solution.py:246
  153.3 10.2 %all_to_all.38.near_ref = bf16[4,2,16,576]{3,2,1,0:T(8,128)(2,1)S(1)} all-to-all(bf16[4,2,16,576]{3,2,1,0:T(8,128)(2,1)S(1)} %shard_map.126), channel_id=1, replica_groups=mesh['x'=4,'z'=8,'y'=4,'c'=2] {'y'}, dimensions={0} | all-to-all | bytes 294912 | tf_op jit(solution)/shard_map/all_to_all | solution.py:246
  163.6 0.0 collective-permute-start.2
  163.6 1.4 collective-permute-done.2.far_ref
  165.0 0.3 shard_map.127
  165.3 1.0 copy.16
  166.3 0.0 reduce-scatter.5.cloned.1.call-done
  166.3 1.0 reshape.63
  167.3 0.7 fusion
  (2 shorter events, 0.1 us)
Async XLA Ops:
  8.3 0.7 copy-start.1
  31.9 5.0 %copy-start.7 = (s32[2,4]{1,0:T(2,128)S(1)}, s32[2,4]{1,0:T(2,128)}, u32[]{:S(2)}) copy-start(s32[2,4]{1,0:T(2,128)} %param.14) | copy-start | bytes 100
  31.9 19.5 %all-to-all-start.1 = ((bf16[4,16,16,576]{3,2,1,0:T(8,128)(2,1)}), bf16[4,16,16,576]{3,2,1,0:T(8,128)(2,1)S(1)}, u32[]{:S(2)}, u32[]{:S(2)}) async-start(bf16[4,16,16,576]{3,2,1,0:T(8,128)(2,1)} %shard_map.120), calls=%async_computation.1 | async-start | bytes 2621440 | tf_op jit(solution)/shard_map/all_to_all | solution.py:246
  36.8 82.7 %reduce-scatter.3.cloned.1.call-start = ((), (), s32[]{:S(2)}) async-start(), calls=%async_computation.9 | async-start | bytes 2621440 | tf_op jit(solution)/shard_map/reduce_scatter | solution.py:321
  51.4 13.7 %copy-start.8 = (s32[2,4]{1,0:T(2,128)S(1)}, s32[2,4]{1,0:T(2,128)}, u32[]{:S(2)}) copy-start(s32[2,4]{1,0:T(2,128)} %param.15) | copy-start | bytes 100
  51.4 13.7 %copy-start.6 = (bf16[512,8,128]{2,1,0:T(8,128)(2,1)S(1)}, bf16[512,8,128]{2,1,0:T(8,128)(2,1)}, u32[]{:S(2)}) copy-start(bf16[512,8,128]{2,1,0:T(8,128)(2,1)} %param.12) | copy-start | bytes 3145732
  65.0 2.1 %collective-permute-start = (bf16[4,8,16,576]{3,2,1,0:T(8,128)(2,1)S(1)}, bf16[4,8,16,576]{3,2,1,0:T(8,128)(2,1)S(1)}, u32[]{:S(2)}, u32[]{:S(2)}) collective-permute-start(bf16[4,8,16,576]{3,2,1,0:T(8,128)(2,1)S(1)} %all_to_all.36.near_ref), channel_id=1, source_target_pairs={{0,1},{1,0},{2,3},{3,2},{4,5},{5,4},{6,7},{7,6},{8,9},{9,8},{10,11... | collective-permute-start | bytes 1769480 | tf_op jit(solution)/shard_map/ppermute | solution.py:250
  65.1 2.0 %copy-start.2 = (f32[512]{0:T(512)S(1)}, f32[512]{0:T(512)}, u32[]{:S(2)}) copy-start(f32[512]{0:T(512)} %param.10) | copy-start | bytes 6148
  65.1 2.0 %copy-start.4 = (bf16[256,1536]{1,0:T(8,128)(2,1)S(1)}, bf16[256,1536]{1,0:T(8,128)(2,1)}, u32[]{:S(2)}) copy-start(bf16[256,1536]{1,0:T(8,128)(2,1)} %query_ref.1) | copy-start | bytes 2359300
  65.1 2.0 %copy-start.5 = (bf16[256,1024]{1,0:T(8,128)(2,1)S(1)}, bf16[256,1024]{1,0:T(8,128)(2,1)}, u32[]{:S(2)}) copy-start(bf16[256,1024]{1,0:T(8,128)(2,1)} %grad_ref.1) | copy-start | bytes 1572868
  90.9 0.9 copy-start.3
  91.8 2.7 %copy-start = (f32[4,10,16,576]{3,2,1,0:T(8,128)S(1)}, f32[4,10,16,576]{3,2,1,0:T(8,128)}, u32[]{:S(2)}) copy-start(f32[4,10,16,576]{3,2,1,0:T(8,128)} %get-tuple-element.12.keep_ref) | copy-start | bytes 4423684
  91.9 2.6 %collective-permute-start.1 = (bf16[4,10,16,576]{3,2,1,0:T(8,128)(2,1)}, bf16[4,10,16,576]{3,2,1,0:T(8,128)(2,1)S(1)}, u32[]{:S(2)}, u32[]{:S(2)}) collective-permute-start(bf16[4,10,16,576]{3,2,1,0:T(8,128)(2,1)} %copy-done.3), channel_id=1, source_target_pairs={{0,1},{1,0},{2,3},{3,2},{4,5},{5,4},{6,7},{7,6},{8,9},{9,8},{10,11... | collective-permute-start | bytes 2211848 | tf_op jit(solution)/shard_map/ppermute | solution.py:250
  95.6 16.9 %all-to-all-start.3 = ((bf16[4,10,16,576]{3,2,1,0:T(8,128)(2,1)}), bf16[4,10,16,576]{3,2,1,0:T(8,128)(2,1)S(1)}, u32[]{:S(2)}, u32[]{:S(2)}) async-start(bf16[4,10,16,576]{3,2,1,0:T(8,128)(2,1)} %shard_map.123), calls=%async_computation.3 | async-start | bytes 1638400 | tf_op jit(solution)/shard_map/all_to_all | solution.py:246
  114.5 21.4 %all-to-all-start.4 = ((bf16[4,16,16,576]{3,2,1,0:T(8,128)(2,1)}), bf16[4,16,16,576]{3,2,1,0:T(8,128)(2,1)S(1)}, u32[]{:S(2)}, u32[]{:S(2)}) async-start(bf16[4,16,16,576]{3,2,1,0:T(8,128)(2,1)} %bitcast.5), calls=%async_computation.4 | async-start | bytes 2621440 | tf_op jit(solution)/shard_map/all_to_all | solution.py:246
  119.5 46.8 %reduce-scatter.5.cloned.1.call-start = ((), (), s32[]{:S(2)}) async-start(), calls=%async_computation.10 | async-start | bytes 589824 | tf_op jit(solution)/shard_map/reduce_scatter | solution.py:322
  163.6 1.4 collective-permute-start.2
Sparse Core Ops, SparseCore 0:
  92.0 26.5 reduce-scatter.2
  123.0 40.0 reduce-scatter.4

commit v2 on v1

v2 whole, which is shorter than its diff:
```python
import functools
import math

import jax
import jax.numpy as jnp
from jax import lax
from jax.experimental import pallas as pl
from jax.experimental.pallas import tpu as pltpu
from jax.sharding import Mesh
from jax.sharding import PartitionSpec as P

LATENT = 512
ROPE = 64
KV = LATENT + ROPE
HEAD_DIM = 128
QDIM = HEAD_DIM + ROPE
BLOCK = 128
SLOTS = 4
BLOCKS_DEV = 2
NX, NZ, NY, NC = 4, 8, 4, 2
SHARES = NY * NC
ROWS = BLOCK // SHARES
HALF = NY * ROWS
HEADS_DEV = 8
TILES = BLOCKS_DEV * (1 + SLOTS)
KEYS = (1 + SLOTS) * BLOCK
COLUMN = NZ * BLOCKS_DEV
PART = LATENT // NX
HEADS_STEP = 4
norm_epsilon = 1e-06

bf16 = jnp.bfloat16
f32 = jnp.float32
VMEM_LIMIT = 48 * 1024 * 1024


def dot(a, b):
    return lax.dot_general(a, b, (((1,), (0,)), ((), ())), preferred_element_type=f32)


def dot_nt(a, b):
    return lax.dot_general(a, b, (((1,), (1,)), ((), ())), preferred_element_type=f32)


def dot_tn(a, b):
    return lax.dot_general(a, b, (((0,), (0,)), ((), ())), preferred_element_type=f32)


def smem():
    return pl.BlockSpec(memory_space=pltpu.SMEM)


def vmem():
    return pl.BlockSpec(memory_space=pltpu.VMEM)


def norm_inverse(raw):
    return lax.rsqrt(jnp.mean(raw * raw, axis=1, keepdims=True) + norm_epsilon)


def share_kernel(share_ref, latent_ref, gain_ref, out_ref):
    for b in range(BLOCKS_DEV):
        start = pl.multiple_of(b * BLOCK + share_ref[0] * ROWS, ROWS)
        raw = latent_ref[pl.ds(start, ROWS), :LATENT].astype(f32)
        keys = (raw * norm_inverse(raw) * gain_ref[...]).astype(bf16)
        rope = latent_ref[pl.ds(start, ROWS), LATENT:]
        for z in range(NZ):
            out_ref[z, b, :, :LATENT] = keys
            out_ref[z, b, :, LATENT:] = rope


def spread_kernel(x_ref, l0, l1, l2, l3, column_ref, out_ref):
    for r, listed in enumerate((l0, l1, l2, l3)):
        to = (x_ref[0] + r) % NX
        for s in range(BLOCKS_DEV * SLOTS):
            out_ref[to, s] = column_ref[listed[s] % COLUMN]


def select_kernel(listed_ref, all_ref, out_ref):
    for s in range(BLOCKS_DEV * SLOTS):
        tile = all_ref[listed_ref[s] // COLUMN, s]
        for y in range(NY):
            out_ref[y, s] = tile


def attend_kernel(
    core_ref, vis_ref, query_ref, grad_ref, key_up_ref, value_up_ref, latent_ref, gain_ref, near_ref, far_ref,
    sgrad_ref, weights_ref, klat, krope, keep_ref, send_ref,
    bias, glat, grope,
):
    step = pl.program_id(0)
    core = core_ref[0]
    scale = 1.0 / math.sqrt(QDIM)

    @pl.when(step == 0)
    def _():
        raw = latent_ref[:, :LATENT].astype(f32)
        own = (raw * norm_inverse(raw) * gain_ref[...]).astype(bf16)
        own = own.reshape(BLOCKS_DEV, NY, NC, ROWS, LATENT)
        rope = latent_ref[:, LATENT:].reshape(BLOCKS_DEV, NY, NC, ROWS, ROPE)
        for b in range(BLOCKS_DEV):
            for side in range(NC):
                for y in range(NY):
                    at = side * HALF + y * ROWS
                    first = core == side
                    klat[b, at : at + ROWS, :] = jnp.where(first, own[b, y, 0], own[b, y, 1])
                    krope[b, at : at + ROWS, :] = jnp.where(first, rope[b, y, 0], rope[b, y, 1])
                    for j in range(SLOTS):
                        src = (near_ref, far_ref)[side]
                        to = (1 + j) * BLOCK + at
                        klat[b, to : to + ROWS, :] = src[y, b * SLOTS + j, :, :LATENT]
                        krope[b, to : to + ROWS, :] = src[y, b * SLOTS + j, :, LATENT:]
        col = lax.broadcasted_iota(jnp.int32, (BLOCK, BLOCK), 1)
        row = lax.broadcasted_iota(jnp.int32, (BLOCK, BLOCK), 0)
        side = jnp.where(col >= HALF, 1, 0)
        rest = col - side * HALF
        piece = rest // ROWS
        owner = jnp.where(core == 0, side, 1 - side)
        offset = (piece * NC + owner) * ROWS + (rest - piece * ROWS)
        for b in range(BLOCKS_DEV):
            bias[b, :, :BLOCK] = jnp.where(offset <= row, 0.0, -jnp.inf)
            for j in range(SLOTS):
                limit = vis_ref[b * SLOTS + j]
                bias[b, :, (1 + j) * BLOCK : (2 + j) * BLOCK] = jnp.where(offset < limit, 0.0, -jnp.inf)
        glat[...] = jnp.zeros_like(glat)
        grope[...] = jnp.zeros_like(grope)

    heads = range(HEADS_STEP)
    nope = [query_ref[:, h * QDIM : h * QDIM + HEAD_DIM] for h in heads]
    rope = [query_ref[:, h * QDIM + HEAD_DIM : (h + 1) * QDIM] for h in heads]
    grad = [grad_ref[:, h * HEAD_DIM : (h + 1) * HEAD_DIM] for h in heads]
    key_up = [key_up_ref[:, h * HEAD_DIM : (h + 1) * HEAD_DIM] for h in heads]
    value_up = [value_up_ref[:, h * HEAD_DIM : (h + 1) * HEAD_DIM] for h in heads]
    absorbed = [dot_nt(nope[h], key_up[h]).astype(bf16) for h in heads]
    mixed_grad = [dot_nt(grad[h], value_up[h]).astype(bf16) for h in heads]

    for b in range(BLOCKS_DEV):
        rows = slice(b * BLOCK, (b + 1) * BLOCK)
        ab = jnp.concatenate([absorbed[h][rows] for h in heads], axis=0)
        rb = jnp.concatenate([rope[h][rows] for h in heads], axis=0)
        mg = jnp.concatenate([mixed_grad[h][rows] for h in heads], axis=0)
        lat = klat[b]
        rop = krope[b]
        mask = jnp.concatenate([bias[b]] * HEADS_STEP, axis=0)
        scores = (dot_nt(ab, lat) + dot_nt(rb, rop)) * scale + mask
        exp_terms = jnp.exp(scores - jnp.max(scores, axis=1, keepdims=True))
        weights = exp_terms * (1.0 / jnp.sum(exp_terms, axis=1, keepdims=True))
        half = weights.astype(bf16)
        weights_ref[b] = half
        weight_grad = dot_nt(mg, lat)
        inner = jnp.sum(weights * weight_grad, axis=1, keepdims=True)
        score_grad = (weights * (weight_grad - inner) * scale).astype(bf16)
        sgrad_ref[b] = score_grad
        both = jnp.concatenate([score_grad, half], axis=0)
        glat[b] += dot_tn(both, jnp.concatenate([ab, mg], axis=0))
        grope[b] += dot_tn(score_grad, rb)

    @pl.when(step == pl.num_programs(0) - 1)
    def _():
        for b in range(BLOCKS_DEV):
            for j in range(1 + SLOTS):
                tile = b if j == 0 else BLOCKS_DEV + b * SLOTS + j - 1
                for y in range(NY):
                    at = j * BLOCK + y * ROWS
                    keep_ref[y, tile, :, :LATENT] = glat[b, at : at + ROWS, :]
                    keep_ref[y, tile, :, LATENT:] = grope[b, at : at + ROWS, :]
                    at = at + HALF
                    send_ref[y, tile, :, :LATENT] = glat[b, at : at + ROWS, :].astype(bf16)
                    send_ref[y, tile, :, LATENT:] = grope[b, at : at + ROWS, :].astype(bf16)


def project_kernel(
    x_ref, query_ref, grad_ref, key_up_ref, value_up_ref, sgrad_ref, weights_ref, klat, krope,
    attn_ref, qgrad_ref, w0_ref, w1_ref, w2_ref, w3_ref,
    wgrad,
):
    heads = range(HEADS_STEP)
    nope = [query_ref[:, h * QDIM : h * QDIM + HEAD_DIM] for h in heads]
    grad = [grad_ref[:, h * HEAD_DIM : (h + 1) * HEAD_DIM] for h in heads]
    key_up = [key_up_ref[:, h * HEAD_DIM : (h + 1) * HEAD_DIM] for h in heads]
    value_up = [value_up_ref[:, h * HEAD_DIM : (h + 1) * HEAD_DIM] for h in heads]
    mixed_parts, full_parts, rope_parts = [], [], []
    for b in range(BLOCKS_DEV):
        score_grad = sgrad_ref[b]
        mixed_parts.append(dot(weights_ref[b], klat[b]).astype(bf16))
        full_parts.append(dot(score_grad, klat[b]).astype(bf16))
        rope_parts.append(dot(score_grad, krope[b]).astype(bf16))

    def head_rows(parts, h):
        return jnp.concatenate([part[h * BLOCK : (h + 1) * BLOCK] for part in parts], axis=0)

    width = HEADS_STEP * HEAD_DIM
    for h in heads:
        mixed = head_rows(mixed_parts, h)
        full = head_rows(full_parts, h)
        attn_ref[:, h * HEAD_DIM : (h + 1) * HEAD_DIM] = dot(mixed, value_up[h]).astype(bf16)
        qgrad_ref[:, h * QDIM : h * QDIM + HEAD_DIM] = dot(full, key_up[h]).astype(bf16)
        qgrad_ref[:, h * QDIM + HEAD_DIM : (h + 1) * QDIM] = head_rows(rope_parts, h)
        at = h * HEAD_DIM
        wgrad[:, at : at + HEAD_DIM] = dot_tn(full, nope[h]).astype(bf16)
        wgrad[:, width + at : width + at + HEAD_DIM] = dot_tn(mixed, grad[h]).astype(bf16)

    for r, out in enumerate((w0_ref, w1_ref, w2_ref, w3_ref)):
        start = pl.multiple_of(((x_ref[0] + r) % NX) * PART, PART)
        out[...] = wgrad[pl.ds(start, PART), :]


def pair_kernel(y_ref, keep_ref, recv_ref, own_ref, s1_ref, s2_ref, s3_ref):
    for r, out in enumerate((own_ref, s1_ref, s2_ref, s3_ref)):
        y = (y_ref[0] + r) % NY
        out[...] = (keep_ref[y] + recv_ref[y].astype(f32)).astype(out.dtype)


def slots_kernel(own_ref, r1_ref, r2_ref, r3_ref, mine_ref, out_ref):
    total = own_ref[...] + r1_ref[...].astype(f32) + r2_ref[...].astype(f32) + r3_ref[...].astype(f32)
    mine_ref[...] = total[:BLOCKS_DEV]
    out_ref[...] = total[BLOCKS_DEV:].astype(bf16)


def column_kernel(x_ref, z_ref, l0, l1, l2, l3, mine_ref, i0, i1, i2, i3, out_ref, acc):
    acc[...] = jnp.zeros_like(acc)
    for b in range(BLOCKS_DEV):
        acc[z_ref[0] * BLOCKS_DEV + b] = mine_ref[b]
    for listed, in_ref in ((l0, i0), (l1, i1), (l2, i2), (l3, i3)):
        for s in range(BLOCKS_DEV * SLOTS):
            block = listed[s]

            @pl.when(block // COLUMN == x_ref[0])
            def _():
                at = block % COLUMN
                acc[at] = acc[at] + in_ref[s].astype(f32)

    for z in range(NZ):
        for b in range(BLOCKS_DEV):
            out_ref[z, b] = acc[z * BLOCKS_DEV + b].astype(bf16)


def line_kernel(in_ref, out_ref):
    total = in_ref[0].astype(f32)
    for z in range(1, NZ):
        total = total + in_ref[z].astype(f32)
    out_ref[...] = total.astype(bf16)


def part_kernel(w0, w1, w2, w3, out_ref):
    for z in range(NZ):
        rows = slice(z * ROWS, (z + 1) * ROWS)
        out_ref[z] = sum(ref[rows].astype(f32) for ref in (w0, w1, w2, w3)).astype(bf16)


def weights_kernel(in_ref, key_ref, value_ref):
    total = sum(in_ref[z].astype(f32) for z in range(NZ))
    for h in range(HEADS_DEV):
        at = (h // HEADS_STEP) * 2 * HEADS_STEP * HEAD_DIM + (h % HEADS_STEP) * HEAD_DIM
        key_ref[:, h, :] = total[:, at : at + HEAD_DIM]
        at = at + HEADS_STEP * HEAD_DIM
        value_ref[:, h, :] = total[:, at : at + HEAD_DIM]


def cores_kernel(core_ref, near_ref, far_ref, out_ref):
    for b in range(BLOCKS_DEV):
        out_ref[b, core_ref[0]] = near_ref[b]
        out_ref[b, 1 - core_ref[0]] = far_ref[b]


def final_kernel(y_ref, i0, i1, i2, i3, latent_ref, gain_ref, out_ref):
    for r, in_ref in enumerate((i0, i1, i2, i3)):
        y = (y_ref[0] - r + NY) % NY
        for b in range(BLOCKS_DEV):
            total = in_ref[b].reshape(NC * ROWS, KV).astype(f32)
            rows = pl.ds(pl.multiple_of(b * BLOCK + y * NC * ROWS, NC * ROWS), NC * ROWS)
            raw = latent_ref[rows, :LATENT].astype(f32)
            inverse = norm_inverse(raw)
            gained = total[:, :LATENT] * gain_ref[...]
            out_ref[rows, :LATENT] = inverse * gained - raw * inverse * inverse * inverse * jnp.mean(
                raw * gained, axis=1, keepdims=True
            )
            out_ref[rows, LATENT:] = total[:, LATENT:]


def call(kernel, out_shape, in_specs, **kw):
    return pl.pallas_call(
        kernel,
        out_shape=out_shape,
        in_specs=in_specs,
        out_specs=kw.pop("out_specs", vmem()),
        compiler_params=pltpu.CompilerParams(vmem_limit_bytes=VMEM_LIMIT),
        **kw,
    )


def shape(*dims, dtype=bf16):
    return jax.ShapeDtypeStruct(dims, dtype)


def exchange(values, axis):
    return lax.all_to_all(values, axis, split_axis=0, concat_axis=0, tiled=True)


def shift(values, axis, count, by):
    return lax.ppermute(values, axis, [(i, (i + by) % count) for i in range(count)])


def swap_cores(values):
    return lax.ppermute(values, "c", [(0, 1), (1, 0)])


def columns(rows, cols):
    return pl.BlockSpec((rows, cols), lambda g: (0, g))


def whole(*dims):
    return pl.BlockSpec(dims, lambda g: (0,) * len(dims))


def cost(flops):
    return pl.CostEstimate(flops=flops, bytes_accessed=8_000_000, transcendentals=0)


def shards(query, latent, norm_gain, key_up, value_up, out_grad, ancestors, visible):
    def index(axis):
        return lax.axis_index(axis).astype(jnp.int32).reshape(1)

    core, x, y, z = index("c"), index("x"), index("y"), index("z")
    share = y * NC + core
    gain = norm_gain.reshape(1, LATENT)
    listed = ancestors.reshape(BLOCKS_DEV * SLOTS)
    limits = visible.reshape(BLOCKS_DEV * SLOTS)
    slots = BLOCKS_DEV * SLOTS
    lists = [listed] + [shift(listed, "x", NX, -r) for r in range(1, NX)]

    mine = call(share_kernel, shape(NZ, BLOCKS_DEV, ROWS, KV), [smem(), vmem(), vmem()])(share, latent, gain)
    key_up_flat = key_up.reshape(LATENT, HEADS_DEV * HEAD_DIM)
    value_up_flat = value_up.reshape(LATENT, HEADS_DEV * HEAD_DIM)
    column = exchange(mine, "z").reshape(COLUMN, ROWS, KV)
    column = call(spread_kernel, shape(NX, slots, ROWS, KV), [smem()] * 5 + [vmem()])(x, *lists, column)
    column, key_up_flat, value_up_flat = lax.optimization_barrier((column, key_up_flat, value_up_flat))
    column = exchange(column, "x")
    picked = call(select_kernel, shape(NY, slots, ROWS, KV), [smem(), vmem()])(listed, column)
    near = exchange(picked, "y")
    far = swap_cores(near)

    tokens = query.shape[0]
    steps = HEADS_DEV // HEADS_STEP
    width = HEADS_STEP * HEAD_DIM
    wcols = 2 * HEADS_DEV * HEAD_DIM
    rows = HEADS_DEV * BLOCK
    lat_keys, rope_keys = (BLOCKS_DEV, KEYS, LATENT), (BLOCKS_DEV, KEYS, ROPE)
    tiles = (NY, TILES, ROWS, KV)
    operands = (query, out_grad, key_up_flat, value_up_flat)
    operand_specs = [columns(tokens, HEADS_STEP * QDIM), columns(tokens, width), columns(LATENT, width), columns(LATENT, width)]
    by_rows = pl.BlockSpec((BLOCKS_DEV, HEADS_STEP * BLOCK, KEYS), lambda g: (0, g, 0))
    score_grad, weights, klat, krope, keep, send = call(
        attend_kernel,
        (shape(BLOCKS_DEV, rows, KEYS),) * 2 + (shape(*lat_keys), shape(*rope_keys), shape(*tiles, dtype=f32), shape(*tiles)),
        [smem()] * 2 + operand_specs + [whole(tokens, KV), whole(1, LATENT)] + [whole(NY, slots, ROWS, KV)] * 2,
        out_specs=(by_rows, by_rows, whole(*lat_keys), whole(*rope_keys), whole(*tiles), whole(*tiles)),
        grid=(steps,),
        scratch_shapes=[
            pltpu.VMEM((BLOCKS_DEV, BLOCK, KEYS), f32),
            pltpu.VMEM(lat_keys, f32),
            pltpu.VMEM(rope_keys, f32),
        ],
        cost_estimate=cost(6_200_000_000),
    )(core, limits, *operands, latent, gain, near, far)

    own, s1, s2, s3 = call(
        pair_kernel,
        (shape(TILES, ROWS, KV, dtype=f32),) + (shape(TILES, ROWS, KV),) * 3,
        [smem(), vmem(), vmem()],
        out_specs=(vmem(),) * 4,
    )(y, keep, swap_cores(send))
    others = [shift(s, "y", NY, r) for r, s in ((1, s1), (2, s2), (3, s3))]
    own, score_grad = lax.optimization_barrier((own, score_grad))
    attn_out, query_grad, *wgrads = call(
        project_kernel,
        (shape(tokens, HEADS_DEV * HEAD_DIM), shape(tokens, HEADS_DEV * QDIM)) + (shape(PART, wcols),) * NX,
        [smem()] + operand_specs + [by_rows, by_rows, whole(*lat_keys), whole(*rope_keys)],
        out_specs=(columns(tokens, width), columns(tokens, HEADS_STEP * QDIM)) + (columns(PART, 2 * width),) * NX,
        grid=(steps,),
        scratch_shapes=[pltpu.VMEM((LATENT, 2 * width), bf16)],
        cost_estimate=cost(4_000_000_000),
    )(x, *operands, score_grad, weights, klat, krope)
    parts = [shift(w, "x", NX, r) for r, w in enumerate(wgrads) if r > 0]
    *others, wgrads[0] = lax.optimization_barrier((*others, wgrads[0]))
    own, spread = call(
        slots_kernel,
        (shape(BLOCKS_DEV, ROWS, KV, dtype=f32), shape(slots, ROWS, KV)),
        [vmem()] * 4,
        out_specs=(vmem(), vmem()),
    )(own, *others)
    others = [shift(spread, "x", NX, -r) for r in range(1, NX)]
    line = call(
        column_kernel,
        shape(NZ, BLOCKS_DEV, ROWS, KV),
        [smem()] * 6 + [vmem()] * 5,
        scratch_shapes=[pltpu.VMEM((COLUMN, ROWS, KV), f32)],
    )(x, z, *lists, own, spread, *others)
    line = exchange(line, "z")
    line, *parts = lax.optimization_barrier((line, *parts))
    part = call(part_kernel, shape(NZ, ROWS, wcols), [vmem()] * NX)(wgrads[0], *parts)
    part = exchange(part, "z")
    total = call(line_kernel, shape(BLOCKS_DEV, ROWS, KV), [vmem()])(line)
    total = call(cores_kernel, shape(BLOCKS_DEV, NC, ROWS, KV), [smem(), vmem(), vmem()])(
        core, total, swap_cores(total)
    )
    others = [shift(total, "y", NY, r) for r in range(1, NY)]
    latent_grad = call(final_kernel, shape(tokens, KV, dtype=f32), [smem()] + [vmem()] * 6)(
        y, total, *others, latent, gain
    )
    grad_shape = shape(PART // NZ, HEADS_DEV, HEAD_DIM, dtype=f32)
    key_up_grad, value_up_grad = call(
        weights_kernel, (grad_shape, grad_shape), [vmem()], out_specs=(vmem(), vmem())
    )(part)
    return attn_out, query_grad, latent_grad, key_up_grad, value_up_grad


def solution(mesh):
    grid = Mesh(mesh.devices.reshape(NX, NZ, NY, NC), ("x", "z", "y", "c"))
    pos, head = ("x", "z"), ("y", "c")
    return jax.shard_map(
        shards,
        mesh=grid,
        in_specs=(
            P(pos, head),
            P(pos, None),
            P(),
            P(None, head, None),
            P(None, head, None),
            P(pos, head),
            P(pos, None),
            P(pos, None),
        ),
        out_specs=(
            P(pos, head),
            P(pos, head),
            P(pos, None),
            P(pos, head, None),
            P(pos, head, None),
        ),
        check_vma=False,
    )
```

time: 178 us -> 148 us (0.83); the launches traced: 175 us -> 147 us
  blocking collectives: 62 us -> 25.5 us
  starting transfers between devices: 13.9 us -> 41.2 us
  between operations: 14.1 us -> 0.83 us
  waiting for transfers between devices: 47.9 us -> 37.7 us
  Pallas kernels: 29.3 us -> 32.1 us
  local copies, waits for them, and re-layouts: 7.47 us -> 9.39 us
    all_to_all x4 -> x2, blocking collectives: 62 us -> 25.5 us  [exchange(): return lax.all_to_all(values, axis, split_axis=0, concat_axis=0, tiled=True)]
    all_to_all x3, waiting for transfers between devices: 43.5 us -> 11.3 us  [exchange(): return lax.all_to_all(values, axis, split_axis=0, concat_axis=0, tiled=True)]
    ppermute x0 -> x15, starting transfers between devices: none -> 25.5 us  [shift(): lax.ppermute(values, axis, [(i, (i + by) % count) for i in range(count)])]
    ppermute x0 -> x15, waiting for transfers between devices: none -> 20.9 us  [shift(): lax.ppermute(values, axis, [(i, (i + by) % count) for i in range(count)])]
    unnamed x20 -> x18, local copies, waits for them, and re-layouts: 3.78 us -> 6.5 us
    pallas_call x8 -> x12, Pallas kernels: 29.2 us -> 31.2 us  [the longest x1 15.9 us: shards(): call(attend_kernel, (shape(BLOCKS_DEV, rows, KEYS),) * 2 + (shape(*lat_ke...]
    all_to_all x3, starting transfers between devices: 13.5 us -> 15.4 us  [exchange(): return lax.all_to_all(values, axis, split_axis=0, concat_axis=0, tiled=True)]
    ppermute x3, waiting for transfers between devices: 3.7 us -> 5.55 us  [swap_cores(): return lax.ppermute(values, 'c', [(0, 1), (1, 0)])]
  transfers between devices with their start and end apart: 8 -> 21, of which waited for: 6 -> 12; matrix products, arithmetic and copies ran while one was open for 2% -> 3% of each run, Pallas kernels for 2% -> 8%
where the time goes in v2:
time: 148 us; the launch traced here: 147 us
  starting transfers between devices  41.2 us (28%)
  waiting for transfers between devices  37.7 us (25%)
  Pallas kernels  32.1 us (22%)
  blocking collectives  25.5 us (17%)
  local copies, waits for them, and re-layouts  9.39 us (6%)
    ppermute x15, starting transfers between devices, shift(): lax.ppermute(values, axis, [(i, (i + by) % count) for i in range(count)])  25.5 us
    all_to_all x2, blocking collectives, exchange(): return lax.all_to_all(values, axis, split_axis=0, concat_axis=0, tiled=True)  25.5 us
    ppermute x15, waiting for transfers between devices, shift(): lax.ppermute(values, axis, [(i, (i + by) % count) for i in range(count)])  20.9 us
    pallas_call x1, Pallas kernels, shards(): call(attend_kernel, (shape(BLOCKS_DEV, rows, KEYS),) * 2 + (shape(*lat_ke...  15.9 us
    all_to_all x3, starting transfers between devices, exchange(): return lax.all_to_all(values, axis, split_axis=0, concat_axis=0, tiled=True)  15.4 us
    all_to_all x3, waiting for transfers between devices, exchange(): return lax.all_to_all(values, axis, split_axis=0, concat_axis=0, tiled=True)  11.3 us
    pallas_call x1, Pallas kernels, shards(): call(project_kernel, (shape(tokens, HEADS_DEV * HEAD_DIM), shape(tokens,...  9.83 us
    unnamed x18, local copies, waits for them, and re-layouts  6.5 us
  transfers between devices with their start and end apart: 21, of which 12 were waited for; matrix products, arithmetic and copies ran while one was open for 3% of the time, Pallas kernels for 8%

profile of v2, /device:TPU:2, one launch (start us, length us, event | category | flops | bytes accessed | tf_op | source)
XLA Modules:
  0.0 146.6 jit_solution(14695885083495097507)
XLA Ops:
  0.6 1.2 copy.13.latent_ref
  1.8 0.0 copy-start.1
  1.8 0.7 copy-done.1
  2.5 0.8 shard_map.119
  3.3 8.5 %all-to-all-start = ((bf16[8,2,16,576]{3,2,1,0:T(8,128)(2,1)}), bf16[8,2,16,576]{3,2,1,0:T(8,128)(2,1)S(1)}, u32[]{:S(2)}, u32[]{:S(2)}) async-start(bf16[8,2,16,576]{3,2,1,0:T(8,128)(2,1)} %shard_map.119), calls=%async_computation | async-start | bytes 655360 | tf_op jit(solution)/shard_map/all_to_all | solution.py:297
  11.8 0.8 reshape.41.l0.listed_ref
  12.6 1.5 %collective-permute-start.2 = (s32[8]{0:T(128)S(1)}, s32[8]{0:T(128)S(1)}, u32[]{:S(2)}, u32[]{:S(2)}) collective-permute-start(s32[8]{0:T(128)S(1)} %reshape.41.l0.listed_ref), channel_id=1, source_target_pairs={{0,64},{64,128},{128,192},{192,0},{1,65},{65,129},{129,193},{193,1... | collective-permute-start | bytes 104 | tf_op jit(solution)/shard_map/ppermute | solution.py:301
  14.0 1.1 collective-permute-start.1
  15.2 2.2 %collective-permute-start = (s32[8]{0:T(128)S(1)}, s32[8]{0:T(128)S(1)}, u32[]{:S(2)}, u32[]{:S(2)}) collective-permute-start(s32[8]{0:T(128)S(1)} %reshape.41.l0.listed_ref), channel_id=1, source_target_pairs={{0,192},{64,0},{128,64},{192,128},{1,193},{65,1},{129,65},{193,129... | collective-permute-start | bytes 104 | tf_op jit(solution)/shard_map/ppermute | solution.py:301
  17.3 2.1 %copy_bitcast_fusion = (bf16[512,1024]{1,0:T(8,128)(2,1)S(1)}, bf16[512,1024]{1,0:T(8,128)(2,1)S(1)}) fusion(bf16[64,8,8,128]{3,2,1,0:T(8,128)(2,1)} %bitcast.16, bf16[64,8,8,128]{3,2,1,0:T(8,128)(2,1)} %bitcast.17), kind=kLoop, calls=%fused_computation | loop fusion | bytes 4194304 | tf_op jit(solution)/shard_map/reshape | solution.py:334
  19.4 0.0 copy-start.7
  19.4 0.0 copy-start.2
  19.4 0.0 collective-permute-done.2.l3
  19.4 0.0 collective-permute-done.1.l2
  19.4 0.0 collective-permute-done.l1
  19.4 5.6 %all-to-all-done = bf16[8,2,16,576]{3,2,1,0:T(8,128)(2,1)S(1)} async-done(((bf16[8,2,16,576]{3,2,1,0:T(8,128)(2,1)}), bf16[8,2,16,576]{3,2,1,0:T(8,128)(2,1)S(1)}, u32[]{:S(2)}, u32[]{:S(2)}) %all-to-all-start) | async-done | bytes 294944 | tf_op jit(solution)/shard_map/all_to_all | solution.py:297
  25.1 0.7 shard_map.120
  25.8 12.4 %all_to_all.25.all_ref = bf16[4,8,16,576]{3,2,1,0:T(8,128)(2,1)S(1)} all-to-all(bf16[4,8,16,576]{3,2,1,0:T(8,128)(2,1)S(1)} %shard_map.120), channel_id=1, replica_groups=mesh['x'=4,'z'=8,'y'=4,'c'=2] {'x'}, dimensions={0} | all-to-all | bytes 1179648 | tf_op jit(solution)/shard_map/all_to_all | solution.py:297
  38.2 0.6 shard_map.121
  38.8 13.1 %all_to_all.26.near_ref = bf16[4,8,16,576]{3,2,1,0:T(8,128)(2,1)S(1)} all-to-all(bf16[4,8,16,576]{3,2,1,0:T(8,128)(2,1)S(1)} %shard_map.121), channel_id=1, replica_groups=mesh['x'=4,'z'=8,'y'=4,'c'=2] {'y'}, dimensions={0} | all-to-all | bytes 1179648 | tf_op jit(solution)/shard_map/all_to_all | solution.py:297
  51.8 0.0 collective-permute-start.3
  51.8 0.1 reshape.48.vis_ref
  51.9 2.1 %collective-permute-done.3.far_ref = bf16[4,8,16,576]{3,2,1,0:T(8,128)(2,1)} collective-permute-done((bf16[4,8,16,576]{3,2,1,0:T(8,128)(2,1)S(1)}, bf16[4,8,16,576]{3,2,1,0:T(8,128)(2,1)}, u32[]{:S(2)}, u32[]{:S(2)}) %collective-permute-start.3) | collective-permute-done | bytes 589856 | tf_op jit(solution)/shard_map/ppermute | solution.py:305
  54.1 1.1 copy-done.3
  55.2 1.0 copy-done.5
  56.2 15.9 %shard_map.122 = (bf16[2,1024,640]{2,1,0:T(8,128)(2,1)}, bf16[2,1024,640]{2,1,0:T(8,128)(2,1)}, bf16[2,640,512]{2,1,0:T(8,128)(2,1)}, bf16[2,640,64]{2,1,0:T(8,1...) custom-call(s32[1]{0:T(128)} %bitcast.2.core_ref, s32[8]{0:T(128)S(1)} %reshape.48.vis_ref, ...), custom_call_target="tpu_custom_call" | custom-call | flops 6200000000 | bytes 8000000 | tf_op jit(solution)/shard_map/pallas_call | solution.py:353
  72.1 0.2 collective-permute-start.4
  72.3 2.2 %collective-permute-done.4.recv_ref = bf16[4,10,16,576]{3,2,1,0:T(8,128)(2,1)S(1)} collective-permute-done((bf16[4,10,16,576]{3,2,1,0:T(8,128)(2,1)S(1)}, bf16[4,10,16,576]{3,2,1,0:T(8,128)(2,1)S(1)}, u32[]{:S(2)}, u32[]{:S(2)}) %collective-permute-start.4) | collective-permute-done | bytes 737312 | tf_op jit(solution)/shard_map/ppermute | solution.py:305
  74.6 1.4 copy-done
  76.0 0.2 shard_map.123
  76.1 0.6 collective-permute-start.5
  76.8 2.1 %collective-permute-start.6 = (bf16[10,16,576]{2,1,0:T(8,128)(2,1)S(1)}, bf16[10,16,576]{2,1,0:T(8,128)(2,1)S(1)}, u32[]{:S(2)}, u32[]{:S(2)}) collective-permute-start(bf16[10,16,576]{2,1,0:T(8,128)(2,1)S(1)} %get-tuple-element.53), channel_id=1, source_target_pairs={{0,4},{2,6},{4,0},{6,2},{1,5},{3,7},{5,1},{7,3},{8,12},{10,14},{12... | collective-permute-start | bytes 552968 | tf_op jit(solution)/shard_map/ppermute | solution.py:301
  78.9 0.9 collective-permute-start.7
  79.7 9.8 %shard_map.124 = (bf16[256,1024]{1,0:T(8,128)(2,1)}, bf16[256,1536]{1,0:T(8,128)(2,1)}, bf16[128,2048]{1,0:T(8,128)(2,1)S(1)}, bf16[128,2048]{1,0:T(8,128)(2,1)}...) custom-call(s32[1]{0:T(128)} %bitcast.x_ref, bf16[256,1536]{1,0:T(8,128)(2,1)S(1)} %copy-done.4, ...), custom_call_target="tpu_custom_call" | custom-call | flops 4000000000 | bytes 8000000 | tf_op jit(solution)/shard_map/pallas_call | solution.py:375
  89.6 0.0 collective-permute-done.5.r1_ref
  89.6 0.0 collective-permute-done.7.r3_ref
  89.6 0.1 shard_map.125
  89.7 0.3 collective-permute-start.10
  90.0 3.3 %collective-permute-start.9 = (bf16[8,16,576]{2,1,0:T(8,128)(2,1)S(1)}, bf16[8,16,576]{2,1,0:T(8,128)(2,1)S(1)}, u32[]{:S(2)}, u32[]{:S(2)}) collective-permute-start(bf16[8,16,576]{2,1,0:T(8,128)(2,1)S(1)} %get-tuple-element.60.i0), channel_id=1, source_target_pairs={{0,128},{64,192},{128,0},{192,64},{1,129},{65,193},{129,1},{193,65... | collective-permute-start | bytes 442376 | tf_op jit(solution)/shard_map/ppermute | solution.py:301
  93.3 0.6 collective-permute-start.8
  93.9 1.5 collective-permute-start.11
  95.3 1.4 collective-permute-start.12
  96.8 0.1 collective-permute-done.10.i3
  96.9 6.0 %collective-permute-start.13 = (bf16[128,2048]{1,0:T(8,128)(2,1)}, bf16[128,2048]{1,0:T(8,128)(2,1)S(1)}, u32[]{:S(2)}, u32[]{:S(2)}) collective-permute-start(bf16[128,2048]{1,0:T(8,128)(2,1)} %get-tuple-element.63), channel_id=1, source_target_pairs={{0,192},{64,0},{128,64},{192,128},{1,193},{65,1},{129,65},{193,129... | collective-permute-start | bytes 1572872 | tf_op jit(solution)/shard_map/ppermute | solution.py:301
  102.9 8.9 %collective-permute-done.8.i1 = bf16[8,16,576]{2,1,0:T(8,128)(2,1)S(1)} collective-permute-done((bf16[8,16,576]{2,1,0:T(8,128)(2,1)S(1)}, bf16[8,16,576]{2,1,0:T(8,128)(2,1)S(1)}, u32[]{:S(2)}, u32[]{:S(2)}) %collective-permute-start.8) | collective-permute-done | bytes 147488 | tf_op jit(solution)/shard_map/ppermute | solution.py:301
  111.7 1.8 %shard_map.126 = bf16[8,2,16,576]{3,2,1,0:T(8,128)(2,1)} custom-call(s32[1]{0:T(128)} %bitcast.x_ref, s32[1]{0:T(128)} %bitcast.5.z_ref, s32[8]{0:T(128)S(1)} %reshape.41.l0.listed_ref, s32[8]{0:T(128)S(1)} %collective-permute-done.l1, s32[8]{0:T(128)S(1)} %collective-permute-done.1.l2, s32[8]{0:T(128)S(1)} %collective-permute-done.2.l3, ...), custom_call_target="tpu_custom_call" | custom-call | tf_op jit(solution)/shard_map/pallas_call | solution.py:393
  113.6 3.4 %all-to-all-start.3 = ((bf16[8,2,16,576]{3,2,1,0:T(8,128)(2,1)}), bf16[8,2,16,576]{3,2,1,0:T(8,128)(2,1)S(1)}, u32[]{:S(2)}, u32[]{:S(2)}) async-start(bf16[8,2,16,576]{3,2,1,0:T(8,128)(2,1)} %shard_map.126), calls=%async_computation.3 | async-start | bytes 655360 | tf_op jit(solution)/shard_map/all_to_all | solution.py:297
  117.0 0.0 collective-permute-done.11.w1
  117.0 6.0 %collective-permute-done.13.w3 = bf16[128,2048]{1,0:T(8,128)(2,1)S(1)} collective-permute-done((bf16[128,2048]{1,0:T(8,128)(2,1)}, bf16[128,2048]{1,0:T(8,128)(2,1)S(1)}, u32[]{:S(2)}, u32[]{:S(2)}) %collective-permute-start.13) | collective-permute-done | bytes 524320 | tf_op jit(solution)/shard_map/ppermute | solution.py:301
  123.1 5.1 %all-to-all-done.3.in_ref = bf16[8,2,16,576]{3,2,1,0:T(8,128)(2,1)S(1)} async-done(((bf16[8,2,16,576]{3,2,1,0:T(8,128)(2,1)}), bf16[8,2,16,576]{3,2,1,0:T(8,128)(2,1)S(1)}, u32[]{:S(2)}, u32[]{:S(2)}) %all-to-all-start.3) | async-done | bytes 294944 | tf_op jit(solution)/shard_map/all_to_all | solution.py:297
  128.1 1.0 shard_map.130
  129.2 3.5 %all-to-all-start.4 = ((bf16[8,16,2048]{2,1,0:T(8,128)(2,1)}), bf16[8,16,2048]{2,1,0:T(8,128)(2,1)S(1)}, u32[]{:S(2)}, u32[]{:S(2)}) async-start(bf16[8,16,2048]{2,1,0:T(8,128)(2,1)} %shard_map.130), calls=%async_computation.4 | async-start | bytes 1048576 | tf_op jit(solution)/shard_map/all_to_all | solution.py:297
  132.7 0.1 collective-permute-start.14
  132.8 1.2 collective-permute-done.14.far_ref
  134.0 2.5 %collective-permute-start.17 = (bf16[2,2,16,576]{3,2,1,0:T(8,128)(2,1)S(1)}, bf16[2,2,16,576]{3,2,1,0:T(8,128)(2,1)S(1)}, u32[]{:S(2)}, u32[]{:S(2)}) collective-permute-start(bf16[2,2,16,576]{3,2,1,0:T(8,128)(2,1)S(1)} %shard_map.128.i0), channel_id=1, source_target_pairs={{0,6},{2,0},{4,2},{6,4},{1,7},{3,1},{5,3},{7,5},{8,14},{10,8},{12,... | collective-permute-start | bytes 221192 | tf_op jit(solution)/shard_map/ppermute | solution.py:301
  136.5 0.8 collective-permute-start.16
  137.3 0.9 collective-permute-start.15
  138.2 2.2 %collective-permute-done.17.i3 = bf16[2,2,16,576]{3,2,1,0:T(8,128)(2,1)S(1)} collective-permute-done((bf16[2,2,16,576]{3,2,1,0:T(8,128)(2,1)S(1)}, bf16[2,2,16,576]{3,2,1,0:T(8,128)(2,1)S(1)}, u32[]{:S(2)}, u32[]{:S(2)}) %collective-permute-start.17) | collective-permute-done | bytes 73760 | tf_op jit(solution)/shard_map/ppermute | solution.py:301
  140.3 2.8 %collective-permute-done.16.i2 = bf16[2,2,16,576]{3,2,1,0:T(8,128)(2,1)S(1)} collective-permute-done((bf16[2,2,16,576]{3,2,1,0:T(8,128)(2,1)S(1)}, bf16[2,2,16,576]{3,2,1,0:T(8,128)(2,1)S(1)}, u32[]{:S(2)}, u32[]{:S(2)}) %collective-permute-start.16) | collective-permute-done | bytes 73760 | tf_op jit(solution)/shard_map/ppermute | solution.py:301
  143.1 0.9 collective-permute-done.15.i1
  144.0 0.3 shard_map.129
  144.3 1.0 copy.16
  145.3 0.6 all-to-all-done.4.in_ref
  145.9 0.8 shard_map.131
  (14 shorter events, 0.1 us)
Async XLA Ops:
  1.8 0.7 copy-start.1
  3.3 21.7 %all-to-all-start = ((bf16[8,2,16,576]{3,2,1,0:T(8,128)(2,1)}), bf16[8,2,16,576]{3,2,1,0:T(8,128)(2,1)S(1)}, u32[]{:S(2)}, u32[]{:S(2)}) async-start(bf16[8,2,16,576]{3,2,1,0:T(8,128)(2,1)} %shard_map.119), calls=%async_computation | async-start | bytes 655360 | tf_op jit(solution)/shard_map/all_to_all | solution.py:297
  12.6 6.8 %collective-permute-start.2 = (s32[8]{0:T(128)S(1)}, s32[8]{0:T(128)S(1)}, u32[]{:S(2)}, u32[]{:S(2)}) collective-permute-start(s32[8]{0:T(128)S(1)} %reshape.41.l0.listed_ref), channel_id=1, source_target_pairs={{0,64},{64,128},{128,192},{192,0},{1,65},{65,129},{129,193},{193,1... | collective-permute-start | bytes 104 | tf_op jit(solution)/shard_map/ppermute | solution.py:301
  14.0 5.4 %collective-permute-start.1 = (s32[8]{0:T(128)S(1)}, s32[8]{0:T(128)S(1)}, u32[]{:S(2)}, u32[]{:S(2)}) collective-permute-start(s32[8]{0:T(128)S(1)} %reshape.41.l0.listed_ref), channel_id=1, source_target_pairs={{0,128},{64,192},{128,0},{192,64},{1,129},{65,193},{129,1},{193,65... | collective-permute-start | bytes 104 | tf_op jit(solution)/shard_map/ppermute | solution.py:301
  15.2 4.3 %collective-permute-start = (s32[8]{0:T(128)S(1)}, s32[8]{0:T(128)S(1)}, u32[]{:S(2)}, u32[]{:S(2)}) collective-permute-start(s32[8]{0:T(128)S(1)} %reshape.41.l0.listed_ref), channel_id=1, source_target_pairs={{0,192},{64,0},{128,64},{192,128},{1,193},{65,1},{129,65},{193,129... | collective-permute-start | bytes 104 | tf_op jit(solution)/shard_map/ppermute | solution.py:301
  19.4 32.5 %copy-start.7 = (s32[2,4]{1,0:T(2,128)S(1)}, s32[2,4]{1,0:T(2,128)}, u32[]{:S(2)}) copy-start(s32[2,4]{1,0:T(2,128)} %param.15) | copy-start | bytes 100
  19.4 34.7 %copy-start.2 = (f32[512]{0:T(512)S(1)}, f32[512]{0:T(512)}, u32[]{:S(2)}) copy-start(f32[512]{0:T(512)} %param.10) | copy-start | bytes 6148
  51.8 2.2 %collective-permute-start.3 = (bf16[4,8,16,576]{3,2,1,0:T(8,128)(2,1)S(1)}, bf16[4,8,16,576]{3,2,1,0:T(8,128)(2,1)}, u32[]{:S(2)}, u32[]{:S(2)}) collective-permute-start(bf16[4,8,16,576]{3,2,1,0:T(8,128)(2,1)S(1)} %all_to_all.26.near_ref), channel_id=1, source_target_pairs={{0,1},{1,0},{2,3},{3,2},{4,5},{5,4},{6,7},{7,6},{8,9},{9,8},{10,11... | collective-permute-start | bytes 1769480 | tf_op jit(solution)/shard_map/ppermute | solution.py:305
  54.1 1.1 copy-start.3
  55.2 1.0 copy-start.5
  56.2 23.5 %copy-start.4 = (bf16[256,1536]{1,0:T(8,128)(2,1)S(1)}, bf16[256,1536]{1,0:T(8,128)(2,1)}, u32[]{:S(2)}) copy-start(bf16[256,1536]{1,0:T(8,128)(2,1)} %query_ref.3) | copy-start | bytes 2359300
  56.2 23.5 %copy-start.6 = (bf16[256,1024]{1,0:T(8,128)(2,1)S(1)}, bf16[256,1024]{1,0:T(8,128)(2,1)}, u32[]{:S(2)}) copy-start(bf16[256,1024]{1,0:T(8,128)(2,1)} %grad_ref.3) | copy-start | bytes 1572868
  72.1 2.4 %collective-permute-start.4 = (bf16[4,10,16,576]{3,2,1,0:T(8,128)(2,1)S(1)}, bf16[4,10,16,576]{3,2,1,0:T(8,128)(2,1)S(1)}, u32[]{:S(2)}, u32[]{:S(2)}) collective-permute-start(bf16[4,10,16,576]{3,2,1,0:T(8,128)(2,1)S(1)} %get-tuple-element.42), channel_id=1, source_target_pairs={{0,1},{1,0},{2,3},{3,2},{4,5},{5,4},{6,7},{7,6},{8,9},{9,8},{10,11... | collective-permute-start | bytes 2211848 | tf_op jit(solution)/shard_map/ppermute | solution.py:305
  74.6 1.4 copy-start
  76.1 13.4 %collective-permute-start.5 = (bf16[10,16,576]{2,1,0:T(8,128)(2,1)S(1)}, bf16[10,16,576]{2,1,0:T(8,128)(2,1)S(1)}, u32[]{:S(2)}, u32[]{:S(2)}) collective-permute-start(bf16[10,16,576]{2,1,0:T(8,128)(2,1)S(1)} %get-tuple-element.52), channel_id=1, source_target_pairs={{0,2},{2,4},{4,6},{6,0},{1,3},{3,5},{5,7},{7,1},{8,10},{10,12},{12... | collective-permute-start | bytes 552968 | tf_op jit(solution)/shard_map/ppermute | solution.py:301
  76.8 12.8 %collective-permute-start.6 = (bf16[10,16,576]{2,1,0:T(8,128)(2,1)S(1)}, bf16[10,16,576]{2,1,0:T(8,128)(2,1)S(1)}, u32[]{:S(2)}, u32[]{:S(2)}) collective-permute-start(bf16[10,16,576]{2,1,0:T(8,128)(2,1)S(1)} %get-tuple-element.53), channel_id=1, source_target_pairs={{0,4},{2,6},{4,0},{6,2},{1,5},{3,7},{5,1},{7,3},{8,12},{10,14},{12... | collective-permute-start | bytes 552968 | tf_op jit(solution)/shard_map/ppermute | solution.py:301
  78.9 10.7 %collective-permute-start.7 = (bf16[10,16,576]{2,1,0:T(8,128)(2,1)S(1)}, bf16[10,16,576]{2,1,0:T(8,128)(2,1)S(1)}, u32[]{:S(2)}, u32[]{:S(2)}) collective-permute-start(bf16[10,16,576]{2,1,0:T(8,128)(2,1)S(1)} %get-tuple-element.54), channel_id=1, source_target_pairs={{0,6},{2,0},{4,2},{6,4},{1,7},{3,1},{5,3},{7,5},{8,14},{10,8},{12,... | collective-permute-start | bytes 552968 | tf_op jit(solution)/shard_map/ppermute | solution.py:301
  89.7 7.2 %collective-permute-start.10 = (bf16[8,16,576]{2,1,0:T(8,128)(2,1)S(1)}, bf16[8,16,576]{2,1,0:T(8,128)(2,1)S(1)}, u32[]{:S(2)}, u32[]{:S(2)}) collective-permute-start(bf16[8,16,576]{2,1,0:T(8,128)(2,1)S(1)} %get-tuple-element.60.i0), channel_id=1, source_target_pairs={{0,64},{64,128},{128,192},{192,0},{1,65},{65,129},{129,193},{193,1... | collective-permute-start | bytes 442376 | tf_op jit(solution)/shard_map/ppermute | solution.py:301
  90.0 12.9 %collective-permute-start.9 = (bf16[8,16,576]{2,1,0:T(8,128)(2,1)S(1)}, bf16[8,16,576]{2,1,0:T(8,128)(2,1)S(1)}, u32[]{:S(2)}, u32[]{:S(2)}) collective-permute-start(bf16[8,16,576]{2,1,0:T(8,128)(2,1)S(1)} %get-tuple-element.60.i0), channel_id=1, source_target_pairs={{0,128},{64,192},{128,0},{192,64},{1,129},{65,193},{129,1},{193,65... | collective-permute-start | bytes 442376 | tf_op jit(solution)/shard_map/ppermute | solution.py:301
  93.3 18.4 %collective-permute-start.8 = (bf16[8,16,576]{2,1,0:T(8,128)(2,1)S(1)}, bf16[8,16,576]{2,1,0:T(8,128)(2,1)S(1)}, u32[]{:S(2)}, u32[]{:S(2)}) collective-permute-start(bf16[8,16,576]{2,1,0:T(8,128)(2,1)S(1)} %get-tuple-element.60.i0), channel_id=1, source_target_pairs={{0,192},{64,0},{128,64},{192,128},{1,193},{65,1},{129,65},{193,129... | collective-permute-start | bytes 442376 | tf_op jit(solution)/shard_map/ppermute | solution.py:301
  93.9 23.1 %collective-permute-start.11 = (bf16[128,2048]{1,0:T(8,128)(2,1)}, bf16[128,2048]{1,0:T(8,128)(2,1)S(1)}, u32[]{:S(2)}, u32[]{:S(2)}) collective-permute-start(bf16[128,2048]{1,0:T(8,128)(2,1)} %get-tuple-element.61), channel_id=1, source_target_pairs={{0,64},{64,128},{128,192},{192,0},{1,65},{65,129},{129,193},{193,1... | collective-permute-start | bytes 1572872 | tf_op jit(solution)/shard_map/ppermute | solution.py:301
  95.3 21.7 %collective-permute-start.12 = (bf16[128,2048]{1,0:T(8,128)(2,1)}, bf16[128,2048]{1,0:T(8,128)(2,1)S(1)}, u32[]{:S(2)}, u32[]{:S(2)}) collective-permute-start(bf16[128,2048]{1,0:T(8,128)(2,1)} %get-tuple-element.62), channel_id=1, source_target_pairs={{0,128},{64,192},{128,0},{192,64},{1,129},{65,193},{129,1},{193,65... | collective-permute-start | bytes 1572872 | tf_op jit(solution)/shard_map/ppermute | solution.py:301
  96.9 26.1 %collective-permute-start.13 = (bf16[128,2048]{1,0:T(8,128)(2,1)}, bf16[128,2048]{1,0:T(8,128)(2,1)S(1)}, u32[]{:S(2)}, u32[]{:S(2)}) collective-permute-start(bf16[128,2048]{1,0:T(8,128)(2,1)} %get-tuple-element.63), channel_id=1, source_target_pairs={{0,192},{64,0},{128,64},{192,128},{1,193},{65,1},{129,65},{193,129... | collective-permute-start | bytes 1572872 | tf_op jit(solution)/shard_map/ppermute | solution.py:301
  113.6 14.5 %all-to-all-start.3 = ((bf16[8,2,16,576]{3,2,1,0:T(8,128)(2,1)}), bf16[8,2,16,576]{3,2,1,0:T(8,128)(2,1)S(1)}, u32[]{:S(2)}, u32[]{:S(2)}) async-start(bf16[8,2,16,576]{3,2,1,0:T(8,128)(2,1)} %shard_map.126), calls=%async_computation.3 | async-start | bytes 655360 | tf_op jit(solution)/shard_map/all_to_all | solution.py:297
  129.2 16.7 %all-to-all-start.4 = ((bf16[8,16,2048]{2,1,0:T(8,128)(2,1)}), bf16[8,16,2048]{2,1,0:T(8,128)(2,1)S(1)}, u32[]{:S(2)}, u32[]{:S(2)}) async-start(bf16[8,16,2048]{2,1,0:T(8,128)(2,1)} %shard_map.130), calls=%async_computation.4 | async-start | bytes 1048576 | tf_op jit(solution)/shard_map/all_to_all | solution.py:297
  132.7 1.3 collective-permute-start.14
  134.0 6.3 %collective-permute-start.17 = (bf16[2,2,16,576]{3,2,1,0:T(8,128)(2,1)S(1)}, bf16[2,2,16,576]{3,2,1,0:T(8,128)(2,1)S(1)}, u32[]{:S(2)}, u32[]{:S(2)}) collective-permute-start(bf16[2,2,16,576]{3,2,1,0:T(8,128)(2,1)S(1)} %shard_map.128.i0), channel_id=1, source_target_pairs={{0,6},{2,0},{4,2},{6,4},{1,7},{3,1},{5,3},{7,5},{8,14},{10,8},{12,... | collective-permute-start | bytes 221192 | tf_op jit(solution)/shard_map/ppermute | solution.py:301
  136.5 6.6 %collective-permute-start.16 = (bf16[2,2,16,576]{3,2,1,0:T(8,128)(2,1)S(1)}, bf16[2,2,16,576]{3,2,1,0:T(8,128)(2,1)S(1)}, u32[]{:S(2)}, u32[]{:S(2)}) collective-permute-start(bf16[2,2,16,576]{3,2,1,0:T(8,128)(2,1)S(1)} %shard_map.128.i0), channel_id=1, source_target_pairs={{0,4},{2,6},{4,0},{6,2},{1,5},{3,7},{5,1},{7,3},{8,12},{10,14},{12... | collective-permute-start | bytes 221192 | tf_op jit(solution)/shard_map/ppermute | solution.py:301
  137.3 6.7 %collective-permute-start.15 = (bf16[2,2,16,576]{3,2,1,0:T(8,128)(2,1)S(1)}, bf16[2,2,16,576]{3,2,1,0:T(8,128)(2,1)S(1)}, u32[]{:S(2)}, u32[]{:S(2)}) collective-permute-start(bf16[2,2,16,576]{3,2,1,0:T(8,128)(2,1)S(1)} %shard_map.128.i0), channel_id=1, source_target_pairs={{0,2},{2,4},{4,6},{6,0},{1,3},{3,5},{5,7},{7,1},{8,10},{10,12},{12... | collective-permute-start | bytes 221192 | tf_op jit(solution)/shard_map/ppermute | solution.py:301

commit v3 on v2

--- a/solution.py
+++ b/solution.py
@@ -69,24 +69,27 @@
             out_ref[z, b, :, LATENT:] = rope
 
 
-def spread_kernel(x_ref, l0, l1, l2, l3, column_ref, out_ref):
-    for r, listed in enumerate((l0, l1, l2, l3)):
-        to = (x_ref[0] + r) % NX
+def spread_kernel(l0, l1, l2, l3, column_ref, o0, o1, o2, o3):
+    for listed, out in ((l0, o0), (l1, o1), (l2, o2), (l3, o3)):
         for s in range(BLOCKS_DEV * SLOTS):
-            out_ref[to, s] = column_ref[listed[s] % COLUMN]
-
-
-def select_kernel(listed_ref, all_ref, out_ref):
+            out[s] = column_ref[listed[s] % COLUMN]
+
+
+def select_kernel(x_ref, listed_ref, i0, i1, i2, i3, out_ref):
     for s in range(BLOCKS_DEV * SLOTS):
-        tile = all_ref[listed_ref[s] // COLUMN, s]
-        for y in range(NY):
-            out_ref[y, s] = tile
+        back = (x_ref[0] - listed_ref[s] // COLUMN + NX) % NX
+        for r, in_ref in enumerate((i0, i1, i2, i3)):
+
+            @pl.when(back == r)
+            def _():
+                out_ref[s] = in_ref[s]
 
 
 def attend_kernel(
-    core_ref, vis_ref, query_ref, grad_ref, key_up_ref, value_up_ref, latent_ref, gain_ref, near_ref, far_ref,
+    core_ref, y_ref, vis_ref, query_ref, grad_ref, key_up_ref, value_up_ref, latent_ref, gain_ref,
+    n0, n1, n2, n3, f0, f1, f2, f3,
     sgrad_ref, weights_ref, klat, krope, keep_ref, send_ref,
-    bias, glat, grope,
+    bias, glat, grope, own,
 ):
     step = pl.program_id(0)
     core = core_ref[0]
@@ -95,28 +98,26 @@
     @pl.when(step == 0)
     def _():
         raw = latent_ref[:, :LATENT].astype(f32)
-        own = (raw * norm_inverse(raw) * gain_ref[...]).astype(bf16)
-        own = own.reshape(BLOCKS_DEV, NY, NC, ROWS, LATENT)
-        rope = latent_ref[:, LATENT:].reshape(BLOCKS_DEV, NY, NC, ROWS, ROPE)
-        for b in range(BLOCKS_DEV):
-            for side in range(NC):
-                for y in range(NY):
-                    at = side * HALF + y * ROWS
-                    first = core == side
-                    klat[b, at : at + ROWS, :] = jnp.where(first, own[b, y, 0], own[b, y, 1])
-                    krope[b, at : at + ROWS, :] = jnp.where(first, rope[b, y, 0], rope[b, y, 1])
+        own[...] = (raw * norm_inverse(raw) * gain_ref[...]).astype(bf16)
+        for side, pieces in enumerate(((n0, n1, n2, n3), (f0, f1, f2, f3))):
+            for r, piece in enumerate(pieces):
+                at = side * HALF + r * ROWS
+                owner = (y_ref[0] - r + NY) % NY * NC + (core + side) % NC
+                for b in range(BLOCKS_DEV):
+                    rows = pl.ds(pl.multiple_of(b * BLOCK + owner * ROWS, ROWS), ROWS)
+                    klat[b, at : at + ROWS, :] = own[rows, :]
+                    krope[b, at : at + ROWS, :] = latent_ref[rows, LATENT:]
                     for j in range(SLOTS):
-                        src = (near_ref, far_ref)[side]
                         to = (1 + j) * BLOCK + at
-                        klat[b, to : to + ROWS, :] = src[y, b * SLOTS + j, :, :LATENT]
-                        krope[b, to : to + ROWS, :] = src[y, b * SLOTS + j, :, LATENT:]
+                        klat[b, to : to + ROWS, :] = piece[b * SLOTS + j, :, :LATENT]
+                        krope[b, to : to + ROWS, :] = piece[b * SLOTS + j, :, LATENT:]
         col = lax.broadcasted_iota(jnp.int32, (BLOCK, BLOCK), 1)
         row = lax.broadcasted_iota(jnp.int32, (BLOCK, BLOCK), 0)
         side = jnp.where(col >= HALF, 1, 0)
         rest = col - side * HALF
-        piece = rest // ROWS
+        piece = (y_ref[0] - rest // ROWS + NY) % NY
         owner = jnp.where(core == 0, side, 1 - side)
-        offset = (piece * NC + owner) * ROWS + (rest - piece * ROWS)
+        offset = (piece * NC + owner) * ROWS + rest % ROWS
         for b in range(BLOCKS_DEV):
             bias[b, :, :BLOCK] = jnp.where(offset <= row, 0.0, -jnp.inf)
             for j in range(SLOTS):
@@ -205,9 +206,9 @@
         out[...] = wgrad[pl.ds(start, PART), :]
 
 
-def pair_kernel(y_ref, keep_ref, recv_ref, own_ref, s1_ref, s2_ref, s3_ref):
+def pair_kernel(keep_ref, recv_ref, own_ref, s1_ref, s2_ref, s3_ref):
     for r, out in enumerate((own_ref, s1_ref, s2_ref, s3_ref)):
-        y = (y_ref[0] + r) % NY
+        y = (NY - r) % NY
         out[...] = (keep_ref[y] + recv_ref[y].astype(f32)).astype(out.dtype)
 
 
@@ -278,13 +279,13 @@
             out_ref[rows, LATENT:] = total[:, LATENT:]
 
 
-def call(kernel, out_shape, in_specs, **kw):
+def call(kernel, out_shape, in_specs, limit=VMEM_LIMIT, **kw):
     return pl.pallas_call(
         kernel,
         out_shape=out_shape,
         in_specs=in_specs,
         out_specs=kw.pop("out_specs", vmem()),
-        compiler_params=pltpu.CompilerParams(vmem_limit_bytes=VMEM_LIMIT),
+        compiler_params=pltpu.CompilerParams(vmem_limit_bytes=limit),
         **kw,
     )
 
@@ -299,6 +300,10 @@
 
 def shift(values, axis, count, by):
     return lax.ppermute(values, axis, [(i, (i + by) % count) for i in range(count)])
+
+
+def in_hbm(values):
+    return pltpu.with_memory_space_constraint(values, pltpu.HBM)
 
 
 def swap_cores(values):
@@ -333,12 +338,13 @@
     key_up_flat = key_up.reshape(LATENT, HEADS_DEV * HEAD_DIM)
     value_up_flat = value_up.reshape(LATENT, HEADS_DEV * HEAD_DIM)
     column = exchange(mine, "z").reshape(COLUMN, ROWS, KV)
-    column = call(spread_kernel, shape(NX, slots, ROWS, KV), [smem()] * 5 + [vmem()])(x, *lists, column)
     column, key_up_flat, value_up_flat = lax.optimization_barrier((column, key_up_flat, value_up_flat))
-    column = exchange(column, "x")
-    picked = call(select_kernel, shape(NY, slots, ROWS, KV), [smem(), vmem()])(listed, column)
-    near = exchange(picked, "y")
-    far = swap_cores(near)
+    tile_list = shape(slots, ROWS, KV)
+    sent = call(spread_kernel, (tile_list,) * NX, [smem()] * NX + [vmem()], out_specs=(vmem(),) * NX)(*lists, column)
+    got = [sent[0]] + [shift(sent[r], "x", NX, r) for r in range(1, NX)]
+    picked = call(select_kernel, tile_list, [smem()] * 2 + [vmem()] * NX)(x, listed, *got)
+    near = [picked] + [shift(picked, "y", NY, r) for r in range(1, NY)]
+    far = [swap_cores(piece) for piece in near]
 
     tokens = query.shape[0]
     steps = HEADS_DEV // HEADS_STEP
@@ -347,29 +353,33 @@
     rows = HEADS_DEV * BLOCK
     lat_keys, rope_keys = (BLOCKS_DEV, KEYS, LATENT), (BLOCKS_DEV, KEYS, ROPE)
     tiles = (NY, TILES, ROWS, KV)
+    query, out_grad = in_hbm(query), in_hbm(out_grad)
     operands = (query, out_grad, key_up_flat, value_up_flat)
     operand_specs = [columns(tokens, HEADS_STEP * QDIM), columns(tokens, width), columns(LATENT, width), columns(LATENT, width)]
     by_rows = pl.BlockSpec((BLOCKS_DEV, HEADS_STEP * BLOCK, KEYS), lambda g: (0, g, 0))
     score_grad, weights, klat, krope, keep, send = call(
         attend_kernel,
-        (shape(BLOCKS_DEV, rows, KEYS),) * 2 + (shape(*lat_keys), shape(*rope_keys), shape(*tiles, dtype=f32), shape(*tiles)),
-        [smem()] * 2 + operand_specs + [whole(tokens, KV), whole(1, LATENT)] + [whole(NY, slots, ROWS, KV)] * 2,
+        (pltpu.HBM((BLOCKS_DEV, rows, KEYS), bf16),) * 2
+        + (pltpu.HBM(lat_keys, bf16), pltpu.HBM(rope_keys, bf16), pltpu.VMEM(tiles, f32), pltpu.HBM(tiles, bf16)),
+        [smem()] * 3 + operand_specs + [whole(tokens, KV), whole(1, LATENT)] + [whole(slots, ROWS, KV)] * (2 * NY),
         out_specs=(by_rows, by_rows, whole(*lat_keys), whole(*rope_keys), whole(*tiles), whole(*tiles)),
         grid=(steps,),
         scratch_shapes=[
             pltpu.VMEM((BLOCKS_DEV, BLOCK, KEYS), f32),
             pltpu.VMEM(lat_keys, f32),
             pltpu.VMEM(rope_keys, f32),
+            pltpu.VMEM((tokens, LATENT), bf16),
         ],
         cost_estimate=cost(6_200_000_000),
-    )(core, limits, *operands, latent, gain, near, far)
+        limit=44 * 1024 * 1024,
+    )(core, y, limits, *operands, latent, gain, *near, *far)
 
     own, s1, s2, s3 = call(
         pair_kernel,
         (shape(TILES, ROWS, KV, dtype=f32),) + (shape(TILES, ROWS, KV),) * 3,
-        [smem(), vmem(), vmem()],
+        [vmem(), vmem()],
         out_specs=(vmem(),) * 4,
-    )(y, keep, swap_cores(send))
+    )(keep, swap_cores(send))
     others = [shift(s, "y", NY, r) for r, s in ((1, s1), (2, s2), (3, s3))]
     own, score_grad = lax.optimization_barrier((own, score_grad))
     attn_out, query_grad, *wgrads = call(
@@ -380,7 +390,7 @@
         grid=(steps,),
         scratch_shapes=[pltpu.VMEM((LATENT, 2 * width), bf16)],
         cost_estimate=cost(4_000_000_000),
-    )(x, *operands, score_grad, weights, klat, krope)
+    )(x, *operands, in_hbm(score_grad), in_hbm(weights), in_hbm(klat), in_hbm(krope))
     parts = [shift(w, "x", NX, r) for r, w in enumerate(wgrads) if r > 0]
     *others, wgrads[0] = lax.optimization_barrier((*others, wgrads[0]))
     own, spread = call(
@@ -397,7 +407,6 @@
         scratch_shapes=[pltpu.VMEM((COLUMN, ROWS, KV), f32)],
     )(x, z, *lists, own, spread, *others)
     line = exchange(line, "z")
-    line, *parts = lax.optimization_barrier((line, *parts))
     part = call(part_kernel, shape(NZ, ROWS, wcols), [vmem()] * NX)(wgrads[0], *parts)
     part = exchange(part, "z")
     total = call(line_kernel, shape(BLOCKS_DEV, ROWS, KV), [vmem()])(line)

time: 148 us -> 140 us (0.946)
  blocking collectives: 25.5 us -> 0 us
  waiting for transfers between devices: 37.7 us -> 53.7 us
  starting transfers between devices: 41.2 us -> 46.2 us
  local copies, waits for them, and re-layouts: 9.39 us -> 5.8 us
    all_to_all x2 -> x0, blocking collectives: 25.5 us -> none  [exchange(): return lax.all_to_all(values, axis, split_axis=0, concat_axis=0, tiled=True)]
    ppermute x15 -> x21, waiting for transfers between devices: 20.9 us -> 38.2 us  [shift(): lax.ppermute(values, axis, [(i, (i + by) % count) for i in range(count)])]
    ppermute x15 -> x21, starting transfers between devices: 25.5 us -> 30.5 us  [shift(): lax.ppermute(values, axis, [(i, (i + by) % count) for i in range(count)])]
    unnamed x18 -> x8, local copies, waits for them, and re-layouts: 6.5 us -> 2.88 us
    ppermute x3 -> x6, waiting for transfers between devices: 5.55 us -> 5.03 us  [swap_cores(): return lax.ppermute(values, 'c', [(0, 1), (1, 0)])]
  transfers between devices with their start and end apart: 21 -> 30, of which waited for: 12 -> 20; matrix products, arithmetic and copies ran while one was open for 3% -> 3% of each run, Pallas kernels for 8% -> 9%
where the time goes in v3:
time: 140 us; the launch traced here: 139 us
  waiting for transfers between devices  53.7 us (38%)
  starting transfers between devices  46.2 us (33%)
  Pallas kernels  32.8 us (23%)
  local copies, waits for them, and re-layouts  5.8 us (4%)
    ppermute x21, waiting for transfers between devices, shift(): lax.ppermute(values, axis, [(i, (i + by) % count) for i in range(count)])  38.2 us
    ppermute x21, starting transfers between devices, shift(): lax.ppermute(values, axis, [(i, (i + by) % count) for i in range(count)])  30.5 us
    pallas_call x1, Pallas kernels, shards(): call(attend_kernel, (pltpu.HBM((BLOCKS_DEV, rows, KEYS), bf16),) * 2 + (p...  15.6 us
    all_to_all x3, starting transfers between devices, exchange(): return lax.all_to_all(values, axis, split_axis=0, concat_axis=0, tiled=True)  15.4 us
    all_to_all x3, waiting for transfers between devices, exchange(): return lax.all_to_all(values, axis, split_axis=0, concat_axis=0, tiled=True)  10.4 us
    pallas_call x1, Pallas kernels, shards(): call(project_kernel, (shape(tokens, HEADS_DEV * HEAD_DIM), shape(tokens,...  10 us
    ppermute x6, waiting for transfers between devices, swap_cores(): return lax.ppermute(values, 'c', [(0, 1), (1, 0)])  5.03 us
    unnamed x8, local copies, waits for them, and re-layouts  2.88 us
  transfers between devices with their start and end apart: 30, of which 20 were waited for; matrix products, arithmetic and copies ran while one was open for 3% of the time, Pallas kernels for 9%

profile of v3, /device:TPU:2, one launch (start us, length us, event | category | flops | bytes accessed | tf_op | source)
XLA Modules:
  0.0 139.3 jit_solution(1573981076842657812)
XLA Ops:
  0.6 1.2 copy.13.latent_ref
  1.8 0.0 copy-start
  1.8 0.7 copy-done
  2.5 0.8 shard_map.119
  3.3 8.5 %all-to-all-start = ((bf16[8,2,16,576]{3,2,1,0:T(8,128)(2,1)}), bf16[8,2,16,576]{3,2,1,0:T(8,128)(2,1)S(1)}, u32[]{:S(2)}, u32[]{:S(2)}) async-start(bf16[8,2,16,576]{3,2,1,0:T(8,128)(2,1)} %shard_map.119), calls=%async_computation | async-start | bytes 655360 | tf_op jit(solution)/shard_map/all_to_all | solution.py:298
  11.8 0.8 reshape.48.l0.listed_ref
  12.6 1.5 %collective-permute-start.2 = (s32[8]{0:T(128)S(1)}, s32[8]{0:T(128)S(1)}, u32[]{:S(2)}, u32[]{:S(2)}) collective-permute-start(s32[8]{0:T(128)S(1)} %reshape.48.l0.listed_ref), channel_id=1, source_target_pairs={{0,64},{64,128},{128,192},{192,0},{1,65},{65,129},{129,193},{193,1... | collective-permute-start | bytes 104 | tf_op jit(solution)/shard_map/ppermute | solution.py:302
  14.0 1.1 collective-permute-start.1
  15.2 2.2 %collective-permute-start = (s32[8]{0:T(128)S(1)}, s32[8]{0:T(128)S(1)}, u32[]{:S(2)}, u32[]{:S(2)}) collective-permute-start(s32[8]{0:T(128)S(1)} %reshape.48.l0.listed_ref), channel_id=1, source_target_pairs={{0,192},{64,0},{128,64},{192,128},{1,193},{65,1},{129,65},{193,129... | collective-permute-start | bytes 104 | tf_op jit(solution)/shard_map/ppermute | solution.py:302
  17.3 2.1 %copy_bitcast_fusion = (bf16[512,1024]{1,0:T(8,128)(2,1)S(1)}, bf16[512,1024]{1,0:T(8,128)(2,1)S(1)}) fusion(bf16[64,8,8,128]{3,2,1,0:T(8,128)(2,1)} %bitcast.16, bf16[64,8,8,128]{3,2,1,0:T(8,128)(2,1)} %bitcast.17), kind=kLoop, calls=%fused_computation | loop fusion | bytes 4194304 | tf_op jit(solution)/shard_map/reshape | solution.py:339
  19.4 5.7 %all-to-all-done = bf16[8,2,16,576]{3,2,1,0:T(8,128)(2,1)S(1)} async-done(((bf16[8,2,16,576]{3,2,1,0:T(8,128)(2,1)}), bf16[8,2,16,576]{3,2,1,0:T(8,128)(2,1)S(1)}, u32[]{:S(2)}, u32[]{:S(2)}) %all-to-all-start) | async-done | bytes 294944 | tf_op jit(solution)/shard_map/all_to_all | solution.py:298
  25.1 1.4 shard_map.120
  26.5 1.5 %collective-permute-start.3 = (bf16[8,16,576]{2,1,0:T(8,128)(2,1)}, bf16[8,16,576]{2,1,0:T(8,128)(2,1)S(1)}, u32[]{:S(2)}, u32[]{:S(2)}) collective-permute-start(bf16[8,16,576]{2,1,0:T(8,128)(2,1)} %get-tuple-element.42), channel_id=1, source_target_pairs={{0,64},{64,128},{128,192},{192,0},{1,65},{65,129},{129,193},{193,1... | collective-permute-start | bytes 442376 | tf_op jit(solution)/shard_map/ppermute | solution.py:302
  28.0 1.1 collective-permute-start.4
  29.1 2.2 %collective-permute-start.5 = (bf16[8,16,576]{2,1,0:T(8,128)(2,1)S(1)}, bf16[8,16,576]{2,1,0:T(8,128)(2,1)S(1)}, u32[]{:S(2)}, u32[]{:S(2)}) collective-permute-start(bf16[8,16,576]{2,1,0:T(8,128)(2,1)S(1)} %get-tuple-element.44), channel_id=1, source_target_pairs={{0,192},{64,0},{128,64},{192,128},{1,193},{65,1},{129,65},{193,129... | collective-permute-start | bytes 442376 | tf_op jit(solution)/shard_map/ppermute | solution.py:302
  31.2 2.2 %collective-permute-done.3.i1 = bf16[8,16,576]{2,1,0:T(8,128)(2,1)S(1)} collective-permute-done((bf16[8,16,576]{2,1,0:T(8,128)(2,1)}, bf16[8,16,576]{2,1,0:T(8,128)(2,1)S(1)}, u32[]{:S(2)}, u32[]{:S(2)}) %collective-permute-start.3) | collective-permute-done | bytes 147488 | tf_op jit(solution)/shard_map/ppermute | solution.py:302
  33.4 2.2 %collective-permute-done.4.i2 = bf16[8,16,576]{2,1,0:T(8,128)(2,1)S(1)} collective-permute-done((bf16[8,16,576]{2,1,0:T(8,128)(2,1)}, bf16[8,16,576]{2,1,0:T(8,128)(2,1)S(1)}, u32[]{:S(2)}, u32[]{:S(2)}) %collective-permute-start.4) | collective-permute-done | bytes 147488 | tf_op jit(solution)/shard_map/ppermute | solution.py:302
  35.6 0.7 collective-permute-done.5.i3
  36.3 0.8 shard_map.121.n0
  37.1 3.1 %collective-permute-start.8 = (bf16[8,16,576]{2,1,0:T(8,128)(2,1)S(1)}, bf16[8,16,576]{2,1,0:T(8,128)(2,1)S(1)}, u32[]{:S(2)}, u32[]{:S(2)}) collective-permute-start(bf16[8,16,576]{2,1,0:T(8,128)(2,1)S(1)} %shard_map.121.n0), channel_id=1, source_target_pairs={{0,6},{2,0},{4,2},{6,4},{1,7},{3,1},{5,3},{7,5},{8,14},{10,8},{12,... | collective-permute-start | bytes 442376 | tf_op jit(solution)/shard_map/ppermute | solution.py:302
  40.2 0.6 collective-permute-start.7
  40.8 1.0 collective-permute-start.6
  41.8 3.0 %collective-permute-done.8.n3 = bf16[8,16,576]{2,1,0:T(8,128)(2,1)S(1)} collective-permute-done((bf16[8,16,576]{2,1,0:T(8,128)(2,1)S(1)}, bf16[8,16,576]{2,1,0:T(8,128)(2,1)S(1)}, u32[]{:S(2)}, u32[]{:S(2)}) %collective-permute-start.8) | collective-permute-done | bytes 147488 | tf_op jit(solution)/shard_map/ppermute | solution.py:302
  44.8 2.3 %collective-permute-done.7.n2 = bf16[8,16,576]{2,1,0:T(8,128)(2,1)S(1)} collective-permute-done((bf16[8,16,576]{2,1,0:T(8,128)(2,1)S(1)}, bf16[8,16,576]{2,1,0:T(8,128)(2,1)S(1)}, u32[]{:S(2)}, u32[]{:S(2)}) %collective-permute-start.7) | collective-permute-done | bytes 147488 | tf_op jit(solution)/shard_map/ppermute | solution.py:302
  47.1 1.6 %collective-permute-done.6.n1 = bf16[8,16,576]{2,1,0:T(8,128)(2,1)S(1)} collective-permute-done((bf16[8,16,576]{2,1,0:T(8,128)(2,1)S(1)}, bf16[8,16,576]{2,1,0:T(8,128)(2,1)S(1)}, u32[]{:S(2)}, u32[]{:S(2)}) %collective-permute-start.6) | collective-permute-done | bytes 147488 | tf_op jit(solution)/shard_map/ppermute | solution.py:302
  48.8 0.1 reshape.47.vis_ref
  48.9 1.4 %collective-permute-done.10.f1 = bf16[8,16,576]{2,1,0:T(8,128)(2,1)} collective-permute-done((bf16[8,16,576]{2,1,0:T(8,128)(2,1)S(1)}, bf16[8,16,576]{2,1,0:T(8,128)(2,1)}, u32[]{:S(2)}, u32[]{:S(2)}) %collective-permute-start.10) | collective-permute-done | bytes 147488 | tf_op jit(solution)/shard_map/ppermute | solution.py:310
  50.3 15.6 %shard_map.122 = (bf16[2,1024,640]{2,1,0:T(8,128)(2,1)}, bf16[2,1024,640]{2,1,0:T(8,128)(2,1)}, bf16[2,640,512]{2,1,0:T(8,128)(2,1)}, bf16[2,640,64]{2,1,0:T(8,1...) custom-call(s32[1]{0:T(128)} %bitcast.2.core_ref, s32[1]{0:T(128)} %bitcast.1.y_ref, ...), custom_call_target="tpu_custom_call" | custom-call | flops 6200000000 | bytes 8000000 | tf_op jit(solution)/shard_map/pallas_call | solution.py:360
  65.9 0.2 collective-permute-start.13
  66.2 2.4 %collective-permute-done.13.recv_ref = bf16[4,10,16,576]{3,2,1,0:T(8,128)(2,1)S(1)} collective-permute-done((bf16[4,10,16,576]{3,2,1,0:T(8,128)(2,1)}, bf16[4,10,16,576]{3,2,1,0:T(8,128)(2,1)S(1)}, u32[]{:S(2)}, u32[]{:S(2)}) %collective-permute-start.13) | collective-permute-done | bytes 737312 | tf_op jit(solution)/shard_map/ppermute | solution.py:310
  68.6 0.1 shard_map.123
  68.7 0.1 collective-permute-start.14
  68.8 2.0 %collective-permute-start.15 = (bf16[10,16,576]{2,1,0:T(8,128)(2,1)S(1)}, bf16[10,16,576]{2,1,0:T(8,128)(2,1)S(1)}, u32[]{:S(2)}, u32[]{:S(2)}) collective-permute-start(bf16[10,16,576]{2,1,0:T(8,128)(2,1)S(1)} %get-tuple-element.57), channel_id=1, source_target_pairs={{0,4},{2,6},{4,0},{6,2},{1,5},{3,7},{5,1},{7,3},{8,12},{10,14},{12... | collective-permute-start | bytes 552968 | tf_op jit(solution)/shard_map/ppermute | solution.py:302
  70.8 1.2 collective-permute-start.16
  72.1 10.0 %shard_map.124 = (bf16[256,1024]{1,0:T(8,128)(2,1)}, bf16[256,1536]{1,0:T(8,128)(2,1)}, bf16[128,2048]{1,0:T(8,128)(2,1)S(1)}, bf16[128,2048]{1,0:T(8,128)(2,1)}...) custom-call(s32[1]{0:T(128)} %bitcast.x_ref, bf16[256,1536]{1,0:T(8,128)(2,1)} %query_ref.3, ...), custom_call_target="tpu_custom_call" | custom-call | flops 4000000000 | bytes 8000000 | tf_op jit(solution)/shard_map/pallas_call | solution.py:385
  82.1 0.1 collective-permute-done.16.r3_ref
  82.2 0.1 shard_map.125
  82.3 1.8 %collective-permute-start.19 = (bf16[8,16,576]{2,1,0:T(8,128)(2,1)S(1)}, bf16[8,16,576]{2,1,0:T(8,128)(2,1)S(1)}, u32[]{:S(2)}, u32[]{:S(2)}) collective-permute-start(bf16[8,16,576]{2,1,0:T(8,128)(2,1)S(1)} %get-tuple-element.64.i0), channel_id=1, source_target_pairs={{0,64},{64,128},{128,192},{192,0},{1,65},{65,129},{129,193},{193,1... | collective-permute-start | bytes 442376 | tf_op jit(solution)/shard_map/ppermute | solution.py:302
  84.1 1.4 %collective-permute-start.18 = (bf16[8,16,576]{2,1,0:T(8,128)(2,1)S(1)}, bf16[8,16,576]{2,1,0:T(8,128)(2,1)S(1)}, u32[]{:S(2)}, u32[]{:S(2)}) collective-permute-start(bf16[8,16,576]{2,1,0:T(8,128)(2,1)S(1)} %get-tuple-element.64.i0), channel_id=1, source_target_pairs={{0,128},{64,192},{128,0},{192,64},{1,129},{65,193},{129,1},{193,65... | collective-permute-start | bytes 442376 | tf_op jit(solution)/shard_map/ppermute | solution.py:302
  85.5 1.7 %collective-permute-start.17 = (bf16[8,16,576]{2,1,0:T(8,128)(2,1)S(1)}, bf16[8,16,576]{2,1,0:T(8,128)(2,1)S(1)}, u32[]{:S(2)}, u32[]{:S(2)}) collective-permute-start(bf16[8,16,576]{2,1,0:T(8,128)(2,1)S(1)} %get-tuple-element.64.i0), channel_id=1, source_target_pairs={{0,192},{64,0},{128,64},{192,128},{1,193},{65,1},{129,65},{193,129... | collective-permute-start | bytes 442376 | tf_op jit(solution)/shard_map/ppermute | solution.py:302
  87.2 0.4 collective-permute-start.24
  87.5 3.3 %collective-permute-start.25 = (bf16[128,2048]{1,0:T(8,128)(2,1)}, bf16[128,2048]{1,0:T(8,128)(2,1)S(1)}, u32[]{:S(2)}, u32[]{:S(2)}) collective-permute-start(bf16[128,2048]{1,0:T(8,128)(2,1)} %get-tuple-element.67), channel_id=1, source_target_pairs={{0,128},{64,192},{128,0},{192,64},{1,129},{65,193},{129,1},{193,65... | collective-permute-start | bytes 1572872 | tf_op jit(solution)/shard_map/ppermute | solution.py:302
  90.9 0.1 collective-permute-done.19.i3
  90.9 0.4 collective-permute-start.26
  91.3 1.4 %collective-permute-done.18.i2 = bf16[8,16,576]{2,1,0:T(8,128)(2,1)S(1)} collective-permute-done((bf16[8,16,576]{2,1,0:T(8,128)(2,1)S(1)}, bf16[8,16,576]{2,1,0:T(8,128)(2,1)S(1)}, u32[]{:S(2)}, u32[]{:S(2)}) %collective-permute-start.18) | collective-permute-done | bytes 147488 | tf_op jit(solution)/shard_map/ppermute | solution.py:302
  92.7 11.5 %collective-permute-done.17.i1 = bf16[8,16,576]{2,1,0:T(8,128)(2,1)S(1)} collective-permute-done((bf16[8,16,576]{2,1,0:T(8,128)(2,1)S(1)}, bf16[8,16,576]{2,1,0:T(8,128)(2,1)S(1)}, u32[]{:S(2)}, u32[]{:S(2)}) %collective-permute-start.17) | collective-permute-done | bytes 147488 | tf_op jit(solution)/shard_map/ppermute | solution.py:302
  104.2 1.9 %shard_map.126 = bf16[8,2,16,576]{3,2,1,0:T(8,128)(2,1)} custom-call(s32[1]{0:T(128)} %bitcast.x_ref, s32[1]{0:T(128)} %bitcast.5.z_ref, s32[8]{0:T(128)S(1)} %reshape.48.l0.listed_ref, s32[8]{0:T(128)S(1)} %collective-permute-done.l1, s32[8]{0:T(128)S(1)} %collective-permute-done.1.l2, s32[8]{0:T(128)S(1)} %collective-permute-done.2.l3, ...), custom_call_target="tpu_custom_call" | custom-call | tf_op jit(solution)/shard_map/pallas_call | solution.py:403
  106.0 3.4 %all-to-all-start.1 = ((bf16[8,2,16,576]{3,2,1,0:T(8,128)(2,1)}), bf16[8,2,16,576]{3,2,1,0:T(8,128)(2,1)S(1)}, u32[]{:S(2)}, u32[]{:S(2)}) async-start(bf16[8,2,16,576]{3,2,1,0:T(8,128)(2,1)} %shard_map.126), calls=%async_computation.1 | async-start | bytes 655360 | tf_op jit(solution)/shard_map/all_to_all | solution.py:298
  109.5 7.1 %collective-permute-done.26.w3 = bf16[128,2048]{1,0:T(8,128)(2,1)S(1)} collective-permute-done((bf16[128,2048]{1,0:T(8,128)(2,1)}, bf16[128,2048]{1,0:T(8,128)(2,1)S(1)}, u32[]{:S(2)}, u32[]{:S(2)}) %collective-permute-start.26) | collective-permute-done | bytes 524320 | tf_op jit(solution)/shard_map/ppermute | solution.py:302
  116.6 1.0 shard_map.130
  117.6 3.0 %all-to-all-done.1.in_ref = bf16[8,2,16,576]{3,2,1,0:T(8,128)(2,1)S(1)} async-done(((bf16[8,2,16,576]{3,2,1,0:T(8,128)(2,1)}), bf16[8,2,16,576]{3,2,1,0:T(8,128)(2,1)S(1)}, u32[]{:S(2)}, u32[]{:S(2)}) %all-to-all-start.1) | async-done | bytes 294944 | tf_op jit(solution)/shard_map/all_to_all | solution.py:298
  120.6 3.5 %all-to-all-start.2 = ((bf16[8,16,2048]{2,1,0:T(8,128)(2,1)}), bf16[8,16,2048]{2,1,0:T(8,128)(2,1)S(1)}, u32[]{:S(2)}, u32[]{:S(2)}) async-start(bf16[8,16,2048]{2,1,0:T(8,128)(2,1)} %shard_map.130), calls=%async_computation.2 | async-start | bytes 1048576 | tf_op jit(solution)/shard_map/all_to_all | solution.py:298
  124.1 0.1 collective-permute-start.20
  124.2 1.2 collective-permute-done.20.far_ref
  125.4 2.8 %collective-permute-start.23 = (bf16[2,2,16,576]{3,2,1,0:T(8,128)(2,1)S(1)}, bf16[2,2,16,576]{3,2,1,0:T(8,128)(2,1)S(1)}, u32[]{:S(2)}, u32[]{:S(2)}) collective-permute-start(bf16[2,2,16,576]{3,2,1,0:T(8,128)(2,1)S(1)} %shard_map.128.i0), channel_id=1, source_target_pairs={{0,6},{2,0},{4,2},{6,4},{1,7},{3,1},{5,3},{7,5},{8,14},{10,8},{12,... | collective-permute-start | bytes 221192 | tf_op jit(solution)/shard_map/ppermute | solution.py:302
  128.3 0.3 collective-permute-start.22
  128.5 0.9 collective-permute-start.21
  129.4 2.6 %collective-permute-done.23.i3 = bf16[2,2,16,576]{3,2,1,0:T(8,128)(2,1)S(1)} collective-permute-done((bf16[2,2,16,576]{3,2,1,0:T(8,128)(2,1)S(1)}, bf16[2,2,16,576]{3,2,1,0:T(8,128)(2,1)S(1)}, u32[]{:S(2)}, u32[]{:S(2)}) %collective-permute-start.23) | collective-permute-done | bytes 73760 | tf_op jit(solution)/shard_map/ppermute | solution.py:302
  132.1 2.8 %collective-permute-done.22.i2 = bf16[2,2,16,576]{3,2,1,0:T(8,128)(2,1)S(1)} collective-permute-done((bf16[2,2,16,576]{3,2,1,0:T(8,128)(2,1)S(1)}, bf16[2,2,16,576]{3,2,1,0:T(8,128)(2,1)S(1)}, u32[]{:S(2)}, u32[]{:S(2)}) %collective-permute-start.22) | collective-permute-done | bytes 73760 | tf_op jit(solution)/shard_map/ppermute | solution.py:302
  134.9 0.6 collective-permute-done.21.i1
  135.5 0.3 shard_map.129
  135.7 1.0 copy.16
  136.7 1.8 %all-to-all-done.2.in_ref = bf16[8,16,2048]{2,1,0:T(8,128)(2,1)S(1)} async-done(((bf16[8,16,2048]{2,1,0:T(8,128)(2,1)}), bf16[8,16,2048]{2,1,0:T(8,128)(2,1)S(1)}, u32[]{:S(2)}, u32[]{:S(2)}) %all-to-all-start.2) | async-done | bytes 524320 | tf_op jit(solution)/shard_map/all_to_all | solution.py:298
  138.6 0.8 shard_map.131
  (20 shorter events, 0.1 us)
Async XLA Ops:
  1.8 0.7 copy-start
  3.3 21.7 %all-to-all-start = ((bf16[8,2,16,576]{3,2,1,0:T(8,128)(2,1)}), bf16[8,2,16,576]{3,2,1,0:T(8,128)(2,1)S(1)}, u32[]{:S(2)}, u32[]{:S(2)}) async-start(bf16[8,2,16,576]{3,2,1,0:T(8,128)(2,1)} %shard_map.119), calls=%async_computation | async-start | bytes 655360 | tf_op jit(solution)/shard_map/all_to_all | solution.py:298
  12.6 12.5 %collective-permute-start.2 = (s32[8]{0:T(128)S(1)}, s32[8]{0:T(128)S(1)}, u32[]{:S(2)}, u32[]{:S(2)}) collective-permute-start(s32[8]{0:T(128)S(1)} %reshape.48.l0.listed_ref), channel_id=1, source_target_pairs={{0,64},{64,128},{128,192},{192,0},{1,65},{65,129},{129,193},{193,1... | collective-permute-start | bytes 104 | tf_op jit(solution)/shard_map/ppermute | solution.py:302
  14.0 11.0 %collective-permute-start.1 = (s32[8]{0:T(128)S(1)}, s32[8]{0:T(128)S(1)}, u32[]{:S(2)}, u32[]{:S(2)}) collective-permute-start(s32[8]{0:T(128)S(1)} %reshape.48.l0.listed_ref), channel_id=1, source_target_pairs={{0,128},{64,192},{128,0},{192,64},{1,129},{65,193},{129,1},{193,65... | collective-permute-start | bytes 104 | tf_op jit(solution)/shard_map/ppermute | solution.py:302
  15.2 9.9 %collective-permute-start = (s32[8]{0:T(128)S(1)}, s32[8]{0:T(128)S(1)}, u32[]{:S(2)}, u32[]{:S(2)}) collective-permute-start(s32[8]{0:T(128)S(1)} %reshape.48.l0.listed_ref), channel_id=1, source_target_pairs={{0,192},{64,0},{128,64},{192,128},{1,193},{65,1},{129,65},{193,129... | collective-permute-start | bytes 104 | tf_op jit(solution)/shard_map/ppermute | solution.py:302
  17.3 31.5 %copy-start.2 = (s32[2,4]{1,0:T(2,128)S(1)}, s32[2,4]{1,0:T(2,128)}, u32[]{:S(2)}) copy-start(s32[2,4]{1,0:T(2,128)} %param.15) | copy-start | bytes 100
  17.3 33.0 %copy-start.1 = (f32[512]{0:T(512)S(1)}, f32[512]{0:T(512)}, u32[]{:S(2)}) copy-start(f32[512]{0:T(512)} %param.10) | copy-start | bytes 6148
  26.5 7.0 %collective-permute-start.3 = (bf16[8,16,576]{2,1,0:T(8,128)(2,1)}, bf16[8,16,576]{2,1,0:T(8,128)(2,1)S(1)}, u32[]{:S(2)}, u32[]{:S(2)}) collective-permute-start(bf16[8,16,576]{2,1,0:T(8,128)(2,1)} %get-tuple-element.42), channel_id=1, source_target_pairs={{0,64},{64,128},{128,192},{192,0},{1,65},{65,129},{129,193},{193,1... | collective-permute-start | bytes 442376 | tf_op jit(solution)/shard_map/ppermute | solution.py:302
  28.0 7.6 %collective-permute-start.4 = (bf16[8,16,576]{2,1,0:T(8,128)(2,1)}, bf16[8,16,576]{2,1,0:T(8,128)(2,1)S(1)}, u32[]{:S(2)}, u32[]{:S(2)}) collective-permute-start(bf16[8,16,576]{2,1,0:T(8,128)(2,1)} %get-tuple-element.43), channel_id=1, source_target_pairs={{0,128},{64,192},{128,0},{192,64},{1,129},{65,193},{129,1},{193,65... | collective-permute-start | bytes 442376 | tf_op jit(solution)/shard_map/ppermute | solution.py:302
  29.1 7.2 %collective-permute-start.5 = (bf16[8,16,576]{2,1,0:T(8,128)(2,1)S(1)}, bf16[8,16,576]{2,1,0:T(8,128)(2,1)S(1)}, u32[]{:S(2)}, u32[]{:S(2)}) collective-permute-start(bf16[8,16,576]{2,1,0:T(8,128)(2,1)S(1)} %get-tuple-element.44), channel_id=1, source_target_pairs={{0,192},{64,0},{128,64},{192,128},{1,193},{65,1},{129,65},{193,129... | collective-permute-start | bytes 442376 | tf_op jit(solution)/shard_map/ppermute | solution.py:302
  37.1 7.7 %collective-permute-start.8 = (bf16[8,16,576]{2,1,0:T(8,128)(2,1)S(1)}, bf16[8,16,576]{2,1,0:T(8,128)(2,1)S(1)}, u32[]{:S(2)}, u32[]{:S(2)}) collective-permute-start(bf16[8,16,576]{2,1,0:T(8,128)(2,1)S(1)} %shard_map.121.n0), channel_id=1, source_target_pairs={{0,6},{2,0},{4,2},{6,4},{1,7},{3,1},{5,3},{7,5},{8,14},{10,8},{12,... | collective-permute-start | bytes 442376 | tf_op jit(solution)/shard_map/ppermute | solution.py:302
  40.2 6.9 %collective-permute-start.7 = (bf16[8,16,576]{2,1,0:T(8,128)(2,1)S(1)}, bf16[8,16,576]{2,1,0:T(8,128)(2,1)S(1)}, u32[]{:S(2)}, u32[]{:S(2)}) collective-permute-start(bf16[8,16,576]{2,1,0:T(8,128)(2,1)S(1)} %shard_map.121.n0), channel_id=1, source_target_pairs={{0,4},{2,6},{4,0},{6,2},{1,5},{3,7},{5,1},{7,3},{8,12},{10,14},{12... | collective-permute-start | bytes 442376 | tf_op jit(solution)/shard_map/ppermute | solution.py:302
  40.8 7.9 %collective-permute-start.6 = (bf16[8,16,576]{2,1,0:T(8,128)(2,1)S(1)}, bf16[8,16,576]{2,1,0:T(8,128)(2,1)S(1)}, u32[]{:S(2)}, u32[]{:S(2)}) collective-permute-start(bf16[8,16,576]{2,1,0:T(8,128)(2,1)S(1)} %shard_map.121.n0), channel_id=1, source_target_pairs={{0,2},{2,4},{4,6},{6,0},{1,3},{3,5},{5,7},{7,1},{8,10},{10,12},{12... | collective-permute-start | bytes 442376 | tf_op jit(solution)/shard_map/ppermute | solution.py:302
  41.8 7.1 %collective-permute-start.9 = (bf16[8,16,576]{2,1,0:T(8,128)(2,1)S(1)}, bf16[8,16,576]{2,1,0:T(8,128)(2,1)S(1)}, u32[]{:S(2)}, u32[]{:S(2)}) collective-permute-start(bf16[8,16,576]{2,1,0:T(8,128)(2,1)S(1)} %shard_map.121.n0), channel_id=1, source_target_pairs={{0,1},{1,0},{2,3},{3,2},{4,5},{5,4},{6,7},{7,6},{8,9},{9,8},{10,11... | collective-permute-start | bytes 442376 | tf_op jit(solution)/shard_map/ppermute | solution.py:310
  44.8 4.0 %collective-permute-start.12 = (bf16[8,16,576]{2,1,0:T(8,128)(2,1)S(1)}, bf16[8,16,576]{2,1,0:T(8,128)(2,1)S(1)}, u32[]{:S(2)}, u32[]{:S(2)}) collective-permute-start(bf16[8,16,576]{2,1,0:T(8,128)(2,1)S(1)} %collective-permute-done.8.n3), channel_id=1, source_target_pairs={{0,1},{1,0},{2,3},{3,2},{4,5},{5,4},{6,7},{7,6},{8,9},{9,8},{10,11... | collective-permute-start | bytes 442376 | tf_op jit(solution)/shard_map/ppermute | solution.py:310
  47.1 1.7 %collective-permute-start.11 = (bf16[8,16,576]{2,1,0:T(8,128)(2,1)S(1)}, bf16[8,16,576]{2,1,0:T(8,128)(2,1)}, u32[]{:S(2)}, u32[]{:S(2)}) collective-permute-start(bf16[8,16,576]{2,1,0:T(8,128)(2,1)S(1)} %collective-permute-done.7.n2), channel_id=1, source_target_pairs={{0,1},{1,0},{2,3},{3,2},{4,5},{5,4},{6,7},{7,6},{8,9},{9,8},{10,11... | collective-permute-start | bytes 442376 | tf_op jit(solution)/shard_map/ppermute | solution.py:310
  48.8 1.5 %collective-permute-start.10 = (bf16[8,16,576]{2,1,0:T(8,128)(2,1)S(1)}, bf16[8,16,576]{2,1,0:T(8,128)(2,1)}, u32[]{:S(2)}, u32[]{:S(2)}) collective-permute-start(bf16[8,16,576]{2,1,0:T(8,128)(2,1)S(1)} %collective-permute-done.6.n1), channel_id=1, source_target_pairs={{0,1},{1,0},{2,3},{3,2},{4,5},{5,4},{6,7},{7,6},{8,9},{9,8},{10,11... | collective-permute-start | bytes 442376 | tf_op jit(solution)/shard_map/ppermute | solution.py:310
  65.9 2.6 %collective-permute-start.13 = (bf16[4,10,16,576]{3,2,1,0:T(8,128)(2,1)}, bf16[4,10,16,576]{3,2,1,0:T(8,128)(2,1)S(1)}, u32[]{:S(2)}, u32[]{:S(2)}) collective-permute-start(bf16[4,10,16,576]{3,2,1,0:T(8,128)(2,1)} %get-tuple-element.46), channel_id=1, source_target_pairs={{0,1},{1,0},{2,3},{3,2},{4,5},{5,4},{6,7},{7,6},{8,9},{9,8},{10,11... | collective-permute-start | bytes 2211848 | tf_op jit(solution)/shard_map/ppermute | solution.py:310
  68.7 13.4 %collective-permute-start.14 = (bf16[10,16,576]{2,1,0:T(8,128)(2,1)S(1)}, bf16[10,16,576]{2,1,0:T(8,128)(2,1)S(1)}, u32[]{:S(2)}, u32[]{:S(2)}) collective-permute-start(bf16[10,16,576]{2,1,0:T(8,128)(2,1)S(1)} %get-tuple-element.56), channel_id=1, source_target_pairs={{0,2},{2,4},{4,6},{6,0},{1,3},{3,5},{5,7},{7,1},{8,10},{10,12},{12... | collective-permute-start | bytes 552968 | tf_op jit(solution)/shard_map/ppermute | solution.py:302
  68.8 13.3 %collective-permute-start.15 = (bf16[10,16,576]{2,1,0:T(8,128)(2,1)S(1)}, bf16[10,16,576]{2,1,0:T(8,128)(2,1)S(1)}, u32[]{:S(2)}, u32[]{:S(2)}) collective-permute-start(bf16[10,16,576]{2,1,0:T(8,128)(2,1)S(1)} %get-tuple-element.57), channel_id=1, source_target_pairs={{0,4},{2,6},{4,0},{6,2},{1,5},{3,7},{5,1},{7,3},{8,12},{10,14},{12... | collective-permute-start | bytes 552968 | tf_op jit(solution)/shard_map/ppermute | solution.py:302
  70.8 11.3 %collective-permute-start.16 = (bf16[10,16,576]{2,1,0:T(8,128)(2,1)S(1)}, bf16[10,16,576]{2,1,0:T(8,128)(2,1)S(1)}, u32[]{:S(2)}, u32[]{:S(2)}) collective-permute-start(bf16[10,16,576]{2,1,0:T(8,128)(2,1)S(1)} %get-tuple-element.58), channel_id=1, source_target_pairs={{0,6},{2,0},{4,2},{6,4},{1,7},{3,1},{5,3},{7,5},{8,14},{10,8},{12,... | collective-permute-start | bytes 552968 | tf_op jit(solution)/shard_map/ppermute | solution.py:302
  82.3 8.7 %collective-permute-start.19 = (bf16[8,16,576]{2,1,0:T(8,128)(2,1)S(1)}, bf16[8,16,576]{2,1,0:T(8,128)(2,1)S(1)}, u32[]{:S(2)}, u32[]{:S(2)}) collective-permute-start(bf16[8,16,576]{2,1,0:T(8,128)(2,1)S(1)} %get-tuple-element.64.i0), channel_id=1, source_target_pairs={{0,64},{64,128},{128,192},{192,0},{1,65},{65,129},{129,193},{193,1... | collective-permute-start | bytes 442376 | tf_op jit(solution)/shard_map/ppermute | solution.py:302
  84.1 8.6 %collective-permute-start.18 = (bf16[8,16,576]{2,1,0:T(8,128)(2,1)S(1)}, bf16[8,16,576]{2,1,0:T(8,128)(2,1)S(1)}, u32[]{:S(2)}, u32[]{:S(2)}) collective-permute-start(bf16[8,16,576]{2,1,0:T(8,128)(2,1)S(1)} %get-tuple-element.64.i0), channel_id=1, source_target_pairs={{0,128},{64,192},{128,0},{192,64},{1,129},{65,193},{129,1},{193,65... | collective-permute-start | bytes 442376 | tf_op jit(solution)/shard_map/ppermute | solution.py:302
  85.5 18.7 %collective-permute-start.17 = (bf16[8,16,576]{2,1,0:T(8,128)(2,1)S(1)}, bf16[8,16,576]{2,1,0:T(8,128)(2,1)S(1)}, u32[]{:S(2)}, u32[]{:S(2)}) collective-permute-start(bf16[8,16,576]{2,1,0:T(8,128)(2,1)S(1)} %get-tuple-element.64.i0), channel_id=1, source_target_pairs={{0,192},{64,0},{128,64},{192,128},{1,193},{65,1},{129,65},{193,129... | collective-permute-start | bytes 442376 | tf_op jit(solution)/shard_map/ppermute | solution.py:302
  87.2 22.3 %collective-permute-start.24 = (bf16[128,2048]{1,0:T(8,128)(2,1)}, bf16[128,2048]{1,0:T(8,128)(2,1)S(1)}, u32[]{:S(2)}, u32[]{:S(2)}) collective-permute-start(bf16[128,2048]{1,0:T(8,128)(2,1)} %get-tuple-element.66), channel_id=1, source_target_pairs={{0,64},{64,128},{128,192},{192,0},{1,65},{65,129},{129,193},{193,1... | collective-permute-start | bytes 1572872 | tf_op jit(solution)/shard_map/ppermute | solution.py:302
  87.5 21.9 %collective-permute-start.25 = (bf16[128,2048]{1,0:T(8,128)(2,1)}, bf16[128,2048]{1,0:T(8,128)(2,1)S(1)}, u32[]{:S(2)}, u32[]{:S(2)}) collective-permute-start(bf16[128,2048]{1,0:T(8,128)(2,1)} %get-tuple-element.67), channel_id=1, source_target_pairs={{0,128},{64,192},{128,0},{192,64},{1,129},{65,193},{129,1},{193,65... | collective-permute-start | bytes 1572872 | tf_op jit(solution)/shard_map/ppermute | solution.py:302
  90.9 25.6 %collective-permute-start.26 = (bf16[128,2048]{1,0:T(8,128)(2,1)}, bf16[128,2048]{1,0:T(8,128)(2,1)S(1)}, u32[]{:S(2)}, u32[]{:S(2)}) collective-permute-start(bf16[128,2048]{1,0:T(8,128)(2,1)} %get-tuple-element.68), channel_id=1, source_target_pairs={{0,192},{64,0},{128,64},{192,128},{1,193},{65,1},{129,65},{193,129... | collective-permute-start | bytes 1572872 | tf_op jit(solution)/shard_map/ppermute | solution.py:302
  106.0 14.5 %all-to-all-start.1 = ((bf16[8,2,16,576]{3,2,1,0:T(8,128)(2,1)}), bf16[8,2,16,576]{3,2,1,0:T(8,128)(2,1)S(1)}, u32[]{:S(2)}, u32[]{:S(2)}) async-start(bf16[8,2,16,576]{3,2,1,0:T(8,128)(2,1)} %shard_map.126), calls=%async_computation.1 | async-start | bytes 655360 | tf_op jit(solution)/shard_map/all_to_all | solution.py:298
  120.6 18.0 %all-to-all-start.2 = ((bf16[8,16,2048]{2,1,0:T(8,128)(2,1)}), bf16[8,16,2048]{2,1,0:T(8,128)(2,1)S(1)}, u32[]{:S(2)}, u32[]{:S(2)}) async-start(bf16[8,16,2048]{2,1,0:T(8,128)(2,1)} %shard_map.130), calls=%async_computation.2 | async-start | bytes 1048576 | tf_op jit(solution)/shard_map/all_to_all | solution.py:298
  124.1 1.3 collective-permute-start.20
  125.4 6.6 %collective-permute-start.23 = (bf16[2,2,16,576]{3,2,1,0:T(8,128)(2,1)S(1)}, bf16[2,2,16,576]{3,2,1,0:T(8,128)(2,1)S(1)}, u32[]{:S(2)}, u32[]{:S(2)}) collective-permute-start(bf16[2,2,16,576]{3,2,1,0:T(8,128)(2,1)S(1)} %shard_map.128.i0), channel_id=1, source_target_pairs={{0,6},{2,0},{4,2},{6,4},{1,7},{3,1},{5,3},{7,5},{8,14},{10,8},{12,... | collective-permute-start | bytes 221192 | tf_op jit(solution)/shard_map/ppermute | solution.py:302
  128.3 6.6 %collective-permute-start.22 = (bf16[2,2,16,576]{3,2,1,0:T(8,128)(2,1)S(1)}, bf16[2,2,16,576]{3,2,1,0:T(8,128)(2,1)S(1)}, u32[]{:S(2)}, u32[]{:S(2)}) collective-permute-start(bf16[2,2,16,576]{3,2,1,0:T(8,128)(2,1)S(1)} %shard_map.128.i0), channel_id=1, source_target_pairs={{0,4},{2,6},{4,0},{6,2},{1,5},{3,7},{5,1},{7,3},{8,12},{10,14},{12... | collective-permute-start | bytes 221192 | tf_op jit(solution)/shard_map/ppermute | solution.py:302
  128.5 6.9 %collective-permute-start.21 = (bf16[2,2,16,576]{3,2,1,0:T(8,128)(2,1)S(1)}, bf16[2,2,16,576]{3,2,1,0:T(8,128)(2,1)S(1)}, u32[]{:S(2)}, u32[]{:S(2)}) collective-permute-start(bf16[2,2,16,576]{3,2,1,0:T(8,128)(2,1)S(1)} %shard_map.128.i0), channel_id=1, source_target_pairs={{0,2},{2,4},{4,6},{6,0},{1,3},{3,5},{5,7},{7,1},{8,10},{10,12},{12... | collective-permute-start | bytes 221192 | tf_op jit(solution)/shard_map/ppermute | solution.py:302

commit v4 on v3

--- a/solution.py
+++ b/solution.py
@@ -135,20 +135,21 @@
     absorbed = [dot_nt(nope[h], key_up[h]).astype(bf16) for h in heads]
     mixed_grad = [dot_nt(grad[h], value_up[h]).astype(bf16) for h in heads]
 
+    staged = []
     for b in range(BLOCKS_DEV):
         rows = slice(b * BLOCK, (b + 1) * BLOCK)
         ab = jnp.concatenate([absorbed[h][rows] for h in heads], axis=0)
         rb = jnp.concatenate([rope[h][rows] for h in heads], axis=0)
         mg = jnp.concatenate([mixed_grad[h][rows] for h in heads], axis=0)
-        lat = klat[b]
-        rop = krope[b]
+        scores = dot_nt(ab, klat[b]) + dot_nt(rb, krope[b])
+        staged.append((ab, rb, mg, scores, dot_nt(mg, klat[b])))
+    for b, (ab, rb, mg, scores, weight_grad) in enumerate(staged):
         mask = jnp.concatenate([bias[b]] * HEADS_STEP, axis=0)
-        scores = (dot_nt(ab, lat) + dot_nt(rb, rop)) * scale + mask
-        exp_terms = jnp.exp(scores - jnp.max(scores, axis=1, keepdims=True))
+        scores = scores * (scale * math.log2(math.e)) + mask
+        exp_terms = jnp.exp2(scores - jnp.max(scores, axis=1, keepdims=True))
         weights = exp_terms * (1.0 / jnp.sum(exp_terms, axis=1, keepdims=True))
         half = weights.astype(bf16)
         weights_ref[b] = half
-        weight_grad = dot_nt(mg, lat)
         inner = jnp.sum(weights * weight_grad, axis=1, keepdims=True)
         score_grad = (weights * (weight_grad - inner) * scale).astype(bf16)
         sgrad_ref[b] = score_grad

time: 140 us -> 138 us (0.986)
  Pallas kernels: 32.8 us -> 31 us
    pallas_call x1, Pallas kernels: 15.6 us -> 13.8 us  [shards(): call(attend_kernel, (pltpu.HBM((BLOCKS_DEV, rows, KEYS), bf16),) * 2 + (p...]
  transfers between devices with their start and end apart: 30 -> 30, of which waited for: 20 -> 20; matrix products, arithmetic and copies ran while one was open for 3% -> 3% of each run, Pallas kernels for 9% -> 10%
where the time goes in v4:
time: 138 us; the launch traced here: 137 us
  waiting for transfers between devices  53.8 us (39%)
  starting transfers between devices  46 us (33%)
  Pallas kernels  31 us (22%)
  local copies, waits for them, and re-layouts  5.8 us (4%)
    ppermute x21, waiting for transfers between devices, shift(): lax.ppermute(values, axis, [(i, (i + by) % count) for i in range(count)])  38.2 us
    ppermute x21, starting transfers between devices, shift(): lax.ppermute(values, axis, [(i, (i + by) % count) for i in range(count)])  30.3 us
    all_to_all x3, starting transfers between devices, exchange(): return lax.all_to_all(values, axis, split_axis=0, concat_axis=0, tiled=True)  15.4 us
    pallas_call x1, Pallas kernels, shards(): call(attend_kernel, (pltpu.HBM((BLOCKS_DEV, rows, KEYS), bf16),) * 2 + (p...  13.8 us
    all_to_all x3, waiting for transfers between devices, exchange(): return lax.all_to_all(values, axis, split_axis=0, concat_axis=0, tiled=True)  10.6 us
    pallas_call x1, Pallas kernels, shards(): call(project_kernel, (shape(tokens, HEADS_DEV * HEAD_DIM), shape(tokens,...  10 us
    ppermute x6, waiting for transfers between devices, swap_cores(): return lax.ppermute(values, 'c', [(0, 1), (1, 0)])  5.03 us
    unnamed x8, local copies, waits for them, and re-layouts  2.88 us
  transfers between devices with their start and end apart: 30, of which 20 were waited for; matrix products, arithmetic and copies ran while one was open for 3% of the time, Pallas kernels for 10%

profile of v4, /device:TPU:2, one launch (start us, length us, event | category | flops | bytes accessed | tf_op | source)
XLA Modules:
  0.0 137.4 jit_solution(240922709258587162)
XLA Ops:
  0.6 1.2 copy.13.latent_ref
  1.8 0.0 copy-start
  1.8 0.7 copy-done
  2.5 0.8 shard_map.119
  3.3 8.5 %all-to-all-start = ((bf16[8,2,16,576]{3,2,1,0:T(8,128)(2,1)}), bf16[8,2,16,576]{3,2,1,0:T(8,128)(2,1)S(1)}, u32[]{:S(2)}, u32[]{:S(2)}) async-start(bf16[8,2,16,576]{3,2,1,0:T(8,128)(2,1)} %shard_map.119), calls=%async_computation | async-start | bytes 655360 | tf_op jit(solution)/shard_map/all_to_all | solution.py:299
  11.8 0.8 reshape.48.l0.listed_ref
  12.6 1.5 %collective-permute-start.2 = (s32[8]{0:T(128)S(1)}, s32[8]{0:T(128)S(1)}, u32[]{:S(2)}, u32[]{:S(2)}) collective-permute-start(s32[8]{0:T(128)S(1)} %reshape.48.l0.listed_ref), channel_id=1, source_target_pairs={{0,64},{64,128},{128,192},{192,0},{1,65},{65,129},{129,193},{193,1... | collective-permute-start | bytes 104 | tf_op jit(solution)/shard_map/ppermute | solution.py:303
  14.0 1.1 collective-permute-start.1
  15.2 2.2 %collective-permute-start = (s32[8]{0:T(128)S(1)}, s32[8]{0:T(128)S(1)}, u32[]{:S(2)}, u32[]{:S(2)}) collective-permute-start(s32[8]{0:T(128)S(1)} %reshape.48.l0.listed_ref), channel_id=1, source_target_pairs={{0,192},{64,0},{128,64},{192,128},{1,193},{65,1},{129,65},{193,129... | collective-permute-start | bytes 104 | tf_op jit(solution)/shard_map/ppermute | solution.py:303
  17.3 2.1 %copy_bitcast_fusion = (bf16[512,1024]{1,0:T(8,128)(2,1)S(1)}, bf16[512,1024]{1,0:T(8,128)(2,1)S(1)}) fusion(bf16[64,8,8,128]{3,2,1,0:T(8,128)(2,1)} %bitcast.16, bf16[64,8,8,128]{3,2,1,0:T(8,128)(2,1)} %bitcast.17), kind=kLoop, calls=%fused_computation | loop fusion | bytes 4194304 | tf_op jit(solution)/shard_map/reshape | solution.py:340
  19.4 5.7 %all-to-all-done = bf16[8,2,16,576]{3,2,1,0:T(8,128)(2,1)S(1)} async-done(((bf16[8,2,16,576]{3,2,1,0:T(8,128)(2,1)}), bf16[8,2,16,576]{3,2,1,0:T(8,128)(2,1)S(1)}, u32[]{:S(2)}, u32[]{:S(2)}) %all-to-all-start) | async-done | bytes 294944 | tf_op jit(solution)/shard_map/all_to_all | solution.py:299
  25.1 1.4 %shard_map.120 = (bf16[8,16,576]{2,1,0:T(8,128)(2,1)S(1)}, bf16[8,16,576]{2,1,0:T(8,128)(2,1)}, bf16[8,16,576]{2,1,0:T(8,128)(2,1)}, bf16[8,16,576]{2,1,0:T(8,128)(2,1)S(1)}) custom-call(s32[8]{0:T(128)S(1)} %reshape.48.l0.listed_ref, s32[8]{0:T(128)S(1)} %collective-permute-done.l1, s32[8]{0:T(128)S(1)} %collective-permute-done.1.l2, ...), custom_call_target="tpu_custom_call" | custom-call | tf_op jit(solution)/shard_map/pallas_call | solution.py:344
  26.5 1.5 %collective-permute-start.3 = (bf16[8,16,576]{2,1,0:T(8,128)(2,1)}, bf16[8,16,576]{2,1,0:T(8,128)(2,1)S(1)}, u32[]{:S(2)}, u32[]{:S(2)}) collective-permute-start(bf16[8,16,576]{2,1,0:T(8,128)(2,1)} %get-tuple-element.42), channel_id=1, source_target_pairs={{0,64},{64,128},{128,192},{192,0},{1,65},{65,129},{129,193},{193,1... | collective-permute-start | bytes 442376 | tf_op jit(solution)/shard_map/ppermute | solution.py:303
  28.0 1.1 collective-permute-start.4
  29.1 2.2 %collective-permute-start.5 = (bf16[8,16,576]{2,1,0:T(8,128)(2,1)S(1)}, bf16[8,16,576]{2,1,0:T(8,128)(2,1)S(1)}, u32[]{:S(2)}, u32[]{:S(2)}) collective-permute-start(bf16[8,16,576]{2,1,0:T(8,128)(2,1)S(1)} %get-tuple-element.44), channel_id=1, source_target_pairs={{0,192},{64,0},{128,64},{192,128},{1,193},{65,1},{129,65},{193,129... | collective-permute-start | bytes 442376 | tf_op jit(solution)/shard_map/ppermute | solution.py:303
  31.2 2.2 %collective-permute-done.3.i1 = bf16[8,16,576]{2,1,0:T(8,128)(2,1)S(1)} collective-permute-done((bf16[8,16,576]{2,1,0:T(8,128)(2,1)}, bf16[8,16,576]{2,1,0:T(8,128)(2,1)S(1)}, u32[]{:S(2)}, u32[]{:S(2)}) %collective-permute-start.3) | collective-permute-done | bytes 147488 | tf_op jit(solution)/shard_map/ppermute | solution.py:303
  33.4 2.2 %collective-permute-done.4.i2 = bf16[8,16,576]{2,1,0:T(8,128)(2,1)S(1)} collective-permute-done((bf16[8,16,576]{2,1,0:T(8,128)(2,1)}, bf16[8,16,576]{2,1,0:T(8,128)(2,1)S(1)}, u32[]{:S(2)}, u32[]{:S(2)}) %collective-permute-start.4) | collective-permute-done | bytes 147488 | tf_op jit(solution)/shard_map/ppermute | solution.py:303
  35.6 0.7 collective-permute-done.5.i3
  36.3 0.8 shard_map.121.n0
  37.1 3.1 %collective-permute-start.8 = (bf16[8,16,576]{2,1,0:T(8,128)(2,1)S(1)}, bf16[8,16,576]{2,1,0:T(8,128)(2,1)S(1)}, u32[]{:S(2)}, u32[]{:S(2)}) collective-permute-start(bf16[8,16,576]{2,1,0:T(8,128)(2,1)S(1)} %shard_map.121.n0), channel_id=1, source_target_pairs={{0,6},{2,0},{4,2},{6,4},{1,7},{3,1},{5,3},{7,5},{8,14},{10,8},{12,... | collective-permute-start | bytes 442376 | tf_op jit(solution)/shard_map/ppermute | solution.py:303
  40.2 0.6 collective-permute-start.7
  40.8 1.0 collective-permute-start.6
  41.8 3.0 %collective-permute-done.8.n3 = bf16[8,16,576]{2,1,0:T(8,128)(2,1)S(1)} collective-permute-done((bf16[8,16,576]{2,1,0:T(8,128)(2,1)S(1)}, bf16[8,16,576]{2,1,0:T(8,128)(2,1)S(1)}, u32[]{:S(2)}, u32[]{:S(2)}) %collective-permute-start.8) | collective-permute-done | bytes 147488 | tf_op jit(solution)/shard_map/ppermute | solution.py:303
  44.8 2.3 %collective-permute-done.7.n2 = bf16[8,16,576]{2,1,0:T(8,128)(2,1)S(1)} collective-permute-done((bf16[8,16,576]{2,1,0:T(8,128)(2,1)S(1)}, bf16[8,16,576]{2,1,0:T(8,128)(2,1)S(1)}, u32[]{:S(2)}, u32[]{:S(2)}) %collective-permute-start.7) | collective-permute-done | bytes 147488 | tf_op jit(solution)/shard_map/ppermute | solution.py:303
  47.1 1.6 %collective-permute-done.6.n1 = bf16[8,16,576]{2,1,0:T(8,128)(2,1)S(1)} collective-permute-done((bf16[8,16,576]{2,1,0:T(8,128)(2,1)S(1)}, bf16[8,16,576]{2,1,0:T(8,128)(2,1)S(1)}, u32[]{:S(2)}, u32[]{:S(2)}) %collective-permute-start.6) | collective-permute-done | bytes 147488 | tf_op jit(solution)/shard_map/ppermute | solution.py:303
  48.8 0.1 reshape.47.vis_ref
  48.9 1.4 %collective-permute-done.10.f1 = bf16[8,16,576]{2,1,0:T(8,128)(2,1)} collective-permute-done((bf16[8,16,576]{2,1,0:T(8,128)(2,1)S(1)}, bf16[8,16,576]{2,1,0:T(8,128)(2,1)}, u32[]{:S(2)}, u32[]{:S(2)}) %collective-permute-start.10) | collective-permute-done | bytes 147488 | tf_op jit(solution)/shard_map/ppermute | solution.py:311
  50.3 13.8 %shard_map.122 = (bf16[2,1024,640]{2,1,0:T(8,128)(2,1)}, bf16[2,1024,640]{2,1,0:T(8,128)(2,1)}, bf16[2,640,512]{2,1,0:T(8,128)(2,1)}, bf16[2,640,64]{2,1,0:T(8,1...) custom-call(s32[1]{0:T(128)} %bitcast.2.core_ref, s32[1]{0:T(128)} %bitcast.1.y_ref, ...), custom_call_target="tpu_custom_call" | custom-call | flops 6200000000 | bytes 8000000 | tf_op jit(solution)/shard_map/pallas_call | solution.py:361
  64.1 0.2 collective-permute-start.13
  64.4 2.4 %collective-permute-done.13.recv_ref = bf16[4,10,16,576]{3,2,1,0:T(8,128)(2,1)S(1)} collective-permute-done((bf16[4,10,16,576]{3,2,1,0:T(8,128)(2,1)}, bf16[4,10,16,576]{3,2,1,0:T(8,128)(2,1)S(1)}, u32[]{:S(2)}, u32[]{:S(2)}) %collective-permute-start.13) | collective-permute-done | bytes 737312 | tf_op jit(solution)/shard_map/ppermute | solution.py:311
  66.8 0.1 shard_map.123
  66.9 0.1 collective-permute-start.14
  67.0 2.0 %collective-permute-start.15 = (bf16[10,16,576]{2,1,0:T(8,128)(2,1)S(1)}, bf16[10,16,576]{2,1,0:T(8,128)(2,1)S(1)}, u32[]{:S(2)}, u32[]{:S(2)}) collective-permute-start(bf16[10,16,576]{2,1,0:T(8,128)(2,1)S(1)} %get-tuple-element.57), channel_id=1, source_target_pairs={{0,4},{2,6},{4,0},{6,2},{1,5},{3,7},{5,1},{7,3},{8,12},{10,14},{12... | collective-permute-start | bytes 552968 | tf_op jit(solution)/shard_map/ppermute | solution.py:303
  69.0 1.2 collective-permute-start.16
  70.3 10.0 %shard_map.124 = (bf16[256,1024]{1,0:T(8,128)(2,1)}, bf16[256,1536]{1,0:T(8,128)(2,1)}, bf16[128,2048]{1,0:T(8,128)(2,1)S(1)}, bf16[128,2048]{1,0:T(8,128)(2,1)}...) custom-call(s32[1]{0:T(128)} %bitcast.x_ref, bf16[256,1536]{1,0:T(8,128)(2,1)} %query_ref.3, ...), custom_call_target="tpu_custom_call" | custom-call | flops 4000000000 | bytes 8000000 | tf_op jit(solution)/shard_map/pallas_call | solution.py:386
  80.3 0.1 collective-permute-done.16.r3_ref
  80.3 0.1 shard_map.125
  80.4 1.6 %collective-permute-start.19 = (bf16[8,16,576]{2,1,0:T(8,128)(2,1)S(1)}, bf16[8,16,576]{2,1,0:T(8,128)(2,1)S(1)}, u32[]{:S(2)}, u32[]{:S(2)}) collective-permute-start(bf16[8,16,576]{2,1,0:T(8,128)(2,1)S(1)} %get-tuple-element.64.i0), channel_id=1, source_target_pairs={{0,64},{64,128},{128,192},{192,0},{1,65},{65,129},{129,193},{193,1... | collective-permute-start | bytes 442376 | tf_op jit(solution)/shard_map/ppermute | solution.py:303
  82.0 1.4 %collective-permute-start.18 = (bf16[8,16,576]{2,1,0:T(8,128)(2,1)S(1)}, bf16[8,16,576]{2,1,0:T(8,128)(2,1)S(1)}, u32[]{:S(2)}, u32[]{:S(2)}) collective-permute-start(bf16[8,16,576]{2,1,0:T(8,128)(2,1)S(1)} %get-tuple-element.64.i0), channel_id=1, source_target_pairs={{0,128},{64,192},{128,0},{192,64},{1,129},{65,193},{129,1},{193,65... | collective-permute-start | bytes 442376 | tf_op jit(solution)/shard_map/ppermute | solution.py:303
  83.5 1.7 %collective-permute-start.17 = (bf16[8,16,576]{2,1,0:T(8,128)(2,1)S(1)}, bf16[8,16,576]{2,1,0:T(8,128)(2,1)S(1)}, u32[]{:S(2)}, u32[]{:S(2)}) collective-permute-start(bf16[8,16,576]{2,1,0:T(8,128)(2,1)S(1)} %get-tuple-element.64.i0), channel_id=1, source_target_pairs={{0,192},{64,0},{128,64},{192,128},{1,193},{65,1},{129,65},{193,129... | collective-permute-start | bytes 442376 | tf_op jit(solution)/shard_map/ppermute | solution.py:303
  85.1 0.4 collective-permute-start.24
  85.5 3.3 %collective-permute-start.25 = (bf16[128,2048]{1,0:T(8,128)(2,1)}, bf16[128,2048]{1,0:T(8,128)(2,1)S(1)}, u32[]{:S(2)}, u32[]{:S(2)}) collective-permute-start(bf16[128,2048]{1,0:T(8,128)(2,1)} %get-tuple-element.67), channel_id=1, source_target_pairs={{0,128},{64,192},{128,0},{192,64},{1,129},{65,193},{129,1},{193,65... | collective-permute-start | bytes 1572872 | tf_op jit(solution)/shard_map/ppermute | solution.py:303
  88.8 0.1 collective-permute-done.19.i3
  88.9 0.4 collective-permute-start.26
  89.3 1.4 %collective-permute-done.18.i2 = bf16[8,16,576]{2,1,0:T(8,128)(2,1)S(1)} collective-permute-done((bf16[8,16,576]{2,1,0:T(8,128)(2,1)S(1)}, bf16[8,16,576]{2,1,0:T(8,128)(2,1)S(1)}, u32[]{:S(2)}, u32[]{:S(2)}) %collective-permute-start.18) | collective-permute-done | bytes 147488 | tf_op jit(solution)/shard_map/ppermute | solution.py:303
  90.7 11.5 %collective-permute-done.17.i1 = bf16[8,16,576]{2,1,0:T(8,128)(2,1)S(1)} collective-permute-done((bf16[8,16,576]{2,1,0:T(8,128)(2,1)S(1)}, bf16[8,16,576]{2,1,0:T(8,128)(2,1)S(1)}, u32[]{:S(2)}, u32[]{:S(2)}) %collective-permute-start.17) | collective-permute-done | bytes 147488 | tf_op jit(solution)/shard_map/ppermute | solution.py:303
  102.2 1.8 %shard_map.126 = bf16[8,2,16,576]{3,2,1,0:T(8,128)(2,1)} custom-call(s32[1]{0:T(128)} %bitcast.x_ref, s32[1]{0:T(128)} %bitcast.5.z_ref, s32[8]{0:T(128)S(1)} %reshape.48.l0.listed_ref, s32[8]{0:T(128)S(1)} %collective-permute-done.l1, s32[8]{0:T(128)S(1)} %collective-permute-done.1.l2, s32[8]{0:T(128)S(1)} %collective-permute-done.2.l3, ...), custom_call_target="tpu_custom_call" | custom-call | tf_op jit(solution)/shard_map/pallas_call | solution.py:404
  104.0 3.4 %all-to-all-start.1 = ((bf16[8,2,16,576]{3,2,1,0:T(8,128)(2,1)}), bf16[8,2,16,576]{3,2,1,0:T(8,128)(2,1)S(1)}, u32[]{:S(2)}, u32[]{:S(2)}) async-start(bf16[8,2,16,576]{3,2,1,0:T(8,128)(2,1)} %shard_map.126), calls=%async_computation.1 | async-start | bytes 655360 | tf_op jit(solution)/shard_map/all_to_all | solution.py:299
  107.5 7.1 %collective-permute-done.26.w3 = bf16[128,2048]{1,0:T(8,128)(2,1)S(1)} collective-permute-done((bf16[128,2048]{1,0:T(8,128)(2,1)}, bf16[128,2048]{1,0:T(8,128)(2,1)S(1)}, u32[]{:S(2)}, u32[]{:S(2)}) %collective-permute-start.26) | collective-permute-done | bytes 524320 | tf_op jit(solution)/shard_map/ppermute | solution.py:303
  114.5 1.0 shard_map.130
  115.6 3.0 %all-to-all-done.1.in_ref = bf16[8,2,16,576]{3,2,1,0:T(8,128)(2,1)S(1)} async-done(((bf16[8,2,16,576]{3,2,1,0:T(8,128)(2,1)}), bf16[8,2,16,576]{3,2,1,0:T(8,128)(2,1)S(1)}, u32[]{:S(2)}, u32[]{:S(2)}) %all-to-all-start.1) | async-done | bytes 294944 | tf_op jit(solution)/shard_map/all_to_all | solution.py:299
  118.5 3.5 %all-to-all-start.2 = ((bf16[8,16,2048]{2,1,0:T(8,128)(2,1)}), bf16[8,16,2048]{2,1,0:T(8,128)(2,1)S(1)}, u32[]{:S(2)}, u32[]{:S(2)}) async-start(bf16[8,16,2048]{2,1,0:T(8,128)(2,1)} %shard_map.130), calls=%async_computation.2 | async-start | bytes 1048576 | tf_op jit(solution)/shard_map/all_to_all | solution.py:299
  122.1 0.1 collective-permute-start.20
  122.2 1.2 collective-permute-done.20.far_ref
  123.4 2.8 %collective-permute-start.23 = (bf16[2,2,16,576]{3,2,1,0:T(8,128)(2,1)S(1)}, bf16[2,2,16,576]{3,2,1,0:T(8,128)(2,1)S(1)}, u32[]{:S(2)}, u32[]{:S(2)}) collective-permute-start(bf16[2,2,16,576]{3,2,1,0:T(8,128)(2,1)S(1)} %shard_map.128.i0), channel_id=1, source_target_pairs={{0,6},{2,0},{4,2},{6,4},{1,7},{3,1},{5,3},{7,5},{8,14},{10,8},{12,... | collective-permute-start | bytes 221192 | tf_op jit(solution)/shard_map/ppermute | solution.py:303
  126.2 0.3 collective-permute-start.22
  126.5 0.9 collective-permute-start.21
  127.4 2.6 %collective-permute-done.23.i3 = bf16[2,2,16,576]{3,2,1,0:T(8,128)(2,1)S(1)} collective-permute-done((bf16[2,2,16,576]{3,2,1,0:T(8,128)(2,1)S(1)}, bf16[2,2,16,576]{3,2,1,0:T(8,128)(2,1)S(1)}, u32[]{:S(2)}, u32[]{:S(2)}) %collective-permute-start.23) | collective-permute-done | bytes 73760 | tf_op jit(solution)/shard_map/ppermute | solution.py:303
  130.0 2.8 %collective-permute-done.22.i2 = bf16[2,2,16,576]{3,2,1,0:T(8,128)(2,1)S(1)} collective-permute-done((bf16[2,2,16,576]{3,2,1,0:T(8,128)(2,1)S(1)}, bf16[2,2,16,576]{3,2,1,0:T(8,128)(2,1)S(1)}, u32[]{:S(2)}, u32[]{:S(2)}) %collective-permute-start.22) | collective-permute-done | bytes 73760 | tf_op jit(solution)/shard_map/ppermute | solution.py:303
  132.9 0.6 collective-permute-done.21.i1
  133.4 0.3 shard_map.129
  133.7 1.0 copy.16
  134.7 1.9 %all-to-all-done.2.in_ref = bf16[8,16,2048]{2,1,0:T(8,128)(2,1)S(1)} async-done(((bf16[8,16,2048]{2,1,0:T(8,128)(2,1)}), bf16[8,16,2048]{2,1,0:T(8,128)(2,1)S(1)}, u32[]{:S(2)}, u32[]{:S(2)}) %all-to-all-start.2) | async-done | bytes 524320 | tf_op jit(solution)/shard_map/all_to_all | solution.py:299
  136.6 0.8 shard_map.131
  (20 shorter events, 0.1 us)
Async XLA Ops:
  1.8 0.7 copy-start
  3.3 21.7 %all-to-all-start = ((bf16[8,2,16,576]{3,2,1,0:T(8,128)(2,1)}), bf16[8,2,16,576]{3,2,1,0:T(8,128)(2,1)S(1)}, u32[]{:S(2)}, u32[]{:S(2)}) async-start(bf16[8,2,16,576]{3,2,1,0:T(8,128)(2,1)} %shard_map.119), calls=%async_computation | async-start | bytes 655360 | tf_op jit(solution)/shard_map/all_to_all | solution.py:299
  12.6 12.5 %collective-permute-start.2 = (s32[8]{0:T(128)S(1)}, s32[8]{0:T(128)S(1)}, u32[]{:S(2)}, u32[]{:S(2)}) collective-permute-start(s32[8]{0:T(128)S(1)} %reshape.48.l0.listed_ref), channel_id=1, source_target_pairs={{0,64},{64,128},{128,192},{192,0},{1,65},{65,129},{129,193},{193,1... | collective-permute-start | bytes 104 | tf_op jit(solution)/shard_map/ppermute | solution.py:303
  14.0 11.0 %collective-permute-start.1 = (s32[8]{0:T(128)S(1)}, s32[8]{0:T(128)S(1)}, u32[]{:S(2)}, u32[]{:S(2)}) collective-permute-start(s32[8]{0:T(128)S(1)} %reshape.48.l0.listed_ref), channel_id=1, source_target_pairs={{0,128},{64,192},{128,0},{192,64},{1,129},{65,193},{129,1},{193,65... | collective-permute-start | bytes 104 | tf_op jit(solution)/shard_map/ppermute | solution.py:303
  15.2 9.9 %collective-permute-start = (s32[8]{0:T(128)S(1)}, s32[8]{0:T(128)S(1)}, u32[]{:S(2)}, u32[]{:S(2)}) collective-permute-start(s32[8]{0:T(128)S(1)} %reshape.48.l0.listed_ref), channel_id=1, source_target_pairs={{0,192},{64,0},{128,64},{192,128},{1,193},{65,1},{129,65},{193,129... | collective-permute-start | bytes 104 | tf_op jit(solution)/shard_map/ppermute | solution.py:303
  17.3 31.5 %copy-start.2 = (s32[2,4]{1,0:T(2,128)S(1)}, s32[2,4]{1,0:T(2,128)}, u32[]{:S(2)}) copy-start(s32[2,4]{1,0:T(2,128)} %param.15) | copy-start | bytes 100
  17.3 33.0 %copy-start.1 = (f32[512]{0:T(512)S(1)}, f32[512]{0:T(512)}, u32[]{:S(2)}) copy-start(f32[512]{0:T(512)} %param.10) | copy-start | bytes 6148
  26.5 7.0 %collective-permute-start.3 = (bf16[8,16,576]{2,1,0:T(8,128)(2,1)}, bf16[8,16,576]{2,1,0:T(8,128)(2,1)S(1)}, u32[]{:S(2)}, u32[]{:S(2)}) collective-permute-start(bf16[8,16,576]{2,1,0:T(8,128)(2,1)} %get-tuple-element.42), channel_id=1, source_target_pairs={{0,64},{64,128},{128,192},{192,0},{1,65},{65,129},{129,193},{193,1... | collective-permute-start | bytes 442376 | tf_op jit(solution)/shard_map/ppermute | solution.py:303
  28.0 7.6 %collective-permute-start.4 = (bf16[8,16,576]{2,1,0:T(8,128)(2,1)}, bf16[8,16,576]{2,1,0:T(8,128)(2,1)S(1)}, u32[]{:S(2)}, u32[]{:S(2)}) collective-permute-start(bf16[8,16,576]{2,1,0:T(8,128)(2,1)} %get-tuple-element.43), channel_id=1, source_target_pairs={{0,128},{64,192},{128,0},{192,64},{1,129},{65,193},{129,1},{193,65... | collective-permute-start | bytes 442376 | tf_op jit(solution)/shard_map/ppermute | solution.py:303
  29.1 7.2 %collective-permute-start.5 = (bf16[8,16,576]{2,1,0:T(8,128)(2,1)S(1)}, bf16[8,16,576]{2,1,0:T(8,128)(2,1)S(1)}, u32[]{:S(2)}, u32[]{:S(2)}) collective-permute-start(bf16[8,16,576]{2,1,0:T(8,128)(2,1)S(1)} %get-tuple-element.44), channel_id=1, source_target_pairs={{0,192},{64,0},{128,64},{192,128},{1,193},{65,1},{129,65},{193,129... | collective-permute-start | bytes 442376 | tf_op jit(solution)/shard_map/ppermute | solution.py:303
  37.1 7.7 %collective-permute-start.8 = (bf16[8,16,576]{2,1,0:T(8,128)(2,1)S(1)}, bf16[8,16,576]{2,1,0:T(8,128)(2,1)S(1)}, u32[]{:S(2)}, u32[]{:S(2)}) collective-permute-start(bf16[8,16,576]{2,1,0:T(8,128)(2,1)S(1)} %shard_map.121.n0), channel_id=1, source_target_pairs={{0,6},{2,0},{4,2},{6,4},{1,7},{3,1},{5,3},{7,5},{8,14},{10,8},{12,... | collective-permute-start | bytes 442376 | tf_op jit(solution)/shard_map/ppermute | solution.py:303
  40.2 6.9 %collective-permute-start.7 = (bf16[8,16,576]{2,1,0:T(8,128)(2,1)S(1)}, bf16[8,16,576]{2,1,0:T(8,128)(2,1)S(1)}, u32[]{:S(2)}, u32[]{:S(2)}) collective-permute-start(bf16[8,16,576]{2,1,0:T(8,128)(2,1)S(1)} %shard_map.121.n0), channel_id=1, source_target_pairs={{0,4},{2,6},{4,0},{6,2},{1,5},{3,7},{5,1},{7,3},{8,12},{10,14},{12... | collective-permute-start | bytes 442376 | tf_op jit(solution)/shard_map/ppermute | solution.py:303
  40.8 7.9 %collective-permute-start.6 = (bf16[8,16,576]{2,1,0:T(8,128)(2,1)S(1)}, bf16[8,16,576]{2,1,0:T(8,128)(2,1)S(1)}, u32[]{:S(2)}, u32[]{:S(2)}) collective-permute-start(bf16[8,16,576]{2,1,0:T(8,128)(2,1)S(1)} %shard_map.121.n0), channel_id=1, source_target_pairs={{0,2},{2,4},{4,6},{6,0},{1,3},{3,5},{5,7},{7,1},{8,10},{10,12},{12... | collective-permute-start | bytes 442376 | tf_op jit(solution)/shard_map/ppermute | solution.py:303
  41.8 7.1 %collective-permute-start.9 = (bf16[8,16,576]{2,1,0:T(8,128)(2,1)S(1)}, bf16[8,16,576]{2,1,0:T(8,128)(2,1)S(1)}, u32[]{:S(2)}, u32[]{:S(2)}) collective-permute-start(bf16[8,16,576]{2,1,0:T(8,128)(2,1)S(1)} %shard_map.121.n0), channel_id=1, source_target_pairs={{0,1},{1,0},{2,3},{3,2},{4,5},{5,4},{6,7},{7,6},{8,9},{9,8},{10,11... | collective-permute-start | bytes 442376 | tf_op jit(solution)/shard_map/ppermute | solution.py:311
  44.8 4.0 %collective-permute-start.12 = (bf16[8,16,576]{2,1,0:T(8,128)(2,1)S(1)}, bf16[8,16,576]{2,1,0:T(8,128)(2,1)S(1)}, u32[]{:S(2)}, u32[]{:S(2)}) collective-permute-start(bf16[8,16,576]{2,1,0:T(8,128)(2,1)S(1)} %collective-permute-done.8.n3), channel_id=1, source_target_pairs={{0,1},{1,0},{2,3},{3,2},{4,5},{5,4},{6,7},{7,6},{8,9},{9,8},{10,11... | collective-permute-start | bytes 442376 | tf_op jit(solution)/shard_map/ppermute | solution.py:311
  47.1 1.7 %collective-permute-start.11 = (bf16[8,16,576]{2,1,0:T(8,128)(2,1)S(1)}, bf16[8,16,576]{2,1,0:T(8,128)(2,1)}, u32[]{:S(2)}, u32[]{:S(2)}) collective-permute-start(bf16[8,16,576]{2,1,0:T(8,128)(2,1)S(1)} %collective-permute-done.7.n2), channel_id=1, source_target_pairs={{0,1},{1,0},{2,3},{3,2},{4,5},{5,4},{6,7},{7,6},{8,9},{9,8},{10,11... | collective-permute-start | bytes 442376 | tf_op jit(solution)/shard_map/ppermute | solution.py:311
  48.8 1.5 %collective-permute-start.10 = (bf16[8,16,576]{2,1,0:T(8,128)(2,1)S(1)}, bf16[8,16,576]{2,1,0:T(8,128)(2,1)}, u32[]{:S(2)}, u32[]{:S(2)}) collective-permute-start(bf16[8,16,576]{2,1,0:T(8,128)(2,1)S(1)} %collective-permute-done.6.n1), channel_id=1, source_target_pairs={{0,1},{1,0},{2,3},{3,2},{4,5},{5,4},{6,7},{7,6},{8,9},{9,8},{10,11... | collective-permute-start | bytes 442376 | tf_op jit(solution)/shard_map/ppermute | solution.py:311
  64.1 2.6 %collective-permute-start.13 = (bf16[4,10,16,576]{3,2,1,0:T(8,128)(2,1)}, bf16[4,10,16,576]{3,2,1,0:T(8,128)(2,1)S(1)}, u32[]{:S(2)}, u32[]{:S(2)}) collective-permute-start(bf16[4,10,16,576]{3,2,1,0:T(8,128)(2,1)} %get-tuple-element.46), channel_id=1, source_target_pairs={{0,1},{1,0},{2,3},{3,2},{4,5},{5,4},{6,7},{7,6},{8,9},{9,8},{10,11... | collective-permute-start | bytes 2211848 | tf_op jit(solution)/shard_map/ppermute | solution.py:311
  66.9 13.4 %collective-permute-start.14 = (bf16[10,16,576]{2,1,0:T(8,128)(2,1)S(1)}, bf16[10,16,576]{2,1,0:T(8,128)(2,1)S(1)}, u32[]{:S(2)}, u32[]{:S(2)}) collective-permute-start(bf16[10,16,576]{2,1,0:T(8,128)(2,1)S(1)} %get-tuple-element.56), channel_id=1, source_target_pairs={{0,2},{2,4},{4,6},{6,0},{1,3},{3,5},{5,7},{7,1},{8,10},{10,12},{12... | collective-permute-start | bytes 552968 | tf_op jit(solution)/shard_map/ppermute | solution.py:303
  67.0 13.3 %collective-permute-start.15 = (bf16[10,16,576]{2,1,0:T(8,128)(2,1)S(1)}, bf16[10,16,576]{2,1,0:T(8,128)(2,1)S(1)}, u32[]{:S(2)}, u32[]{:S(2)}) collective-permute-start(bf16[10,16,576]{2,1,0:T(8,128)(2,1)S(1)} %get-tuple-element.57), channel_id=1, source_target_pairs={{0,4},{2,6},{4,0},{6,2},{1,5},{3,7},{5,1},{7,3},{8,12},{10,14},{12... | collective-permute-start | bytes 552968 | tf_op jit(solution)/shard_map/ppermute | solution.py:303
  69.0 11.3 %collective-permute-start.16 = (bf16[10,16,576]{2,1,0:T(8,128)(2,1)S(1)}, bf16[10,16,576]{2,1,0:T(8,128)(2,1)S(1)}, u32[]{:S(2)}, u32[]{:S(2)}) collective-permute-start(bf16[10,16,576]{2,1,0:T(8,128)(2,1)S(1)} %get-tuple-element.58), channel_id=1, source_target_pairs={{0,6},{2,0},{4,2},{6,4},{1,7},{3,1},{5,3},{7,5},{8,14},{10,8},{12,... | collective-permute-start | bytes 552968 | tf_op jit(solution)/shard_map/ppermute | solution.py:303
  80.4 8.4 %collective-permute-start.19 = (bf16[8,16,576]{2,1,0:T(8,128)(2,1)S(1)}, bf16[8,16,576]{2,1,0:T(8,128)(2,1)S(1)}, u32[]{:S(2)}, u32[]{:S(2)}) collective-permute-start(bf16[8,16,576]{2,1,0:T(8,128)(2,1)S(1)} %get-tuple-element.64.i0), channel_id=1, source_target_pairs={{0,64},{64,128},{128,192},{192,0},{1,65},{65,129},{129,193},{193,1... | collective-permute-start | bytes 442376 | tf_op jit(solution)/shard_map/ppermute | solution.py:303
  82.0 8.6 %collective-permute-start.18 = (bf16[8,16,576]{2,1,0:T(8,128)(2,1)S(1)}, bf16[8,16,576]{2,1,0:T(8,128)(2,1)S(1)}, u32[]{:S(2)}, u32[]{:S(2)}) collective-permute-start(bf16[8,16,576]{2,1,0:T(8,128)(2,1)S(1)} %get-tuple-element.64.i0), channel_id=1, source_target_pairs={{0,128},{64,192},{128,0},{192,64},{1,129},{65,193},{129,1},{193,65... | collective-permute-start | bytes 442376 | tf_op jit(solution)/shard_map/ppermute | solution.py:303
  83.5 18.7 %collective-permute-start.17 = (bf16[8,16,576]{2,1,0:T(8,128)(2,1)S(1)}, bf16[8,16,576]{2,1,0:T(8,128)(2,1)S(1)}, u32[]{:S(2)}, u32[]{:S(2)}) collective-permute-start(bf16[8,16,576]{2,1,0:T(8,128)(2,1)S(1)} %get-tuple-element.64.i0), channel_id=1, source_target_pairs={{0,192},{64,0},{128,64},{192,128},{1,193},{65,1},{129,65},{193,129... | collective-permute-start | bytes 442376 | tf_op jit(solution)/shard_map/ppermute | solution.py:303
  85.1 22.3 %collective-permute-start.24 = (bf16[128,2048]{1,0:T(8,128)(2,1)}, bf16[128,2048]{1,0:T(8,128)(2,1)S(1)}, u32[]{:S(2)}, u32[]{:S(2)}) collective-permute-start(bf16[128,2048]{1,0:T(8,128)(2,1)} %get-tuple-element.66), channel_id=1, source_target_pairs={{0,64},{64,128},{128,192},{192,0},{1,65},{65,129},{129,193},{193,1... | collective-permute-start | bytes 1572872 | tf_op jit(solution)/shard_map/ppermute | solution.py:303
  85.5 21.9 %collective-permute-start.25 = (bf16[128,2048]{1,0:T(8,128)(2,1)}, bf16[128,2048]{1,0:T(8,128)(2,1)S(1)}, u32[]{:S(2)}, u32[]{:S(2)}) collective-permute-start(bf16[128,2048]{1,0:T(8,128)(2,1)} %get-tuple-element.67), channel_id=1, source_target_pairs={{0,128},{64,192},{128,0},{192,64},{1,129},{65,193},{129,1},{193,65... | collective-permute-start | bytes 1572872 | tf_op jit(solution)/shard_map/ppermute | solution.py:303
  88.9 25.6 %collective-permute-start.26 = (bf16[128,2048]{1,0:T(8,128)(2,1)}, bf16[128,2048]{1,0:T(8,128)(2,1)S(1)}, u32[]{:S(2)}, u32[]{:S(2)}) collective-permute-start(bf16[128,2048]{1,0:T(8,128)(2,1)} %get-tuple-element.68), channel_id=1, source_target_pairs={{0,192},{64,0},{128,64},{192,128},{1,193},{65,1},{129,65},{193,129... | collective-permute-start | bytes 1572872 | tf_op jit(solution)/shard_map/ppermute | solution.py:303
  104.0 14.5 %all-to-all-start.1 = ((bf16[8,2,16,576]{3,2,1,0:T(8,128)(2,1)}), bf16[8,2,16,576]{3,2,1,0:T(8,128)(2,1)S(1)}, u32[]{:S(2)}, u32[]{:S(2)}) async-start(bf16[8,2,16,576]{3,2,1,0:T(8,128)(2,1)} %shard_map.126), calls=%async_computation.1 | async-start | bytes 655360 | tf_op jit(solution)/shard_map/all_to_all | solution.py:299
  118.5 18.1 %all-to-all-start.2 = ((bf16[8,16,2048]{2,1,0:T(8,128)(2,1)}), bf16[8,16,2048]{2,1,0:T(8,128)(2,1)S(1)}, u32[]{:S(2)}, u32[]{:S(2)}) async-start(bf16[8,16,2048]{2,1,0:T(8,128)(2,1)} %shard_map.130), calls=%async_computation.2 | async-start | bytes 1048576 | tf_op jit(solution)/shard_map/all_to_all | solution.py:299
  122.1 1.3 collective-permute-start.20
  123.4 6.6 %collective-permute-start.23 = (bf16[2,2,16,576]{3,2,1,0:T(8,128)(2,1)S(1)}, bf16[2,2,16,576]{3,2,1,0:T(8,128)(2,1)S(1)}, u32[]{:S(2)}, u32[]{:S(2)}) collective-permute-start(bf16[2,2,16,576]{3,2,1,0:T(8,128)(2,1)S(1)} %shard_map.128.i0), channel_id=1, source_target_pairs={{0,6},{2,0},{4,2},{6,4},{1,7},{3,1},{5,3},{7,5},{8,14},{10,8},{12,... | collective-permute-start | bytes 221192 | tf_op jit(solution)/shard_map/ppermute | solution.py:303
  126.2 6.6 %collective-permute-start.22 = (bf16[2,2,16,576]{3,2,1,0:T(8,128)(2,1)S(1)}, bf16[2,2,16,576]{3,2,1,0:T(8,128)(2,1)S(1)}, u32[]{:S(2)}, u32[]{:S(2)}) collective-permute-start(bf16[2,2,16,576]{3,2,1,0:T(8,128)(2,1)S(1)} %shard_map.128.i0), channel_id=1, source_target_pairs={{0,4},{2,6},{4,0},{6,2},{1,5},{3,7},{5,1},{7,3},{8,12},{10,14},{12... | collective-permute-start | bytes 221192 | tf_op jit(solution)/shard_map/ppermute | solution.py:303
  126.5 6.9 %collective-permute-start.21 = (bf16[2,2,16,576]{3,2,1,0:T(8,128)(2,1)S(1)}, bf16[2,2,16,576]{3,2,1,0:T(8,128)(2,1)S(1)}, u32[]{:S(2)}, u32[]{:S(2)}) collective-permute-start(bf16[2,2,16,576]{3,2,1,0:T(8,128)(2,1)S(1)} %shard_map.128.i0), channel_id=1, source_target_pairs={{0,2},{2,4},{4,6},{6,0},{1,3},{3,5},{5,7},{7,1},{8,10},{10,12},{12... | collective-permute-start | bytes 221192 | tf_op jit(solution)/shard_map/ppermute | solution.py:303

commit v5 on v4

--- a/solution.py
+++ b/solution.py
@@ -173,7 +173,7 @@
 
 def project_kernel(
     x_ref, query_ref, grad_ref, key_up_ref, value_up_ref, sgrad_ref, weights_ref, klat, krope,
-    attn_ref, qgrad_ref, w0_ref, w1_ref, w2_ref, w3_ref,
+    attn_ref, qgrad_ref, w0_ref, w1_ref, w3_ref, w2a_ref, w2b_ref,
     wgrad,
 ):
     heads = range(HEADS_STEP)
@@ -202,9 +202,17 @@
         wgrad[:, at : at + HEAD_DIM] = dot_tn(full, nope[h]).astype(bf16)
         wgrad[:, width + at : width + at + HEAD_DIM] = dot_tn(mixed, grad[h]).astype(bf16)
 
-    for r, out in enumerate((w0_ref, w1_ref, w2_ref, w3_ref)):
-        start = pl.multiple_of(((x_ref[0] + r) % NX) * PART, PART)
-        out[...] = wgrad[pl.ds(start, PART), :]
+    for out, r, skip in ((w0_ref, 0, 0), (w1_ref, 1, 0), (w3_ref, 3, 0), (w2a_ref, 2, 0), (w2b_ref, 2, PART // 2)):
+        start = pl.multiple_of(((x_ref[0] + r) % NX) * PART + skip, PART // 2)
+        out[...] = wgrad[pl.ds(start, out.shape[0]), :]
+
+
+def relay_kernel(w1_ref, w3_ref, a_ref, b_ref, u1_ref, u3_ref):
+    half = PART // 2
+    u1_ref[:half] = (w1_ref[:half].astype(f32) + a_ref[...].astype(f32)).astype(bf16)
+    u1_ref[half:] = w1_ref[half:]
+    u3_ref[:half] = w3_ref[:half]
+    u3_ref[half:] = (w3_ref[half:].astype(f32) + b_ref[...].astype(f32)).astype(bf16)
 
 
 def pair_kernel(keep_ref, recv_ref, own_ref, s1_ref, s2_ref, s3_ref):
@@ -244,10 +252,10 @@
     out_ref[...] = total.astype(bf16)
 
 
-def part_kernel(w0, w1, w2, w3, out_ref):
+def part_kernel(w0, w1, w3, out_ref):
     for z in range(NZ):
         rows = slice(z * ROWS, (z + 1) * ROWS)
-        out_ref[z] = sum(ref[rows].astype(f32) for ref in (w0, w1, w2, w3)).astype(bf16)
+        out_ref[z] = sum(ref[rows].astype(f32) for ref in (w0, w1, w3)).astype(bf16)
 
 
 def weights_kernel(in_ref, key_ref, value_ref):
@@ -385,15 +393,18 @@
     own, score_grad = lax.optimization_barrier((own, score_grad))
     attn_out, query_grad, *wgrads = call(
         project_kernel,
-        (shape(tokens, HEADS_DEV * HEAD_DIM), shape(tokens, HEADS_DEV * QDIM)) + (shape(PART, wcols),) * NX,
+        (shape(tokens, HEADS_DEV * HEAD_DIM), shape(tokens, HEADS_DEV * QDIM)) + (shape(PART, wcols),) * 3 + (shape(PART // 2, wcols),) * 2,
         [smem()] + operand_specs + [by_rows, by_rows, whole(*lat_keys), whole(*rope_keys)],
-        out_specs=(columns(tokens, width), columns(tokens, HEADS_STEP * QDIM)) + (columns(PART, 2 * width),) * NX,
+        out_specs=(columns(tokens, width), columns(tokens, HEADS_STEP * QDIM)) + (columns(PART, 2 * width),) * 3 + (columns(PART // 2, 2 * width),) * 2,
         grid=(steps,),
         scratch_shapes=[pltpu.VMEM((LATENT, 2 * width), bf16)],
         cost_estimate=cost(4_000_000_000),
     )(x, *operands, in_hbm(score_grad), in_hbm(weights), in_hbm(klat), in_hbm(krope))
-    parts = [shift(w, "x", NX, r) for r, w in enumerate(wgrads) if r > 0]
-    *others, wgrads[0] = lax.optimization_barrier((*others, wgrads[0]))
+    w0, w1, w3, w2a, w2b = wgrads
+    relayed = (shift(w2a, "x", NX, 1), shift(w2b, "x", NX, -1))
+    u1, u3 = call(relay_kernel, (shape(PART, wcols),) * 2, [vmem()] * 4, out_specs=(vmem(),) * 2)(w1, w3, *relayed)
+    parts = [shift(u1, "x", NX, 1), shift(u3, "x", NX, -1)]
+    *others, w0 = lax.optimization_barrier((*others, w0))
     own, spread = call(
         slots_kernel,
         (shape(BLOCKS_DEV, ROWS, KV, dtype=f32), shape(slots, ROWS, KV)),
@@ -408,7 +419,7 @@
         scratch_shapes=[pltpu.VMEM((COLUMN, ROWS, KV), f32)],
     )(x, z, *lists, own, spread, *others)
     line = exchange(line, "z")
-    part = call(part_kernel, shape(NZ, ROWS, wcols), [vmem()] * NX)(wgrads[0], *parts)
+    part = call(part_kernel, shape(NZ, ROWS, wcols), [vmem()] * 3)(w0, *parts)
     part = exchange(part, "z")
     total = call(line_kernel, shape(BLOCKS_DEV, ROWS, KV), [vmem()])(line)
     total = call(cores_kernel, shape(BLOCKS_DEV, NC, ROWS, KV), [smem(), vmem(), vmem()])(

time: 138 us -> 133 us (0.964)
  waiting for transfers between devices: 53.8 us -> 47.4 us
    ppermute x21 -> x22, waiting for transfers between devices: 38.2 us -> 28.8 us  [shift(): lax.ppermute(values, axis, [(i, (i + by) % count) for i in range(count)])]
    all_to_all x3, waiting for transfers between devices: 10.6 us -> 13.6 us  [exchange(): return lax.all_to_all(values, axis, split_axis=0, concat_axis=0, tiled=True)]
    ppermute x21 -> x22, starting transfers between devices: 30.3 us -> 30.4 us  [shift(): lax.ppermute(values, axis, [(i, (i + by) % count) for i in range(count)])]
  transfers between devices with their start and end apart: 30 -> 31, of which waited for: 20 -> 20; matrix products, arithmetic and copies ran while one was open for 3% -> 3% of each run, Pallas kernels for 10% -> 11%
where the time goes in v5:
time: 133 us; the launch traced here: 132 us
  waiting for transfers between devices  47.4 us (36%)
  starting transfers between devices  46.1 us (35%)
  Pallas kernels  31.9 us (24%)
  local copies, waits for them, and re-layouts  5.8 us (4%)
    ppermute x22, starting transfers between devices, shift(): lax.ppermute(values, axis, [(i, (i + by) % count) for i in range(count)])  30.4 us
    ppermute x22, waiting for transfers between devices, shift(): lax.ppermute(values, axis, [(i, (i + by) % count) for i in range(count)])  28.8 us
    all_to_all x3, starting transfers between devices, exchange(): return lax.all_to_all(values, axis, split_axis=0, concat_axis=0, tiled=True)  15.4 us
    pallas_call x1, Pallas kernels, shards(): call(attend_kernel, (pltpu.HBM((BLOCKS_DEV, rows, KEYS), bf16),) * 2 + (p...  13.9 us
    all_to_all x3, waiting for transfers between devices, exchange(): return lax.all_to_all(values, axis, split_axis=0, concat_axis=0, tiled=True)  13.6 us
    pallas_call x1, Pallas kernels, shards(): call(project_kernel, (shape(tokens, HEADS_DEV * HEAD_DIM), shape(tokens,...  9.72 us
    ppermute x6, waiting for transfers between devices, swap_cores(): return lax.ppermute(values, 'c', [(0, 1), (1, 0)])  5.05 us
    unnamed x8, local copies, waits for them, and re-layouts  2.88 us
  transfers between devices with their start and end apart: 31, of which 20 were waited for; matrix products, arithmetic and copies ran while one was open for 3% of the time, Pallas kernels for 11%

profile of v5, /device:TPU:2, one launch (start us, length us, event | category | flops | bytes accessed | tf_op | source)
XLA Modules:
  0.0 132.0 jit_solution(2516368056930015827)
XLA Ops:
  0.6 1.2 copy.13.latent_ref
  1.8 0.7 copy-done
  2.5 0.8 shard_map.119
  3.3 8.5 %all-to-all-start = ((bf16[8,2,16,576]{3,2,1,0:T(8,128)(2,1)}), bf16[8,2,16,576]{3,2,1,0:T(8,128)(2,1)S(1)}, u32[]{:S(2)}, u32[]{:S(2)}) async-start(bf16[8,2,16,576]{3,2,1,0:T(8,128)(2,1)} %shard_map.119), calls=%async_computation | async-start | bytes 655360 | tf_op jit(solution)/shard_map/all_to_all | solution.py:307
  11.8 0.8 reshape.48.l0.listed_ref
  12.6 1.5 %collective-permute-start.2 = (s32[8]{0:T(128)S(1)}, s32[8]{0:T(128)S(1)}, u32[]{:S(2)}, u32[]{:S(2)}) collective-permute-start(s32[8]{0:T(128)S(1)} %reshape.48.l0.listed_ref), channel_id=1, source_target_pairs={{0,64},{64,128},{128,192},{192,0},{1,65},{65,129},{129,193},{193,1... | collective-permute-start | bytes 104 | tf_op jit(solution)/shard_map/ppermute | solution.py:311
  14.0 1.1 collective-permute-start.1
  15.2 2.2 %collective-permute-start = (s32[8]{0:T(128)S(1)}, s32[8]{0:T(128)S(1)}, u32[]{:S(2)}, u32[]{:S(2)}) collective-permute-start(s32[8]{0:T(128)S(1)} %reshape.48.l0.listed_ref), channel_id=1, source_target_pairs={{0,192},{64,0},{128,64},{192,128},{1,193},{65,1},{129,65},{193,129... | collective-permute-start | bytes 104 | tf_op jit(solution)/shard_map/ppermute | solution.py:311
  17.3 2.1 %copy_bitcast_fusion = (bf16[512,1024]{1,0:T(8,128)(2,1)S(1)}, bf16[512,1024]{1,0:T(8,128)(2,1)S(1)}) fusion(bf16[64,8,8,128]{3,2,1,0:T(8,128)(2,1)} %bitcast.16, bf16[64,8,8,128]{3,2,1,0:T(8,128)(2,1)} %bitcast.17), kind=kLoop, calls=%fused_computation | loop fusion | bytes 4194304 | tf_op jit(solution)/shard_map/reshape | solution.py:348
  19.4 5.7 %all-to-all-done = bf16[8,2,16,576]{3,2,1,0:T(8,128)(2,1)S(1)} async-done(((bf16[8,2,16,576]{3,2,1,0:T(8,128)(2,1)}), bf16[8,2,16,576]{3,2,1,0:T(8,128)(2,1)S(1)}, u32[]{:S(2)}, u32[]{:S(2)}) %all-to-all-start) | async-done | bytes 294944 | tf_op jit(solution)/shard_map/all_to_all | solution.py:307
  25.1 1.4 %shard_map.120 = (bf16[8,16,576]{2,1,0:T(8,128)(2,1)S(1)}, bf16[8,16,576]{2,1,0:T(8,128)(2,1)}, bf16[8,16,576]{2,1,0:T(8,128)(2,1)}, bf16[8,16,576]{2,1,0:T(8,128)(2,1)S(1)}) custom-call(s32[8]{0:T(128)S(1)} %reshape.48.l0.listed_ref, s32[8]{0:T(128)S(1)} %collective-permute-done.l1, s32[8]{0:T(128)S(1)} %collective-permute-done.1.l2, ...), custom_call_target="tpu_custom_call" | custom-call | tf_op jit(solution)/shard_map/pallas_call | solution.py:352
  26.5 1.5 %collective-permute-start.3 = (bf16[8,16,576]{2,1,0:T(8,128)(2,1)}, bf16[8,16,576]{2,1,0:T(8,128)(2,1)S(1)}, u32[]{:S(2)}, u32[]{:S(2)}) collective-permute-start(bf16[8,16,576]{2,1,0:T(8,128)(2,1)} %get-tuple-element.45), channel_id=1, source_target_pairs={{0,64},{64,128},{128,192},{192,0},{1,65},{65,129},{129,193},{193,1... | collective-permute-start | bytes 442376 | tf_op jit(solution)/shard_map/ppermute | solution.py:311
  28.0 1.1 collective-permute-start.4
  29.1 2.2 %collective-permute-start.5 = (bf16[8,16,576]{2,1,0:T(8,128)(2,1)S(1)}, bf16[8,16,576]{2,1,0:T(8,128)(2,1)S(1)}, u32[]{:S(2)}, u32[]{:S(2)}) collective-permute-start(bf16[8,16,576]{2,1,0:T(8,128)(2,1)S(1)} %get-tuple-element.47), channel_id=1, source_target_pairs={{0,192},{64,0},{128,64},{192,128},{1,193},{65,1},{129,65},{193,129... | collective-permute-start | bytes 442376 | tf_op jit(solution)/shard_map/ppermute | solution.py:311
  31.2 2.2 %collective-permute-done.3.i1 = bf16[8,16,576]{2,1,0:T(8,128)(2,1)S(1)} collective-permute-done((bf16[8,16,576]{2,1,0:T(8,128)(2,1)}, bf16[8,16,576]{2,1,0:T(8,128)(2,1)S(1)}, u32[]{:S(2)}, u32[]{:S(2)}) %collective-permute-start.3) | collective-permute-done | bytes 147488 | tf_op jit(solution)/shard_map/ppermute | solution.py:311
  33.4 2.2 %collective-permute-done.4.i2 = bf16[8,16,576]{2,1,0:T(8,128)(2,1)S(1)} collective-permute-done((bf16[8,16,576]{2,1,0:T(8,128)(2,1)}, bf16[8,16,576]{2,1,0:T(8,128)(2,1)S(1)}, u32[]{:S(2)}, u32[]{:S(2)}) %collective-permute-start.4) | collective-permute-done | bytes 147488 | tf_op jit(solution)/shard_map/ppermute | solution.py:311
  35.6 0.7 collective-permute-done.5.i3
  36.3 0.8 shard_map.121.n0
  37.1 3.1 %collective-permute-start.8 = (bf16[8,16,576]{2,1,0:T(8,128)(2,1)S(1)}, bf16[8,16,576]{2,1,0:T(8,128)(2,1)S(1)}, u32[]{:S(2)}, u32[]{:S(2)}) collective-permute-start(bf16[8,16,576]{2,1,0:T(8,128)(2,1)S(1)} %shard_map.121.n0), channel_id=1, source_target_pairs={{0,6},{2,0},{4,2},{6,4},{1,7},{3,1},{5,3},{7,5},{8,14},{10,8},{12,... | collective-permute-start | bytes 442376 | tf_op jit(solution)/shard_map/ppermute | solution.py:311
  40.2 0.6 collective-permute-start.7
  40.8 1.0 collective-permute-start.6
  41.8 3.0 %collective-permute-done.8.n3 = bf16[8,16,576]{2,1,0:T(8,128)(2,1)S(1)} collective-permute-done((bf16[8,16,576]{2,1,0:T(8,128)(2,1)S(1)}, bf16[8,16,576]{2,1,0:T(8,128)(2,1)S(1)}, u32[]{:S(2)}, u32[]{:S(2)}) %collective-permute-start.8) | collective-permute-done | bytes 147488 | tf_op jit(solution)/shard_map/ppermute | solution.py:311
  44.8 2.3 %collective-permute-done.7.n2 = bf16[8,16,576]{2,1,0:T(8,128)(2,1)S(1)} collective-permute-done((bf16[8,16,576]{2,1,0:T(8,128)(2,1)S(1)}, bf16[8,16,576]{2,1,0:T(8,128)(2,1)S(1)}, u32[]{:S(2)}, u32[]{:S(2)}) %collective-permute-start.7) | collective-permute-done | bytes 147488 | tf_op jit(solution)/shard_map/ppermute | solution.py:311
  47.1 1.6 %collective-permute-done.6.n1 = bf16[8,16,576]{2,1,0:T(8,128)(2,1)S(1)} collective-permute-done((bf16[8,16,576]{2,1,0:T(8,128)(2,1)S(1)}, bf16[8,16,576]{2,1,0:T(8,128)(2,1)S(1)}, u32[]{:S(2)}, u32[]{:S(2)}) %collective-permute-start.6) | collective-permute-done | bytes 147488 | tf_op jit(solution)/shard_map/ppermute | solution.py:311
  48.8 0.1 reshape.47.vis_ref
  48.9 1.4 %collective-permute-done.10.f1 = bf16[8,16,576]{2,1,0:T(8,128)(2,1)} collective-permute-done((bf16[8,16,576]{2,1,0:T(8,128)(2,1)S(1)}, bf16[8,16,576]{2,1,0:T(8,128)(2,1)}, u32[]{:S(2)}, u32[]{:S(2)}) %collective-permute-start.10) | collective-permute-done | bytes 147488 | tf_op jit(solution)/shard_map/ppermute | solution.py:319
  50.3 13.9 %shard_map.122 = (bf16[2,1024,640]{2,1,0:T(8,128)(2,1)}, bf16[2,1024,640]{2,1,0:T(8,128)(2,1)}, bf16[2,640,512]{2,1,0:T(8,128)(2,1)}, bf16[2,640,64]{2,1,0:T(8,1...) custom-call(s32[1]{0:T(128)} %bitcast.2.core_ref, s32[1]{0:T(128)} %bitcast.1.y_ref, ...), custom_call_target="tpu_custom_call" | custom-call | flops 6200000000 | bytes 8000000 | tf_op jit(solution)/shard_map/pallas_call | solution.py:369
  64.2 0.2 collective-permute-start.13
  64.4 2.4 %collective-permute-done.13.recv_ref = bf16[4,10,16,576]{3,2,1,0:T(8,128)(2,1)S(1)} collective-permute-done((bf16[4,10,16,576]{3,2,1,0:T(8,128)(2,1)}, bf16[4,10,16,576]{3,2,1,0:T(8,128)(2,1)S(1)}, u32[]{:S(2)}, u32[]{:S(2)}) %collective-permute-start.13) | collective-permute-done | bytes 737312 | tf_op jit(solution)/shard_map/ppermute | solution.py:319
  66.8 0.2 shard_map.123
  67.0 0.1 collective-permute-start.14
  67.1 2.0 %collective-permute-start.15 = (bf16[10,16,576]{2,1,0:T(8,128)(2,1)S(1)}, bf16[10,16,576]{2,1,0:T(8,128)(2,1)S(1)}, u32[]{:S(2)}, u32[]{:S(2)}) collective-permute-start(bf16[10,16,576]{2,1,0:T(8,128)(2,1)S(1)} %get-tuple-element.60), channel_id=1, source_target_pairs={{0,4},{2,6},{4,0},{6,2},{1,5},{3,7},{5,1},{7,3},{8,12},{10,14},{12... | collective-permute-start | bytes 552968 | tf_op jit(solution)/shard_map/ppermute | solution.py:311
  69.1 1.2 collective-permute-start.16
  70.4 9.7 %shard_map.124 = (bf16[256,1024]{1,0:T(8,128)(2,1)}, bf16[256,1536]{1,0:T(8,128)(2,1)}, bf16[128,2048]{1,0:T(8,128)(2,1)S(1)}, bf16[128,2048]{1,0:T(8,128)(2,1)S...) custom-call(s32[1]{0:T(128)} %bitcast.x_ref, ...), custom_call_target="tpu_custom_call" | custom-call | flops 4000000000 | bytes 8000000 | tf_op jit(solution)/shard_map/pallas_call | solution.py:394
  80.1 1.5 %collective-permute-start.24 = (bf16[64,2048]{1,0:T(8,128)(2,1)S(1)}, bf16[64,2048]{1,0:T(8,128)(2,1)S(1)}, u32[]{:S(2)}, u32[]{:S(2)}) collective-permute-start(bf16[64,2048]{1,0:T(8,128)(2,1)S(1)} %get-tuple-element.71), channel_id=1, source_target_pairs={{0,64},{64,128},{128,192},{192,0},{1,65},{65,129},{129,193},{193,1... | collective-permute-start | bytes 786440 | tf_op jit(solution)/shard_map/ppermute | solution.py:311
  81.6 0.5 collective-permute-start.25
  82.1 0.1 shard_map.125
  82.2 1.6 %collective-permute-start.19 = (bf16[8,16,576]{2,1,0:T(8,128)(2,1)S(1)}, bf16[8,16,576]{2,1,0:T(8,128)(2,1)S(1)}, u32[]{:S(2)}, u32[]{:S(2)}) collective-permute-start(bf16[8,16,576]{2,1,0:T(8,128)(2,1)S(1)} %get-tuple-element.67.i0), channel_id=1, source_target_pairs={{0,64},{64,128},{128,192},{192,0},{1,65},{65,129},{129,193},{193,1... | collective-permute-start | bytes 442376 | tf_op jit(solution)/shard_map/ppermute | solution.py:311
  83.8 2.7 %collective-permute-start.18 = (bf16[8,16,576]{2,1,0:T(8,128)(2,1)S(1)}, bf16[8,16,576]{2,1,0:T(8,128)(2,1)S(1)}, u32[]{:S(2)}, u32[]{:S(2)}) collective-permute-start(bf16[8,16,576]{2,1,0:T(8,128)(2,1)S(1)} %get-tuple-element.67.i0), channel_id=1, source_target_pairs={{0,128},{64,192},{128,0},{192,64},{1,129},{65,193},{129,1},{193,65... | collective-permute-start | bytes 442376 | tf_op jit(solution)/shard_map/ppermute | solution.py:311
  86.5 0.4 collective-permute-start.17
  86.9 2.4 %collective-permute-done.24.a_ref = bf16[64,2048]{1,0:T(8,128)(2,1)S(1)} collective-permute-done((bf16[64,2048]{1,0:T(8,128)(2,1)S(1)}, bf16[64,2048]{1,0:T(8,128)(2,1)S(1)}, u32[]{:S(2)}, u32[]{:S(2)}) %collective-permute-start.24) | collective-permute-done | bytes 262176 | tf_op jit(solution)/shard_map/ppermute | solution.py:311
  89.3 4.1 %collective-permute-done.25.b_ref = bf16[64,2048]{1,0:T(8,128)(2,1)S(1)} collective-permute-done((bf16[64,2048]{1,0:T(8,128)(2,1)S(1)}, bf16[64,2048]{1,0:T(8,128)(2,1)S(1)}, u32[]{:S(2)}, u32[]{:S(2)}) %collective-permute-start.25) | collective-permute-done | bytes 262176 | tf_op jit(solution)/shard_map/ppermute | solution.py:311
  93.4 1.1 shard_map.130
  94.5 2.0 %collective-permute-start.27 = (bf16[128,2048]{1,0:T(8,128)(2,1)}, bf16[128,2048]{1,0:T(8,128)(2,1)S(1)}, u32[]{:S(2)}, u32[]{:S(2)}) collective-permute-start(bf16[128,2048]{1,0:T(8,128)(2,1)} %get-tuple-element.74), channel_id=1, source_target_pairs={{0,192},{64,0},{128,64},{192,128},{1,193},{65,1},{129,65},{193,129... | collective-permute-start | bytes 1572872 | tf_op jit(solution)/shard_map/ppermute | solution.py:311
  96.5 1.1 collective-permute-done.17.i1
  97.7 1.9 %shard_map.126 = bf16[8,2,16,576]{3,2,1,0:T(8,128)(2,1)} custom-call(s32[1]{0:T(128)} %bitcast.x_ref, s32[1]{0:T(128)} %bitcast.5.z_ref, s32[8]{0:T(128)S(1)} %reshape.48.l0.listed_ref, s32[8]{0:T(128)S(1)} %collective-permute-done.l1, s32[8]{0:T(128)S(1)} %collective-permute-done.1.l2, s32[8]{0:T(128)S(1)} %collective-permute-done.2.l3, ...), custom_call_target="tpu_custom_call" | custom-call | tf_op jit(solution)/shard_map/pallas_call | solution.py:415
  99.5 3.4 %all-to-all-start.1 = ((bf16[8,2,16,576]{3,2,1,0:T(8,128)(2,1)}), bf16[8,2,16,576]{3,2,1,0:T(8,128)(2,1)S(1)}, u32[]{:S(2)}, u32[]{:S(2)}) async-start(bf16[8,2,16,576]{3,2,1,0:T(8,128)(2,1)} %shard_map.126), calls=%async_computation.1 | async-start | bytes 655360 | tf_op jit(solution)/shard_map/all_to_all | solution.py:307
  103.0 3.2 %collective-permute-done.26.w1 = bf16[128,2048]{1,0:T(8,128)(2,1)S(1)} collective-permute-done((bf16[128,2048]{1,0:T(8,128)(2,1)}, bf16[128,2048]{1,0:T(8,128)(2,1)S(1)}, u32[]{:S(2)}, u32[]{:S(2)}) %collective-permute-start.26) | collective-permute-done | bytes 524320 | tf_op jit(solution)/shard_map/ppermute | solution.py:311
  106.1 1.2 collective-permute-done.27.w3
  107.4 1.0 shard_map.131
  108.4 5.7 %all-to-all-done.1.in_ref = bf16[8,2,16,576]{3,2,1,0:T(8,128)(2,1)S(1)} async-done(((bf16[8,2,16,576]{3,2,1,0:T(8,128)(2,1)}), bf16[8,2,16,576]{3,2,1,0:T(8,128)(2,1)S(1)}, u32[]{:S(2)}, u32[]{:S(2)}) %all-to-all-start.1) | async-done | bytes 294944 | tf_op jit(solution)/shard_map/all_to_all | solution.py:307
  114.1 3.5 %all-to-all-start.2 = ((bf16[8,16,2048]{2,1,0:T(8,128)(2,1)}), bf16[8,16,2048]{2,1,0:T(8,128)(2,1)S(1)}, u32[]{:S(2)}, u32[]{:S(2)}) async-start(bf16[8,16,2048]{2,1,0:T(8,128)(2,1)} %shard_map.131), calls=%async_computation.2 | async-start | bytes 1048576 | tf_op jit(solution)/shard_map/all_to_all | solution.py:307
  117.6 0.1 collective-permute-start.20
  117.7 1.2 collective-permute-done.20.far_ref
  118.9 1.0 collective-permute-start.23
  120.0 2.0 %collective-permute-start.22 = (bf16[2,2,16,576]{3,2,1,0:T(8,128)(2,1)S(1)}, bf16[2,2,16,576]{3,2,1,0:T(8,128)(2,1)S(1)}, u32[]{:S(2)}, u32[]{:S(2)}) collective-permute-start(bf16[2,2,16,576]{3,2,1,0:T(8,128)(2,1)S(1)} %shard_map.128.i0), channel_id=1, source_target_pairs={{0,4},{2,6},{4,0},{6,2},{1,5},{3,7},{5,1},{7,3},{8,12},{10,14},{12... | collective-permute-start | bytes 221192 | tf_op jit(solution)/shard_map/ppermute | solution.py:311
  121.9 1.1 collective-permute-start.21
  123.1 0.4 collective-permute-done.23.i3
  123.5 3.0 %collective-permute-done.22.i2 = bf16[2,2,16,576]{3,2,1,0:T(8,128)(2,1)S(1)} collective-permute-done((bf16[2,2,16,576]{3,2,1,0:T(8,128)(2,1)S(1)}, bf16[2,2,16,576]{3,2,1,0:T(8,128)(2,1)S(1)}, u32[]{:S(2)}, u32[]{:S(2)}) %collective-permute-start.22) | collective-permute-done | bytes 73760 | tf_op jit(solution)/shard_map/ppermute | solution.py:311
  126.5 1.2 collective-permute-done.21.i1
  127.7 0.3 shard_map.129
  128.0 1.0 copy.16
  129.0 2.3 %all-to-all-done.2.in_ref = bf16[8,16,2048]{2,1,0:T(8,128)(2,1)S(1)} async-done(((bf16[8,16,2048]{2,1,0:T(8,128)(2,1)}), bf16[8,16,2048]{2,1,0:T(8,128)(2,1)S(1)}, u32[]{:S(2)}, u32[]{:S(2)}) %all-to-all-start.2) | async-done | bytes 524320 | tf_op jit(solution)/shard_map/all_to_all | solution.py:307
  131.3 0.8 shard_map.132
  (23 shorter events, 0.1 us)
Async XLA Ops:
  1.8 0.7 copy-start
  3.3 21.7 %all-to-all-start = ((bf16[8,2,16,576]{3,2,1,0:T(8,128)(2,1)}), bf16[8,2,16,576]{3,2,1,0:T(8,128)(2,1)S(1)}, u32[]{:S(2)}, u32[]{:S(2)}) async-start(bf16[8,2,16,576]{3,2,1,0:T(8,128)(2,1)} %shard_map.119), calls=%async_computation | async-start | bytes 655360 | tf_op jit(solution)/shard_map/all_to_all | solution.py:307
  12.6 12.5 %collective-permute-start.2 = (s32[8]{0:T(128)S(1)}, s32[8]{0:T(128)S(1)}, u32[]{:S(2)}, u32[]{:S(2)}) collective-permute-start(s32[8]{0:T(128)S(1)} %reshape.48.l0.listed_ref), channel_id=1, source_target_pairs={{0,64},{64,128},{128,192},{192,0},{1,65},{65,129},{129,193},{193,1... | collective-permute-start | bytes 104 | tf_op jit(solution)/shard_map/ppermute | solution.py:311
  14.0 11.0 %collective-permute-start.1 = (s32[8]{0:T(128)S(1)}, s32[8]{0:T(128)S(1)}, u32[]{:S(2)}, u32[]{:S(2)}) collective-permute-start(s32[8]{0:T(128)S(1)} %reshape.48.l0.listed_ref), channel_id=1, source_target_pairs={{0,128},{64,192},{128,0},{192,64},{1,129},{65,193},{129,1},{193,65... | collective-permute-start | bytes 104 | tf_op jit(solution)/shard_map/ppermute | solution.py:311
  15.2 9.9 %collective-permute-start = (s32[8]{0:T(128)S(1)}, s32[8]{0:T(128)S(1)}, u32[]{:S(2)}, u32[]{:S(2)}) collective-permute-start(s32[8]{0:T(128)S(1)} %reshape.48.l0.listed_ref), channel_id=1, source_target_pairs={{0,192},{64,0},{128,64},{192,128},{1,193},{65,1},{129,65},{193,129... | collective-permute-start | bytes 104 | tf_op jit(solution)/shard_map/ppermute | solution.py:311
  17.3 31.5 %copy-start.2 = (s32[2,4]{1,0:T(2,128)S(1)}, s32[2,4]{1,0:T(2,128)}, u32[]{:S(2)}) copy-start(s32[2,4]{1,0:T(2,128)} %param.15) | copy-start | bytes 100
  17.3 33.0 %copy-start.1 = (f32[512]{0:T(512)S(1)}, f32[512]{0:T(512)}, u32[]{:S(2)}) copy-start(f32[512]{0:T(512)} %param.10) | copy-start | bytes 6148
  26.5 7.0 %collective-permute-start.3 = (bf16[8,16,576]{2,1,0:T(8,128)(2,1)}, bf16[8,16,576]{2,1,0:T(8,128)(2,1)S(1)}, u32[]{:S(2)}, u32[]{:S(2)}) collective-permute-start(bf16[8,16,576]{2,1,0:T(8,128)(2,1)} %get-tuple-element.45), channel_id=1, source_target_pairs={{0,64},{64,128},{128,192},{192,0},{1,65},{65,129},{129,193},{193,1... | collective-permute-start | bytes 442376 | tf_op jit(solution)/shard_map/ppermute | solution.py:311
  28.0 7.6 %collective-permute-start.4 = (bf16[8,16,576]{2,1,0:T(8,128)(2,1)}, bf16[8,16,576]{2,1,0:T(8,128)(2,1)S(1)}, u32[]{:S(2)}, u32[]{:S(2)}) collective-permute-start(bf16[8,16,576]{2,1,0:T(8,128)(2,1)} %get-tuple-element.46), channel_id=1, source_target_pairs={{0,128},{64,192},{128,0},{192,64},{1,129},{65,193},{129,1},{193,65... | collective-permute-start | bytes 442376 | tf_op jit(solution)/shard_map/ppermute | solution.py:311
  29.1 7.2 %collective-permute-start.5 = (bf16[8,16,576]{2,1,0:T(8,128)(2,1)S(1)}, bf16[8,16,576]{2,1,0:T(8,128)(2,1)S(1)}, u32[]{:S(2)}, u32[]{:S(2)}) collective-permute-start(bf16[8,16,576]{2,1,0:T(8,128)(2,1)S(1)} %get-tuple-element.47), channel_id=1, source_target_pairs={{0,192},{64,0},{128,64},{192,128},{1,193},{65,1},{129,65},{193,129... | collective-permute-start | bytes 442376 | tf_op jit(solution)/shard_map/ppermute | solution.py:311
  37.1 7.7 %collective-permute-start.8 = (bf16[8,16,576]{2,1,0:T(8,128)(2,1)S(1)}, bf16[8,16,576]{2,1,0:T(8,128)(2,1)S(1)}, u32[]{:S(2)}, u32[]{:S(2)}) collective-permute-start(bf16[8,16,576]{2,1,0:T(8,128)(2,1)S(1)} %shard_map.121.n0), channel_id=1, source_target_pairs={{0,6},{2,0},{4,2},{6,4},{1,7},{3,1},{5,3},{7,5},{8,14},{10,8},{12,... | collective-permute-start | bytes 442376 | tf_op jit(solution)/shard_map/ppermute | solution.py:311
  40.2 6.9 %collective-permute-start.7 = (bf16[8,16,576]{2,1,0:T(8,128)(2,1)S(1)}, bf16[8,16,576]{2,1,0:T(8,128)(2,1)S(1)}, u32[]{:S(2)}, u32[]{:S(2)}) collective-permute-start(bf16[8,16,576]{2,1,0:T(8,128)(2,1)S(1)} %shard_map.121.n0), channel_id=1, source_target_pairs={{0,4},{2,6},{4,0},{6,2},{1,5},{3,7},{5,1},{7,3},{8,12},{10,14},{12... | collective-permute-start | bytes 442376 | tf_op jit(solution)/shard_map/ppermute | solution.py:311
  40.8 7.9 %collective-permute-start.6 = (bf16[8,16,576]{2,1,0:T(8,128)(2,1)S(1)}, bf16[8,16,576]{2,1,0:T(8,128)(2,1)S(1)}, u32[]{:S(2)}, u32[]{:S(2)}) collective-permute-start(bf16[8,16,576]{2,1,0:T(8,128)(2,1)S(1)} %shard_map.121.n0), channel_id=1, source_target_pairs={{0,2},{2,4},{4,6},{6,0},{1,3},{3,5},{5,7},{7,1},{8,10},{10,12},{12... | collective-permute-start | bytes 442376 | tf_op jit(solution)/shard_map/ppermute | solution.py:311
  41.8 7.1 %collective-permute-start.9 = (bf16[8,16,576]{2,1,0:T(8,128)(2,1)S(1)}, bf16[8,16,576]{2,1,0:T(8,128)(2,1)S(1)}, u32[]{:S(2)}, u32[]{:S(2)}) collective-permute-start(bf16[8,16,576]{2,1,0:T(8,128)(2,1)S(1)} %shard_map.121.n0), channel_id=1, source_target_pairs={{0,1},{1,0},{2,3},{3,2},{4,5},{5,4},{6,7},{7,6},{8,9},{9,8},{10,11... | collective-permute-start | bytes 442376 | tf_op jit(solution)/shard_map/ppermute | solution.py:319
  44.8 4.0 %collective-permute-start.12 = (bf16[8,16,576]{2,1,0:T(8,128)(2,1)S(1)}, bf16[8,16,576]{2,1,0:T(8,128)(2,1)S(1)}, u32[]{:S(2)}, u32[]{:S(2)}) collective-permute-start(bf16[8,16,576]{2,1,0:T(8,128)(2,1)S(1)} %collective-permute-done.8.n3), channel_id=1, source_target_pairs={{0,1},{1,0},{2,3},{3,2},{4,5},{5,4},{6,7},{7,6},{8,9},{9,8},{10,11... | collective-permute-start | bytes 442376 | tf_op jit(solution)/shard_map/ppermute | solution.py:319
  47.1 1.7 %collective-permute-start.11 = (bf16[8,16,576]{2,1,0:T(8,128)(2,1)S(1)}, bf16[8,16,576]{2,1,0:T(8,128)(2,1)}, u32[]{:S(2)}, u32[]{:S(2)}) collective-permute-start(bf16[8,16,576]{2,1,0:T(8,128)(2,1)S(1)} %collective-permute-done.7.n2), channel_id=1, source_target_pairs={{0,1},{1,0},{2,3},{3,2},{4,5},{5,4},{6,7},{7,6},{8,9},{9,8},{10,11... | collective-permute-start | bytes 442376 | tf_op jit(solution)/shard_map/ppermute | solution.py:319
  48.8 1.5 %collective-permute-start.10 = (bf16[8,16,576]{2,1,0:T(8,128)(2,1)S(1)}, bf16[8,16,576]{2,1,0:T(8,128)(2,1)}, u32[]{:S(2)}, u32[]{:S(2)}) collective-permute-start(bf16[8,16,576]{2,1,0:T(8,128)(2,1)S(1)} %collective-permute-done.6.n1), channel_id=1, source_target_pairs={{0,1},{1,0},{2,3},{3,2},{4,5},{5,4},{6,7},{7,6},{8,9},{9,8},{10,11... | collective-permute-start | bytes 442376 | tf_op jit(solution)/shard_map/ppermute | solution.py:319
  64.2 2.6 %collective-permute-start.13 = (bf16[4,10,16,576]{3,2,1,0:T(8,128)(2,1)}, bf16[4,10,16,576]{3,2,1,0:T(8,128)(2,1)S(1)}, u32[]{:S(2)}, u32[]{:S(2)}) collective-permute-start(bf16[4,10,16,576]{3,2,1,0:T(8,128)(2,1)} %get-tuple-element.49), channel_id=1, source_target_pairs={{0,1},{1,0},{2,3},{3,2},{4,5},{5,4},{6,7},{7,6},{8,9},{9,8},{10,11... | collective-permute-start | bytes 2211848 | tf_op jit(solution)/shard_map/ppermute | solution.py:319
  67.0 15.1 %collective-permute-start.14 = (bf16[10,16,576]{2,1,0:T(8,128)(2,1)S(1)}, bf16[10,16,576]{2,1,0:T(8,128)(2,1)S(1)}, u32[]{:S(2)}, u32[]{:S(2)}) collective-permute-start(bf16[10,16,576]{2,1,0:T(8,128)(2,1)S(1)} %get-tuple-element.59), channel_id=1, source_target_pairs={{0,2},{2,4},{4,6},{6,0},{1,3},{3,5},{5,7},{7,1},{8,10},{10,12},{12... | collective-permute-start | bytes 552968 | tf_op jit(solution)/shard_map/ppermute | solution.py:311
  67.1 15.0 %collective-permute-start.15 = (bf16[10,16,576]{2,1,0:T(8,128)(2,1)S(1)}, bf16[10,16,576]{2,1,0:T(8,128)(2,1)S(1)}, u32[]{:S(2)}, u32[]{:S(2)}) collective-permute-start(bf16[10,16,576]{2,1,0:T(8,128)(2,1)S(1)} %get-tuple-element.60), channel_id=1, source_target_pairs={{0,4},{2,6},{4,0},{6,2},{1,5},{3,7},{5,1},{7,3},{8,12},{10,14},{12... | collective-permute-start | bytes 552968 | tf_op jit(solution)/shard_map/ppermute | solution.py:311
  69.1 13.0 %collective-permute-start.16 = (bf16[10,16,576]{2,1,0:T(8,128)(2,1)S(1)}, bf16[10,16,576]{2,1,0:T(8,128)(2,1)S(1)}, u32[]{:S(2)}, u32[]{:S(2)}) collective-permute-start(bf16[10,16,576]{2,1,0:T(8,128)(2,1)S(1)} %get-tuple-element.61), channel_id=1, source_target_pairs={{0,6},{2,0},{4,2},{6,4},{1,7},{3,1},{5,3},{7,5},{8,14},{10,8},{12,... | collective-permute-start | bytes 552968 | tf_op jit(solution)/shard_map/ppermute | solution.py:311
  80.1 9.2 %collective-permute-start.24 = (bf16[64,2048]{1,0:T(8,128)(2,1)S(1)}, bf16[64,2048]{1,0:T(8,128)(2,1)S(1)}, u32[]{:S(2)}, u32[]{:S(2)}) collective-permute-start(bf16[64,2048]{1,0:T(8,128)(2,1)S(1)} %get-tuple-element.71), channel_id=1, source_target_pairs={{0,64},{64,128},{128,192},{192,0},{1,65},{65,129},{129,193},{193,1... | collective-permute-start | bytes 786440 | tf_op jit(solution)/shard_map/ppermute | solution.py:311
  81.6 11.8 %collective-permute-start.25 = (bf16[64,2048]{1,0:T(8,128)(2,1)S(1)}, bf16[64,2048]{1,0:T(8,128)(2,1)S(1)}, u32[]{:S(2)}, u32[]{:S(2)}) collective-permute-start(bf16[64,2048]{1,0:T(8,128)(2,1)S(1)} %get-tuple-element.72), channel_id=1, source_target_pairs={{0,192},{64,0},{128,64},{192,128},{1,193},{65,1},{129,65},{193,129... | collective-permute-start | bytes 786440 | tf_op jit(solution)/shard_map/ppermute | solution.py:311
  82.2 14.3 %collective-permute-start.19 = (bf16[8,16,576]{2,1,0:T(8,128)(2,1)S(1)}, bf16[8,16,576]{2,1,0:T(8,128)(2,1)S(1)}, u32[]{:S(2)}, u32[]{:S(2)}) collective-permute-start(bf16[8,16,576]{2,1,0:T(8,128)(2,1)S(1)} %get-tuple-element.67.i0), channel_id=1, source_target_pairs={{0,64},{64,128},{128,192},{192,0},{1,65},{65,129},{129,193},{193,1... | collective-permute-start | bytes 442376 | tf_op jit(solution)/shard_map/ppermute | solution.py:311
  83.8 12.7 %collective-permute-start.18 = (bf16[8,16,576]{2,1,0:T(8,128)(2,1)S(1)}, bf16[8,16,576]{2,1,0:T(8,128)(2,1)S(1)}, u32[]{:S(2)}, u32[]{:S(2)}) collective-permute-start(bf16[8,16,576]{2,1,0:T(8,128)(2,1)S(1)} %get-tuple-element.67.i0), channel_id=1, source_target_pairs={{0,128},{64,192},{128,0},{192,64},{1,129},{65,193},{129,1},{193,65... | collective-permute-start | bytes 442376 | tf_op jit(solution)/shard_map/ppermute | solution.py:311
  86.5 11.2 %collective-permute-start.17 = (bf16[8,16,576]{2,1,0:T(8,128)(2,1)S(1)}, bf16[8,16,576]{2,1,0:T(8,128)(2,1)S(1)}, u32[]{:S(2)}, u32[]{:S(2)}) collective-permute-start(bf16[8,16,576]{2,1,0:T(8,128)(2,1)S(1)} %get-tuple-element.67.i0), channel_id=1, source_target_pairs={{0,192},{64,0},{128,64},{192,128},{1,193},{65,1},{129,65},{193,129... | collective-permute-start | bytes 442376 | tf_op jit(solution)/shard_map/ppermute | solution.py:311
  94.5 11.6 %collective-permute-start.26 = (bf16[128,2048]{1,0:T(8,128)(2,1)}, bf16[128,2048]{1,0:T(8,128)(2,1)S(1)}, u32[]{:S(2)}, u32[]{:S(2)}) collective-permute-start(bf16[128,2048]{1,0:T(8,128)(2,1)} %get-tuple-element.73), channel_id=1, source_target_pairs={{0,64},{64,128},{128,192},{192,0},{1,65},{65,129},{129,193},{193,1... | collective-permute-start | bytes 1572872 | tf_op jit(solution)/shard_map/ppermute | solution.py:311
  94.5 12.9 %collective-permute-start.27 = (bf16[128,2048]{1,0:T(8,128)(2,1)}, bf16[128,2048]{1,0:T(8,128)(2,1)S(1)}, u32[]{:S(2)}, u32[]{:S(2)}) collective-permute-start(bf16[128,2048]{1,0:T(8,128)(2,1)} %get-tuple-element.74), channel_id=1, source_target_pairs={{0,192},{64,0},{128,64},{192,128},{1,193},{65,1},{129,65},{193,129... | collective-permute-start | bytes 1572872 | tf_op jit(solution)/shard_map/ppermute | solution.py:311
  99.5 14.5 %all-to-all-start.1 = ((bf16[8,2,16,576]{3,2,1,0:T(8,128)(2,1)}), bf16[8,2,16,576]{3,2,1,0:T(8,128)(2,1)S(1)}, u32[]{:S(2)}, u32[]{:S(2)}) async-start(bf16[8,2,16,576]{3,2,1,0:T(8,128)(2,1)} %shard_map.126), calls=%async_computation.1 | async-start | bytes 655360 | tf_op jit(solution)/shard_map/all_to_all | solution.py:307
  114.1 17.2 %all-to-all-start.2 = ((bf16[8,16,2048]{2,1,0:T(8,128)(2,1)}), bf16[8,16,2048]{2,1,0:T(8,128)(2,1)S(1)}, u32[]{:S(2)}, u32[]{:S(2)}) async-start(bf16[8,16,2048]{2,1,0:T(8,128)(2,1)} %shard_map.131), calls=%async_computation.2 | async-start | bytes 1048576 | tf_op jit(solution)/shard_map/all_to_all | solution.py:307
  117.6 1.3 collective-permute-start.20
  118.9 4.6 %collective-permute-start.23 = (bf16[2,2,16,576]{3,2,1,0:T(8,128)(2,1)S(1)}, bf16[2,2,16,576]{3,2,1,0:T(8,128)(2,1)S(1)}, u32[]{:S(2)}, u32[]{:S(2)}) collective-permute-start(bf16[2,2,16,576]{3,2,1,0:T(8,128)(2,1)S(1)} %shard_map.128.i0), channel_id=1, source_target_pairs={{0,6},{2,0},{4,2},{6,4},{1,7},{3,1},{5,3},{7,5},{8,14},{10,8},{12,... | collective-permute-start | bytes 221192 | tf_op jit(solution)/shard_map/ppermute | solution.py:311
  120.0 6.5 %collective-permute-start.22 = (bf16[2,2,16,576]{3,2,1,0:T(8,128)(2,1)S(1)}, bf16[2,2,16,576]{3,2,1,0:T(8,128)(2,1)S(1)}, u32[]{:S(2)}, u32[]{:S(2)}) collective-permute-start(bf16[2,2,16,576]{3,2,1,0:T(8,128)(2,1)S(1)} %shard_map.128.i0), channel_id=1, source_target_pairs={{0,4},{2,6},{4,0},{6,2},{1,5},{3,7},{5,1},{7,3},{8,12},{10,14},{12... | collective-permute-start | bytes 221192 | tf_op jit(solution)/shard_map/ppermute | solution.py:311
  121.9 5.8 %collective-permute-start.21 = (bf16[2,2,16,576]{3,2,1,0:T(8,128)(2,1)S(1)}, bf16[2,2,16,576]{3,2,1,0:T(8,128)(2,1)S(1)}, u32[]{:S(2)}, u32[]{:S(2)}) collective-permute-start(bf16[2,2,16,576]{3,2,1,0:T(8,128)(2,1)S(1)} %shard_map.128.i0), channel_id=1, source_target_pairs={{0,2},{2,4},{4,6},{6,0},{1,3},{3,5},{5,7},{7,1},{8,10},{10,12},{12... | collective-permute-start | bytes 221192 | tf_op jit(solution)/shard_map/ppermute | solution.py:311
